TPU v7x, 32 devices: a whole 2x2x4 slice. The times are simulated.
32 devices in a mesh: groups: 2 (over y), seq: 4 (over z), blk: 4 (over x, core).
Axes of the slice: x: 2, y: 2, z: 4, core: 2. Of those that a mesh axis runs over, the one named last changes fastest.
Arguments:
- candidates: bfloat16 [8, 512, 512], P(('groups', 'blk'), 'seq'), parts along dimension 0, may hold values from -6 to 6
- gate_values: bfloat16 [8, 512, 512], P(('groups', 'blk'), 'seq'), parts along dimension 0, may hold values from -6 to 6
- hist_keys: bfloat16 [16384, 512], P(('groups', 'seq', 'blk')), parts along dimension 0, may hold values from -6 to 6
- hist_values: bfloat16 [16384, 512], P(('groups', 'seq', 'blk')), parts along dimension 0, may hold values from -17 to 17
- pattern: int32 [32, 16], P('groups'), parts along dimension 0, may hold values from 0 to 1, as said below
Outputs:
- result: bfloat16 [8, 512, 512], P(('groups', 'blk'), 'seq'), parts along dimension 0
There are 2 independent parts, one for each index of `groups`. A program takes and returns all parts, laid end to end along the dimension named above; each array names one. Nothing has to cross between parts.
Inputs may be any that keep to these rules, and one draw needn't show every extreme that they name: `pattern`: every entry is 0 or 1; the last history block is admitted for every candidate block.
All inputs are finite; a program needn't handle non-finite values.
Results may differ from a plain program's by a relative error of at most 0.005.
Values may be sent and summed in bfloat16 or wider, within the bound.
No kernel may reach another device: no remote copies, remote signals or barrier semaphores. Data moves between devices by JAX's collectives and lax.ppermute only.
A program may use at most 64 MiB of HBM per device.

v0:
```python
import jax
import jax.numpy as jnp
from jax import lax
from jax.sharding import PartitionSpec as P

HEADS = 4
CAND_BLOCK = 128


def shifted(block, axis, distance):
    devices = range(lax.axis_size(axis))
    route = [((i - distance) % len(devices), i) for i in devices]
    return lax.ppermute(block, axis, route)


def attend_block(queries, key_block, value_block, live_rows):
    row_count = queries.shape[0]
    width = queries.shape[1]
    head_dim = width // HEADS
    query_heads = queries.reshape(row_count, HEADS, head_dim)
    key_heads = key_block.reshape(key_block.shape[0], HEADS, head_dim)
    value_heads = value_block.reshape(value_block.shape[0], HEADS, head_dim)
    scores = jnp.einsum("qhd,khd->hqk", query_heads, key_heads, preferred_element_type=jnp.float32)
    weights = (jax.nn.silu(scores * head_dim ** (-0.5)) * live_rows[None, :, None]).astype(
        jnp.bfloat16
    )
    mixed = jnp.einsum("hqk,khd->qhd", weights, value_heads, preferred_element_type=jnp.float32)
    return mixed.reshape(row_count, width)


def attend(queries, key_block, value_block, live_rows):
    pieces = attend_block(queries, key_block, value_block, live_rows)
    return pieces


def live_mask(pattern, owner_index, block_index, row_count):
    column = lax.dynamic_slice_in_dim(pattern, block_index, 1, 1)[:, 0]
    block_count = row_count // CAND_BLOCK
    chosen = lax.dynamic_slice_in_dim(column, owner_index * block_count, block_count, 0)
    return jnp.repeat(chosen.astype(jnp.float32), CAND_BLOCK)


def on_device(candidates, gate_values, hist_keys, hist_values, pattern):
    queries = lax.all_gather(candidates, "seq", axis=1, tiled=True)[0]
    cycle_size = lax.axis_size("blk")
    cycle_index = lax.axis_index("blk")
    seq_index = lax.axis_index("seq")
    row_count = queries.shape[0]
    running = jnp.zeros((row_count, queries.shape[1]), jnp.float32)
    moving = queries
    own_block = seq_index * cycle_size + cycle_index
    for turn_index in range(cycle_size):
        if turn_index + 1 < cycle_size:
            following = shifted(moving, "blk", 1)
        owner_index = (cycle_index - turn_index) % cycle_size
        live_rows = live_mask(pattern, owner_index, own_block, row_count)
        running = shifted(running + attend(moving, hist_keys, hist_values, live_rows), "blk", 1)
        if turn_index + 1 < cycle_size:
            moving = following
    summed = lax.psum_scatter(running, "seq", scatter_dimension=0, tiled=True)
    mean_square = jnp.mean(summed * summed, axis=1, keepdims=True)
    normed = summed * lax.rsqrt(mean_square + 1e-05)
    result = (normed * gate_values[0].astype(jnp.float32)).astype(jnp.bfloat16)
    return result[None]


def solution(mesh):
    in_specs = (
        P(("groups", "blk"), "seq", None),
        P(("groups", "blk"), "seq", None),
        P(("groups", "seq", "blk"), None),
        P(("groups", "seq", "blk"), None),
        P("groups", None),
    )
    out_specs = P(("groups", "blk"), "seq", None)
    return jax.shard_map(
        on_device, mesh=mesh, in_specs=in_specs, out_specs=out_specs, check_vma=False
    )
```

profile of v0, /device:TPU:0, one launch (start us, length us, event | category | flops | bytes accessed | tf_op | source)
XLA Modules:
  0.0 131.8 jit_solution(3600134700320135416)
XLA Ops:
  6.5 0.0 copy-start
  6.5 0.0 copy-start.2
  6.5 0.0 reduce-scatter.2.cloned.1.call-start
  6.5 1.1 copy.18
  7.7 16.7 %all_gather.3 = bf16[1,512,512]{1,2,0:T(8,128)(2,1)S(1)} all-gather(bf16[1,128,512]{1,2,0:T(8,128)(2,1)S(1)} %copy.18), channel_id=1, replica_groups=mesh['groups'=2,'seq'=4,'blk'=4] {'seq'}, dimensions={1}, use_global_device_ids=true | all-gather | bytes 655360 | tf_op jit(solution)/shard_map/all_gather | solution.py:44
  24.3 0.0 collective-permute-start.1
  24.3 0.0 copy-done.2
  24.3 1.0 copy.39
  25.4 0.0 copy-done.5
  25.4 0.2 convert_reduce_fusion
  25.6 0.1 broadcast_bitcast_fusion.3
  25.7 0.0 copy-done
  25.7 3.2 %fusion = f32[4,512,128]{1,2,0:T(8,128)S(1)} fusion(bf16[512,4,128]{0,2,1:T(8,128)(2,1)} %bitcast.75, bf16[512,4,128]{0,2,1:T(8,128)(2,1)S(1)} %bitcast.74, f32[512]{0:T(512)S(1)} %broadcast_bitcast_fusion.3, bf16[512,512]{1,0:T(8,128)(2,1)S(1)} %copy-done), kind=kOutput, calls=%fused_computation.4 | convolution fusion | flops 544210944 | bytes 2623488 | tf_op jit(solution)/shard_map/hqk,khd->qhd/dot_general | solution.py:27
  28.9 0.3 copy.22
  29.2 1.7 %collective-permute-start = (f32[512,512]{1,0:T(8,128)S(1)}, f32[512,512]{1,0:T(8,128)}, u32[]{:S(2)}, u32[]{:S(2)}) collective-permute-start(f32[512,512]{1,0:T(8,128)S(1)} %copy.22), channel_id=1, source_target_pairs={{3,0},{0,1},{1,2},{2,3},{7,4},{4,5},{5,6},{6,7},{11,8},{8,9},{9,10... | collective-permute-start | bytes 3145736 | tf_op jit(solution)/shard_map/ppermute | solution.py:13
  30.9 0.1 broadcast_bitcast_fusion.2
  30.9 2.1 %collective-permute-done.1 = bf16[512,512]{0,1:T(8,128)(2,1)} collective-permute-done((bf16[512,512]{0,1:T(8,128)(2,1)S(1)}, bf16[512,512]{0,1:T(8,128)(2,1)}, u32[]{:S(2)}, u32[]{:S(2)}) %collective-permute-start.1) | collective-permute-done | bytes 524320 | tf_op jit(solution)/shard_map/ppermute | solution.py:13
  33.0 0.0 collective-permute-start.3
  33.0 4.4 %fusion.1 = f32[4,512,128]{1,2,0:T(8,128)} fusion(bf16[512,4,128]{0,2,1:T(8,128)(2,1)} %bitcast.76, bf16[512,4,128]{0,2,1:T(8,128)(2,1)} %bitcast.5, f32[512]{0:T(512)S(1)} %broadcast_bitcast_fusion.2, bf16[512,512]{1,0:T(8,128)(2,1)S(1)} %copy-done), kind=kOutput, calls=%fused_computation.5 | convolution fusion | flops 544210944 | bytes 2623488 | tf_op jit(solution)/shard_map/hqk,khd->qhd/dot_general | solution.py:27
  37.4 1.6 %copy.26 = f32[512,512]{1,0:T(8,128)S(1)} copy(f32[512,512]{0,1:T(8,128)} %bitcast.71) | data formatting | bytes 2097152 | tf_op jit(solution)/shard_map/reshape | solution.py:28
  39.0 0.0 copy-start.3
  39.0 5.3 %collective-permute-done = f32[512,512]{1,0:T(8,128)} collective-permute-done((f32[512,512]{1,0:T(8,128)S(1)}, f32[512,512]{1,0:T(8,128)}, u32[]{:S(2)}, u32[]{:S(2)}) %collective-permute-start) | collective-permute-done | bytes 1048608 | tf_op jit(solution)/shard_map/ppermute | solution.py:13
  44.3 1.4 %add.88 = f32[512,512]{1,0:T(8,128)S(1)} add(f32[512,512]{1,0:T(8,128)} %collective-permute-done, f32[512,512]{1,0:T(8,128)S(1)} %copy.26) | non-fusion elementwise | flops 262144 | bytes 3145728 | tf_op jit(solution)/shard_map/add | solution.py:57
  45.7 0.1 collective-permute-start.2
  45.8 0.1 broadcast_bitcast_fusion.1
  45.8 4.0 %collective-permute-done.3 = bf16[512,512]{0,1:T(8,128)(2,1)} collective-permute-done((bf16[512,512]{0,1:T(8,128)(2,1)}, bf16[512,512]{0,1:T(8,128)(2,1)}, u32[]{:S(2)}, u32[]{:S(2)}) %collective-permute-start.3) | collective-permute-done | bytes 524320 | tf_op jit(solution)/shard_map/ppermute | solution.py:13
  49.9 0.0 collective-permute-start.5
  49.9 0.0 copy-done.3
  49.9 4.2 %fusion.2 = f32[4,512,128]{1,2,0:T(8,128)} fusion(bf16[512,4,128]{0,2,1:T(8,128)(2,1)S(1)} %bitcast.77, bf16[512,4,128]{0,2,1:T(8,128)(2,1)} %bitcast.9, f32[512]{0:T(512)S(1)} %broadcast_bitcast_fusion.1, bf16[512,512]{1,0:T(8,128)(2,1)S(1)} %copy-done), kind=kOutput, calls=%fused_computation.6 | convolution fusion | flops 544210944 | bytes 2623488 | tf_op jit(solution)/shard_map/hqk,khd->qhd/dot_general | solution.py:27
  54.1 1.6 %copy.30 = f32[512,512]{1,0:T(8,128)S(1)} copy(f32[512,512]{0,1:T(8,128)} %bitcast.72) | data formatting | bytes 2097152 | tf_op jit(solution)/shard_map/reshape | solution.py:28
  55.7 5.4 %collective-permute-done.2 = f32[512,512]{1,0:T(8,128)} collective-permute-done((f32[512,512]{1,0:T(8,128)S(1)}, f32[512,512]{1,0:T(8,128)}, u32[]{:S(2)}, u32[]{:S(2)}) %collective-permute-start.2) | collective-permute-done | bytes 1048608 | tf_op jit(solution)/shard_map/ppermute | solution.py:13
  61.1 1.4 %add.92 = f32[512,512]{1,0:T(8,128)S(1)} add(f32[512,512]{1,0:T(8,128)} %collective-permute-done.2, f32[512,512]{1,0:T(8,128)S(1)} %copy.30) | non-fusion elementwise | flops 262144 | bytes 3145728 | tf_op jit(solution)/shard_map/add | solution.py:57
  62.6 0.1 collective-permute-start.4
  62.6 0.1 broadcast_bitcast_fusion
  62.7 4.0 %collective-permute-done.5 = bf16[512,512]{0,1:T(8,128)(2,1)} collective-permute-done((bf16[512,512]{0,1:T(8,128)(2,1)}, bf16[512,512]{0,1:T(8,128)(2,1)}, u32[]{:S(2)}, u32[]{:S(2)}) %collective-permute-start.5) | collective-permute-done | bytes 524320 | tf_op jit(solution)/shard_map/ppermute | solution.py:13
  66.7 4.2 %fusion.3 = f32[4,512,128]{1,2,0:T(8,128)} fusion(bf16[512,4,128]{0,2,1:T(8,128)(2,1)S(1)} %bitcast.78, bf16[512,4,128]{0,2,1:T(8,128)(2,1)} %bitcast.13, f32[512]{0:T(512)S(1)} %broadcast_bitcast_fusion, bf16[512,512]{1,0:T(8,128)(2,1)S(1)} %copy-done), kind=kOutput, calls=%fused_computation.7 | convolution fusion | flops 544210944 | bytes 2623488 | tf_op jit(solution)/shard_map/hqk,khd->qhd/dot_general | solution.py:27
  71.0 1.6 %copy.34 = f32[512,512]{1,0:T(8,128)S(1)} copy(f32[512,512]{0,1:T(8,128)} %bitcast.69) | data formatting | bytes 2097152 | tf_op jit(solution)/shard_map/reshape | solution.py:28
  72.5 5.4 %collective-permute-done.4 = f32[512,512]{1,0:T(8,128)} collective-permute-done((f32[512,512]{1,0:T(8,128)S(1)}, f32[512,512]{1,0:T(8,128)}, u32[]{:S(2)}, u32[]{:S(2)}) %collective-permute-start.4) | collective-permute-done | bytes 1048608 | tf_op jit(solution)/shard_map/ppermute | solution.py:13
  78.0 1.4 %add.96 = f32[512,512]{1,0:T(8,128)S(1)} add(f32[512,512]{1,0:T(8,128)} %collective-permute-done.4, f32[512,512]{1,0:T(8,128)S(1)} %copy.34) | non-fusion elementwise | flops 262144 | bytes 3145728 | tf_op jit(solution)/shard_map/add | solution.py:57
  79.4 0.0 copy-start.4
  79.4 0.1 collective-permute-start.6
  79.5 14.2 %collective-permute-done.6 = f32[512,512]{1,0:T(8,128)S(1)} collective-permute-done((f32[512,512]{1,0:T(8,128)S(1)}, f32[512,512]{1,0:T(8,128)S(1)}, u32[]{:S(2)}, u32[]{:S(2)}) %collective-permute-start.6) | collective-permute-done | bytes 1048608 | tf_op jit(solution)/shard_map/ppermute | solution.py:13
  93.7 1.0 copy-done.1
  94.7 0.0 reduce-scatter.2.cloned.1.call-update
  94.7 27.4 %reduce-scatter.2.cloned.1.call-done = f32[128,512]{1,0:T(8,128)} async-done(((f32[512,512]{1,0:T(8,128)}), f32[128,512]{1,0:T(8,128)}) %reduce-scatter.2.cloned.1.call-update) | async-done | bytes 262160 | tf_op jit(solution)/shard_map/reduce_scatter | solution.py:60
  122.1 1.1 multiply_reduce_fusion
  123.2 0.0 copy-done.4
  123.2 1.7 %fusion.21 = bf16[1,128,512]{2,1,0:T(8,128)(2,1)} fusion(f32[128,512]{1,0:T(8,128)} %reduce-scatter.2.cloned.1.call-done, bf16[1,128,512]{2,1,0:T(8,128)(2,1)S(1)} %copy-done.4, f32[128]{0:T(128)S(1)} %add_rsqrt_fusion), kind=kLoop, calls=%fused_computation.19 | loop fusion | flops 262144 | bytes 524800 | tf_op jit(solution)/shard_map/broadcast_in_dim | solution.py:64
  (3 shorter events, 0.0 us)
Async XLA Ops:
  6.5 19.1 %copy-start = (bf16[512,512]{1,0:T(8,128)(2,1)S(1)}, bf16[512,512]{1,0:T(8,128)(2,1)}, u32[]{:S(2)}) copy-start(bf16[512,512]{1,0:T(8,128)(2,1)} %param.7) | copy-start | bytes 1572868
  6.5 17.8 %copy-start.2 = (bf16[512,512]{1,0:T(8,128)(2,1)S(1)}, bf16[512,512]{1,0:T(8,128)(2,1)}, u32[]{:S(2)}) copy-start(bf16[512,512]{1,0:T(8,128)(2,1)} %param.8) | copy-start | bytes 1572868
  6.5 18.8 %copy-start.5 = (s32[16,16]{1,0:T(8,128)S(1)}, s32[16,16]{1,0:T(8,128)}, u32[]{:S(2)}) copy-start(s32[16,16]{1,0:T(8,128)} %param.9) | copy-start | bytes 3076
  6.5 115.6 %reduce-scatter.2.cloned.1.call-start = ((), (), s32[]{:S(2)}) async-start(), calls=%async_computation.1 | async-start | bytes 1310720 | tf_op jit(solution)/shard_map/reduce_scatter | solution.py:60
  24.3 8.7 %collective-permute-start.1 = (bf16[512,512]{0,1:T(8,128)(2,1)S(1)}, bf16[512,512]{0,1:T(8,128)(2,1)}, u32[]{:S(2)}, u32[]{:S(2)}) collective-permute-start(bf16[512,512]{0,1:T(8,128)(2,1)S(1)} %bitcast.73), channel_id=1, source_target_pairs={{3,0},{0,1},{1,2},{2,3},{7,4},{4,5},{5,6},{6,7},{11,8},{8,9},{9,10... | collective-permute-start | bytes 1572872 | tf_op jit(solution)/shard_map/ppermute | solution.py:13
  29.2 15.1 %collective-permute-start = (f32[512,512]{1,0:T(8,128)S(1)}, f32[512,512]{1,0:T(8,128)}, u32[]{:S(2)}, u32[]{:S(2)}) collective-permute-start(f32[512,512]{1,0:T(8,128)S(1)} %copy.22), channel_id=1, source_target_pairs={{3,0},{0,1},{1,2},{2,3},{7,4},{4,5},{5,6},{6,7},{11,8},{8,9},{9,10... | collective-permute-start | bytes 3145736 | tf_op jit(solution)/shard_map/ppermute | solution.py:13
  33.0 16.9 %collective-permute-start.3 = (bf16[512,512]{0,1:T(8,128)(2,1)}, bf16[512,512]{0,1:T(8,128)(2,1)}, u32[]{:S(2)}, u32[]{:S(2)}) collective-permute-start(bf16[512,512]{0,1:T(8,128)(2,1)} %collective-permute-done.1), channel_id=1, source_target_pairs={{3,0},{0,1},{1,2},{2,3},{7,4},{4,5},{5,6},{6,7},{11,8},{8,9},{9,10... | collective-permute-start | bytes 1572872 | tf_op jit(solution)/shard_map/ppermute | solution.py:13
  39.0 10.9 %copy-start.3 = (bf16[512,512]{0,1:T(8,128)(2,1)S(1)}, bf16[512,512]{0,1:T(8,128)(2,1)}, u32[]{:S(2)}) copy-start(bf16[512,512]{0,1:T(8,128)(2,1)} %copy.39) | copy-start | bytes 1572868
  45.7 15.4 %collective-permute-start.2 = (f32[512,512]{1,0:T(8,128)S(1)}, f32[512,512]{1,0:T(8,128)}, u32[]{:S(2)}, u32[]{:S(2)}) collective-permute-start(f32[512,512]{1,0:T(8,128)S(1)} %add.88), channel_id=1, source_target_pairs={{3,0},{0,1},{1,2},{2,3},{7,4},{4,5},{5,6},{6,7},{11,8},{8,9},{9,10... | collective-permute-start | bytes 3145736 | tf_op jit(solution)/shard_map/ppermute | solution.py:13
  49.9 16.9 %collective-permute-start.5 = (bf16[512,512]{0,1:T(8,128)(2,1)}, bf16[512,512]{0,1:T(8,128)(2,1)}, u32[]{:S(2)}, u32[]{:S(2)}) collective-permute-start(bf16[512,512]{0,1:T(8,128)(2,1)} %collective-permute-done.3), channel_id=1, source_target_pairs={{3,0},{0,1},{1,2},{2,3},{7,4},{4,5},{5,6},{6,7},{11,8},{8,9},{9,10... | collective-permute-start | bytes 1572872 | tf_op jit(solution)/shard_map/ppermute | solution.py:13
  62.6 15.4 %collective-permute-start.4 = (f32[512,512]{1,0:T(8,128)S(1)}, f32[512,512]{1,0:T(8,128)}, u32[]{:S(2)}, u32[]{:S(2)}) collective-permute-start(f32[512,512]{1,0:T(8,128)S(1)} %add.92), channel_id=1, source_target_pairs={{3,0},{0,1},{1,2},{2,3},{7,4},{4,5},{5,6},{6,7},{11,8},{8,9},{9,10... | collective-permute-start | bytes 3145736 | tf_op jit(solution)/shard_map/ppermute | solution.py:13
  79.4 43.8 %copy-start.4 = (bf16[1,128,512]{2,1,0:T(8,128)(2,1)S(1)}, bf16[1,128,512]{2,1,0:T(8,128)(2,1)}, u32[]{:S(2)}) copy-start(bf16[1,128,512]{2,1,0:T(8,128)(2,1)} %param.6) | copy-start | bytes 393220
  79.4 14.3 %collective-permute-start.6 = (f32[512,512]{1,0:T(8,128)S(1)}, f32[512,512]{1,0:T(8,128)S(1)}, u32[]{:S(2)}, u32[]{:S(2)}) collective-permute-start(f32[512,512]{1,0:T(8,128)S(1)} %add.96), channel_id=1, source_target_pairs={{3,0},{0,1},{1,2},{2,3},{7,4},{4,5},{5,6},{6,7},{11,8},{8,9},{9,10... | collective-permute-start | bytes 3145736 | tf_op jit(solution)/shard_map/ppermute | solution.py:13
  93.7 1.0 copy-start.1
Sparse Core Ops, SparseCore 0:
  94.8 27.2 reduce-scatter.1
where the time goes:
time: 132 us
  waiting for transfers between devices  68 us (52%)
  blocking collectives  16.7 us (13%)
  matrix products  16 us (12%)
  between operations  13.5 us (10%)
  local copies, waits for them, and re-layouts  8.41 us (6%)
  other arithmetic  7.29 us (6%)
  starting transfers between devices  1.84 us (1%)
    ppermute x7, waiting for transfers between devices, shifted(): return lax.ppermute(block, axis, route)  40.6 us
    reduce_scatter x1, waiting for transfers between devices, on_device(): summed = lax.psum_scatter(running, 'seq', scatter_dimension=0, tiled=True)  27.4 us
    all_gather x1, blocking collectives, on_device(): queries = lax.all_gather(candidates, 'seq', axis=1, tiled=True)[0]  16.7 us
    dot_general x4, matrix products, attend_block(): jnp.einsum('hqk,khd->qhd', weights, value_heads, preferred_element_type=j...  16 us
    reshape x4, local copies, waits for them, and re-layouts, attend_block(): return mixed.reshape(row_count, width)  4.99 us
    add x3, other arithmetic, on_device(): running + attend(moving, hist_keys, hist_values, live_rows)  4.29 us
  transfers between devices with their start and end apart: 8, of which 8 were waited for; matrix products, arithmetic and copies ran while one was open for 19% of the time, Pallas kernels for 0%

commit v1 on v0

v1 whole, which is shorter than its diff:
```python
import functools

import jax
import jax.numpy as jnp
from jax import lax
from jax.experimental import pallas as pl
from jax.experimental.pallas import tpu as pltpu
from jax.sharding import PartitionSpec as P

HEADS = 4
HEAD_DIM = 128
CAND_BLOCK = 128
HALF_SCALE = 0.5 * HEAD_DIM ** (-0.5)
CHUNKS = ((0, 1), (2, 3))
VMEM_LIMIT = 48 * 1024 * 1024


def swapped(block, axis, mask):
    size = lax.axis_size(axis)
    return lax.ppermute(block, axis, [(i, i ^ mask) for i in range(size)])


def attend_kernel(heads, row_count, block_masks, hist_masks, has_start, *refs):
    pattern_ref, refs = refs[0], refs[1:]
    row_refs, refs = refs[:row_count], refs[row_count:]
    hist_refs, refs = refs[: len(hist_masks)], refs[len(hist_masks) :]
    start_refs, refs = (refs[:row_count], refs[row_count:]) if has_start else (None, refs)
    out_refs = refs
    seq = lax.axis_index("seq")
    blk = lax.axis_index("blk")
    blk_size = lax.axis_size("blk")
    live = []
    for mask in hist_masks:
        column = seq * blk_size + (blk ^ mask)
        live.append(
            [
                pattern_ref[blk * row_count + place, column].astype(jnp.float32) * HALF_SCALE
                for place in [(seq ^ m) if m is not None else i for i, m in enumerate(block_masks)]
            ]
        )
    width = len(heads) * HEAD_DIM
    for at, head in enumerate(heads):
        queries = jnp.concatenate(
            [ref[:, head * HEAD_DIM : (head + 1) * HEAD_DIM] for ref in row_refs], axis=0
        )
        total = None
        for hist_ref, scales in zip(hist_refs, live):
            keys = hist_ref[:, at * HEAD_DIM : (at + 1) * HEAD_DIM]
            values = hist_ref[:, width + at * HEAD_DIM : width + (at + 1) * HEAD_DIM]
            scores = lax.dot_general(
                queries, keys, (((1,), (1,)), ((), ())), preferred_element_type=jnp.float32
            )
            weights = []
            for i, scale in enumerate(scales):
                half = scores[i * CAND_BLOCK : (i + 1) * CAND_BLOCK] * scale
                weights.append((half + half * jnp.tanh(half)).astype(jnp.bfloat16))
            mixed = jnp.dot(
                jnp.concatenate(weights, axis=0), values, preferred_element_type=jnp.float32
            )
            total = mixed if total is None else total + mixed
        for i, out_ref in enumerate(out_refs):
            piece = total[i * CAND_BLOCK : (i + 1) * CAND_BLOCK]
            columns = slice(at * HEAD_DIM, (at + 1) * HEAD_DIM)
            if has_start:
                piece = piece + start_refs[i][:, columns]
            out_ref[:, columns] = piece.astype(out_ref.dtype)


def attend(pattern, rows, hist, heads, block_masks, hist_masks, start=None, kinds=None):
    row_count = len(rows)
    width = len(heads) * HEAD_DIM
    kinds = kinds or [jnp.float32] * row_count
    events = hist[0].shape[0]
    flops = 4 * row_count * CAND_BLOCK * events * len(hist) * width
    inputs = [pattern, *rows, *hist, *(start or [])]
    vmem = pl.BlockSpec(memory_space=pltpu.VMEM)
    return pl.pallas_call(
        functools.partial(
            attend_kernel, heads, row_count, block_masks, hist_masks, start is not None
        ),
        out_shape=[jax.ShapeDtypeStruct((CAND_BLOCK, width), kind) for kind in kinds],
        in_specs=[pl.BlockSpec(memory_space=pltpu.SMEM)] + [vmem] * (len(inputs) - 1),
        out_specs=[vmem] * row_count,
        compiler_params=pltpu.CompilerParams(vmem_limit_bytes=VMEM_LIMIT),
        cost_estimate=pl.CostEstimate(
            flops=flops,
            transcendentals=flops // (4 * HEAD_DIM),
            bytes_accessed=sum(x.size * x.dtype.itemsize for x in inputs),
        ),
    )(*inputs)


def finish_kernel(parts, gate_ref, *refs):
    out_ref = refs[-1]
    summed, at = [], 0
    for count in parts:
        total = refs[at][...].astype(jnp.float32)
        for ref in refs[at + 1 : at + count]:
            total = total + ref[...].astype(jnp.float32)
        summed.append(total)
        at += count
    summed = jnp.concatenate(summed, axis=1)
    mean_square = jnp.mean(summed * summed, axis=1, keepdims=True)
    normed = summed * lax.rsqrt(mean_square + 1e-05)
    out_ref[...] = (normed * gate_ref[...].astype(jnp.float32)).astype(out_ref.dtype)


def finish(gate, pieces):
    arrays = [x for piece in pieces for x in piece]
    vmem = pl.BlockSpec(memory_space=pltpu.VMEM)
    return pl.pallas_call(
        functools.partial(finish_kernel, [len(piece) for piece in pieces]),
        out_shape=jax.ShapeDtypeStruct(gate.shape, gate.dtype),
        in_specs=[vmem] * (1 + len(arrays)),
        out_specs=vmem,
    )(gate, *arrays)


def gather_rows(block):
    if lax.axis_size("seq") == 4 and block.shape[0] == CAND_BLOCK:
        far = swapped(block, "seq", 2)
        near = swapped(block, "seq", 1)
        return [block, near, far, swapped(far, "seq", 1)], [0, 1, 2, 3]
    rows = lax.all_gather(block, "seq", axis=0, tiled=True)
    count = rows.shape[0] // CAND_BLOCK
    return [rows[i * CAND_BLOCK : (i + 1) * CAND_BLOCK] for i in range(count)], [None] * count


def scatter_sums(pieces, block_masks):
    if block_masks[0] is None:
        rows = jnp.concatenate(pieces, axis=0)
        return [lax.psum_scatter(rows, "seq", scatter_dimension=0, tiled=True)]
    own, near, far, both = pieces
    passed = swapped(both, "seq", 1)
    far = (far + passed.astype(jnp.float32)).astype(jnp.bfloat16)
    return [own, swapped(near, "seq", 1), swapped(far, "seq", 2)]


def on_device(candidates, gate_values, hist_keys, hist_values, pattern):
    hists = []
    for heads in CHUNKS:
        columns = slice(heads[0] * HEAD_DIM, (heads[-1] + 1) * HEAD_DIM)
        hists.append(jnp.concatenate([hist_keys[:, columns], hist_values[:, columns]], axis=1))
    across = [swapped(hist, "blk", 2) for hist in hists]
    rows, block_masks = gather_rows(candidates[0])
    beside = [swapped(hist, "blk", 1) for hist in hists]
    pieces = []
    for i, heads in enumerate(CHUNKS):
        kinds = [jnp.float32, jnp.bfloat16, jnp.float32, jnp.bfloat16]
        if block_masks[0] is None:
            kinds = [jnp.float32] * len(rows)
        start = attend(pattern, rows, [hists[i], beside[i]], heads, block_masks, [0, 1])
        diagonal = swapped(across[i], "blk", 1)
        sums = attend(
            pattern, rows, [across[i], diagonal], heads, block_masks, [2, 3], start, kinds
        )
        pieces.append(scatter_sums(sums, block_masks))
    return finish(gate_values[0], pieces)[None]


def solution(mesh):
    in_specs = (
        P(("groups", "blk"), "seq", None),
        P(("groups", "blk"), "seq", None),
        P(("groups", "seq", "blk"), None),
        P(("groups", "seq", "blk"), None),
        P("groups", None),
    )
    out_specs = P(("groups", "blk"), "seq", None)
    return jax.shard_map(
        on_device, mesh=mesh, in_specs=in_specs, out_specs=out_specs, check_vma=False
    )
```

time: 132 us -> 63.4 us (0.48)
  waiting for transfers between devices: 68 us -> 30.4 us
  starting transfers between devices: 1.84 us -> 20.3 us
  blocking collectives: 16.7 us -> 0 us
  matrix products: 16 us -> 0 us
  between operations: 13.5 us -> 0.13 us
  Pallas kernels: 0 us -> 10.5 us
  other arithmetic: 7.29 us -> 0.1 us
  local copies, waits for them, and re-layouts: 8.41 us -> 1.89 us
    reduce_scatter x1 -> x0, waiting for transfers between devices: 27.4 us -> none  [on_device(): summed = lax.psum_scatter(running, 'seq', scatter_dimension=0, tiled=True)]
    ppermute x7 -> x15, starting transfers between devices: 1.84 us -> 20.3 us  [swapped(): return lax.ppermute(block, axis, [(i, i ^ mask) for i in range(size)])]
    all_gather x1 -> x0, blocking collectives: 16.7 us -> none  [on_device(): queries = lax.all_gather(candidates, 'seq', axis=1, tiled=True)[0]]
    dot_general x4 -> x0, matrix products: 16 us -> none  [attend_block(): jnp.einsum('hqk,khd->qhd', weights, value_heads, preferred_element_type=j...]
    pallas_call x0 -> x5, Pallas kernels: none -> 10.5 us  [the longest x4 8.54 us: attend(): pl.pallas_call(functools.partial(attend_kernel, heads, row_count, block_m...]
    ppermute x7 -> x15, waiting for transfers between devices: 40.6 us -> 30.4 us  [swapped(): return lax.ppermute(block, axis, [(i, i ^ mask) for i in range(size)])]
    reshape x5 -> x0, local copies, waits for them, and re-layouts: 6.02 us -> none  [the longest x4 4.99 us: attend_block(): return mixed.reshape(row_count, width)]
    add x3 -> x0, other arithmetic: 4.29 us -> none  [on_device(): running + attend(moving, hist_keys, hist_values, live_rows)]
  transfers between devices with their start and end apart: 8 -> 15, of which waited for: 8 -> 7; matrix products, arithmetic and copies ran while one was open for 19% -> 0% of each run, Pallas kernels for 0% -> 14%
where the time goes in v1:
time: 63.4 us; the launch traced here: 63.2 us
  waiting for transfers between devices  30.4 us (48%)
  starting transfers between devices  20.3 us (32%)
  Pallas kernels  10.5 us (17%)
  local copies, waits for them, and re-layouts  1.89 us (3%)
    ppermute x15, waiting for transfers between devices, swapped(): return lax.ppermute(block, axis, [(i, i ^ mask) for i in range(size)])  30.4 us
    ppermute x15, starting transfers between devices, swapped(): return lax.ppermute(block, axis, [(i, i ^ mask) for i in range(size)])  20.3 us
    pallas_call x4, Pallas kernels, attend(): pl.pallas_call(functools.partial(attend_kernel, heads, row_count, block_m...  8.54 us
    pallas_call x1, Pallas kernels, finish(): pl.pallas_call(functools.partial(finish_kernel, [len(piece) for piece in...  1.92 us
  transfers between devices with their start and end apart: 15, of which 7 were waited for; matrix products, arithmetic and copies ran while one was open for 0% of the time, Pallas kernels for 14%

profile of v1, /device:TPU:0, one launch (start us, length us, event | category | flops | bytes accessed | tf_op | source)
XLA Modules:
  0.0 63.2 jit_solution(4401490835047683886)
XLA Ops:
  0.0 1.3 %fusion = (bf16[512,256]{1,0:T(8,128)(2,1)S(1)}, bf16[512,256]{1,0:T(8,128)(2,1)S(1)}, bf16[512,256]{1,0:T(8,128)(2,1)S(1)}, bf16[512,256]{1,0:T(8,128)(2,1)S(1)}) fusion(bf16[512,512]{1,0:T(8,128)(2,1)} %param.7, bf16[512,512]{1,0:T(8,128)(2,1)} %param.8), kind=kLoop, calls=%fused_computation.4 | loop fusion | bytes 2097152 | tf_op jit(solution)/shard_map/slice | solution.py:143
  1.3 3.0 %collective-permute-start.3 = (bf16[512,512]{1,0:T(8,128)(2,1)S(1)}, bf16[512,512]{1,0:T(8,128)(2,1)S(1)}, u32[]{:S(2)}, u32[]{:S(2)}) collective-permute-start(bf16[512,512]{1,0:T(8,128)(2,1)S(1)} %pad_maximum_fusion.refs_5_), channel_id=1, source_target_pairs={{0,2},{1,3},{2,0},{3,1},{4,6},{5,7},{6,4},{7,5},{8,10},{9,11},{10,... | collective-permute-start | bytes 1572872 | tf_op jit(solution)/shard_map/ppermute | solution.py:20
  4.3 0.0 copy-start
  4.4 0.1 collective-permute-start.9
  4.5 0.0 collective-permute-start.5
  4.5 12.5 %collective-permute-done.3.refs_5_ = bf16[512,512]{1,0:T(8,128)(2,1)S(1)} collective-permute-done((bf16[512,512]{1,0:T(8,128)(2,1)S(1)}, bf16[512,512]{1,0:T(8,128)(2,1)S(1)}, u32[]{:S(2)}, u32[]{:S(2)}) %collective-permute-start.3) | collective-permute-done | bytes 524320 | tf_op jit(solution)/shard_map/ppermute | solution.py:20
  17.1 0.0 collective-permute-start.4
  17.1 0.5 collective-permute-start.11
  17.6 0.0 copy-done
  17.6 3.2 %collective-permute-start.1 = (bf16[128,512]{1,0:T(8,128)(2,1)S(1)}, bf16[128,512]{1,0:T(8,128)(2,1)S(1)}, u32[]{:S(2)}, u32[]{:S(2)}) collective-permute-start(bf16[128,512]{1,0:T(8,128)(2,1)S(1)} %bitcast.3), channel_id=1, source_target_pairs={{0,8},{4,12},{8,0},{12,4},{1,9},{5,13},{9,1},{13,5},{2,10},{6,14},... | collective-permute-start | bytes 393224 | tf_op jit(solution)/shard_map/ppermute | solution.py:20
  20.7 6.7 %collective-permute-done.9.refs_5_ = bf16[512,512]{1,0:T(8,128)(2,1)S(1)} collective-permute-done((bf16[512,512]{1,0:T(8,128)(2,1)S(1)}, bf16[512,512]{1,0:T(8,128)(2,1)S(1)}, u32[]{:S(2)}, u32[]{:S(2)}) %collective-permute-start.9) | collective-permute-done | bytes 524320 | tf_op jit(solution)/shard_map/ppermute | solution.py:20
  27.5 0.0 collective-permute-start.10
  27.5 0.0 collective-permute-done.1.refs_3_
  27.5 1.8 %collective-permute-start = (bf16[128,512]{1,0:T(8,128)(2,1)S(1)}, bf16[128,512]{1,0:T(8,128)(2,1)S(1)}, u32[]{:S(2)}, u32[]{:S(2)}) collective-permute-start(bf16[128,512]{1,0:T(8,128)(2,1)S(1)} %bitcast.4), channel_id=1, source_target_pairs={{0,4},{4,0},{8,12},{12,8},{1,5},{5,1},{9,13},{13,9},{2,6},{6,2},{1... | collective-permute-start | bytes 393224 | tf_op jit(solution)/shard_map/ppermute | solution.py:20
  29.3 4.2 %collective-permute-done.refs_2_ = bf16[128,512]{1,0:T(8,128)(2,1)S(1)} collective-permute-done((bf16[128,512]{1,0:T(8,128)(2,1)S(1)}, bf16[128,512]{1,0:T(8,128)(2,1)S(1)}, u32[]{:S(2)}, u32[]{:S(2)}) %collective-permute-start) | collective-permute-done | bytes 131104 | tf_op jit(solution)/shard_map/ppermute | solution.py:20
  33.5 1.7 %collective-permute-start.2 = (bf16[128,512]{1,0:T(8,128)(2,1)S(1)}, bf16[128,512]{1,0:T(8,128)(2,1)S(1)}, u32[]{:S(2)}, u32[]{:S(2)}) collective-permute-start(bf16[128,512]{1,0:T(8,128)(2,1)S(1)} %collective-permute-done.1.refs_3_), channel_id=1, source_target_pairs={{0,4},{4,0},{8,12},{12,8},{1,5},{5,1},{9,13},{13,9},{2,6},{6,2},{1... | collective-permute-start | bytes 393224 | tf_op jit(solution)/shard_map/ppermute | solution.py:20
  35.2 3.5 %collective-permute-done.2.refs_4_ = bf16[128,512]{1,0:T(8,128)(2,1)S(1)} collective-permute-done((bf16[128,512]{1,0:T(8,128)(2,1)S(1)}, bf16[128,512]{1,0:T(8,128)(2,1)S(1)}, u32[]{:S(2)}, u32[]{:S(2)}) %collective-permute-start.2) | collective-permute-done | bytes 131104 | tf_op jit(solution)/shard_map/ppermute | solution.py:20
  38.7 0.0 collective-permute-done.5.refs_6_
  38.7 0.0 copy-done.3
  38.7 2.3 %shard_map.55 = (f32[128,256]{1,0:T(8,128)S(1)}, f32[128,256]{1,0:T(8,128)S(1)}, f32[128,256]{1,0:T(8,128)S(1)}, f32[128,256]{1,0:T(8,128)S(1)}) custom-call(s32[16,16]{1,0:T(8,128)S(1)} %copy-done.3, bf16[128,512]{1,0:T(8,128)(2,1)S(1)} %bitcast.5, bf16[128,512]{1,0:T(8,128)(2,1)S(1)} %collective-permute-done.refs_2_, ...), custom_call_target="tpu_custom_call" | custom-call | flops 536870912 | bytes 1573888 | tf_op jit(solution)/shard_map/pallas_call | solution.py:77
  41.0 0.0 collective-permute-done.4.refs_6_
  41.0 2.0 %shard_map.56 = (f32[128,256]{1,0:T(8,128)S(1)}, bf16[128,256]{1,0:T(8,128)(2,1)S(1)}, f32[128,256]{1,0:T(8,128)S(1)}, bf16[128,256]{1,0:T(8,128)(2,1)S(1)}) custom-call(s32[16,16]{1,0:T(8,128)S(1)} %copy-done.3, bf16[128,512]{1,0:T(8,128)(2,1)S(1)} %bitcast.6, bf16[128,512]{1,0:T(8,128)(2,1)S(1)} %collective-permute-done.refs_2_, ...), custom_call_target="tpu_custom_call" | custom-call | flops 536870912 | bytes 2098176 | tf_op jit(solution)/shard_map/pallas_call | solution.py:77
  43.0 0.0 copy-start.1
  43.0 1.7 %collective-permute-start.7 = (bf16[128,256]{1,0:T(8,128)(2,1)S(1)}, bf16[128,256]{1,0:T(8,128)(2,1)S(1)}, u32[]{:S(2)}, u32[]{:S(2)}) collective-permute-start(bf16[128,256]{1,0:T(8,128)(2,1)S(1)} %get-tuple-element.28), channel_id=1, source_target_pairs={{0,4},{4,0},{8,12},{12,8},{1,5},{5,1},{9,13},{13,9},{2,6},{6,2},{1... | collective-permute-start | bytes 196616 | tf_op jit(solution)/shard_map/ppermute | solution.py:20
  44.7 0.0 collective-permute-done.11.refs_6_
  44.7 2.3 %shard_map.57 = (f32[128,256]{1,0:T(8,128)S(1)}, f32[128,256]{1,0:T(8,128)S(1)}, f32[128,256]{1,0:T(8,128)S(1)}, f32[128,256]{1,0:T(8,128)S(1)}) custom-call(s32[16,16]{1,0:T(8,128)S(1)} %copy-done.3, bf16[128,512]{1,0:T(8,128)(2,1)S(1)} %bitcast.7, bf16[128,512]{1,0:T(8,128)(2,1)S(1)} %collective-permute-done.refs_2_, ...), custom_call_target="tpu_custom_call" | custom-call | flops 536870912 | bytes 1573888 | tf_op jit(solution)/shard_map/pallas_call | solution.py:77
  47.0 0.0 copy-done.1
  47.0 0.4 collective-permute-start.6
  47.5 0.0 collective-permute-done.10.refs_6_
  47.5 2.0 %shard_map.58 = (f32[128,256]{1,0:T(8,128)S(1)}, bf16[128,256]{1,0:T(8,128)(2,1)S(1)}, f32[128,256]{1,0:T(8,128)S(1)}, bf16[128,256]{1,0:T(8,128)(2,1)S(1)}) custom-call(s32[16,16]{1,0:T(8,128)S(1)} %copy-done.3, bf16[128,512]{1,0:T(8,128)(2,1)S(1)} %bitcast.8, bf16[128,512]{1,0:T(8,128)(2,1)S(1)} %collective-permute-done.refs_2_, ...), custom_call_target="tpu_custom_call" | custom-call | flops 536870912 | bytes 2098176 | tf_op jit(solution)/shard_map/pallas_call | solution.py:77
  49.5 0.0 copy-start.2
  49.5 1.7 %collective-permute-start.12 = (bf16[128,256]{1,0:T(8,128)(2,1)S(1)}, bf16[128,256]{1,0:T(8,128)(2,1)S(1)}, u32[]{:S(2)}, u32[]{:S(2)}) collective-permute-start(bf16[128,256]{1,0:T(8,128)(2,1)S(1)} %get-tuple-element.34), channel_id=1, source_target_pairs={{0,4},{4,0},{8,12},{12,8},{1,5},{5,1},{9,13},{13,9},{2,6},{6,2},{1... | collective-permute-start | bytes 196616 | tf_op jit(solution)/shard_map/ppermute | solution.py:20
  51.2 0.4 collective-permute-start.13
  51.6 0.0 collective-permute-done.7
  51.6 0.0 copy-done.2
  51.6 2.7 %collective-permute-start.8 = (bf16[128,256]{1,0:T(8,128)(2,1)S(1)}, bf16[128,256]{1,0:T(8,128)(2,1)S(1)}, u32[]{:S(2)}, u32[]{:S(2)}) collective-permute-start(bf16[128,256]{1,0:T(8,128)(2,1)S(1)} %add_convert_fusion.1), channel_id=1, source_target_pairs={{0,8},{4,12},{8,0},{12,4},{1,9},{5,13},{9,1},{13,5},{2,10},{6,14},... | collective-permute-start | bytes 196616 | tf_op jit(solution)/shard_map/ppermute | solution.py:20
  54.3 1.1 %collective-permute-done.13 = bf16[128,256]{1,0:T(8,128)(2,1)S(1)} collective-permute-done((bf16[128,256]{1,0:T(8,128)(2,1)S(1)}, bf16[128,256]{1,0:T(8,128)(2,1)S(1)}, u32[]{:S(2)}, u32[]{:S(2)}) %collective-permute-start.13) | collective-permute-done | bytes 65568 | tf_op jit(solution)/shard_map/ppermute | solution.py:20
  55.5 2.9 %collective-permute-start.14 = (bf16[128,256]{1,0:T(8,128)(2,1)S(1)}, bf16[128,256]{1,0:T(8,128)(2,1)S(1)}, u32[]{:S(2)}, u32[]{:S(2)}) collective-permute-start(bf16[128,256]{1,0:T(8,128)(2,1)S(1)} %add_convert_fusion), channel_id=1, source_target_pairs={{0,8},{4,12},{8,0},{12,4},{1,9},{5,13},{9,1},{13,5},{2,10},{6,14},... | collective-permute-start | bytes 196616 | tf_op jit(solution)/shard_map/ppermute | solution.py:20
  58.4 0.0 collective-permute-done.6.refs_1_
  58.4 0.0 collective-permute-done.12.refs_4_
  58.4 0.0 copy-start.5
  58.4 0.4 collective-permute-done.8.refs_2_
  58.8 1.9 %collective-permute-done.14.refs_5_ = bf16[128,256]{1,0:T(8,128)(2,1)S(1)} collective-permute-done((bf16[128,256]{1,0:T(8,128)(2,1)S(1)}, bf16[128,256]{1,0:T(8,128)(2,1)S(1)}, u32[]{:S(2)}, u32[]{:S(2)}) %collective-permute-start.14) | collective-permute-done | bytes 65568 | tf_op jit(solution)/shard_map/ppermute | solution.py:20
  60.7 0.0 copy-done.4
  60.7 0.0 copy-done.5
  60.7 0.0 copy-done.6
  60.7 0.6 copy-done.7
  61.3 1.9 %shard_map.59 = bf16[128,512]{1,0:T(8,128)(2,1)} custom-call(bf16[128,512]{1,0:T(8,128)(2,1)} %bitcast.9, f32[128,256]{1,0:T(8,128)} %copy-done.1, bf16[128,256]{1,0:T(8,128)(2,1)} %copy-done.4, bf16[128,256]{1,0:T(8,128)(2,1)} %copy-done.6, f32[128,256]{1,0:T(8,128)} %copy-done.2, bf16[128,256]{1,0:T(8,128)(2,1)} %copy-done.5, bf16[128,256]{1,0:T(8,128)(2,1)} %copy-done.7), custom_call_target="tpu_custom_call" | custom-call | tf_op jit(solution)/shard_map/pallas_call | solution.py:111
  (8 shorter events, 0.1 us)
Async XLA Ops:
  1.3 15.8 %collective-permute-start.3 = (bf16[512,512]{1,0:T(8,128)(2,1)S(1)}, bf16[512,512]{1,0:T(8,128)(2,1)S(1)}, u32[]{:S(2)}, u32[]{:S(2)}) collective-permute-start(bf16[512,512]{1,0:T(8,128)(2,1)S(1)} %pad_maximum_fusion.refs_5_), channel_id=1, source_target_pairs={{0,2},{1,3},{2,0},{3,1},{4,6},{5,7},{6,4},{7,5},{8,10},{9,11},{10,... | collective-permute-start | bytes 1572872 | tf_op jit(solution)/shard_map/ppermute | solution.py:20
  4.3 13.3 %copy-start = (bf16[1,128,512]{2,1,0:T(8,128)(2,1)S(1)}, bf16[1,128,512]{2,1,0:T(8,128)(2,1)}, u32[]{:S(2)}) copy-start(bf16[1,128,512]{2,1,0:T(8,128)(2,1)} %param.5) | copy-start | bytes 393220
  4.3 34.4 %copy-start.3 = (s32[16,16]{1,0:T(8,128)S(1)}, s32[16,16]{1,0:T(8,128)}, u32[]{:S(2)}) copy-start(s32[16,16]{1,0:T(8,128)} %refs_0_.7) | copy-start | bytes 3076
  4.4 23.1 %collective-permute-start.9 = (bf16[512,512]{1,0:T(8,128)(2,1)S(1)}, bf16[512,512]{1,0:T(8,128)(2,1)S(1)}, u32[]{:S(2)}, u32[]{:S(2)}) collective-permute-start(bf16[512,512]{1,0:T(8,128)(2,1)S(1)} %pad_maximum_fusion.1.refs_5_), channel_id=1, source_target_pairs={{0,2},{1,3},{2,0},{3,1},{4,6},{5,7},{6,4},{7,5},{8,10},{9,11},{10,... | collective-permute-start | bytes 1572872 | tf_op jit(solution)/shard_map/ppermute | solution.py:20
  4.5 34.2 %collective-permute-start.5 = (bf16[512,512]{1,0:T(8,128)(2,1)S(1)}, bf16[512,512]{1,0:T(8,128)(2,1)S(1)}, u32[]{:S(2)}, u32[]{:S(2)}) collective-permute-start(bf16[512,512]{1,0:T(8,128)(2,1)S(1)} %pad_maximum_fusion.refs_5_), channel_id=1, source_target_pairs={{0,1},{1,0},{2,3},{3,2},{4,5},{5,4},{6,7},{7,6},{8,9},{9,8},{10,11... | collective-permute-start | bytes 1572872 | tf_op jit(solution)/shard_map/ppermute | solution.py:20
  17.1 23.9 %collective-permute-start.4 = (bf16[512,512]{1,0:T(8,128)(2,1)S(1)}, bf16[512,512]{1,0:T(8,128)(2,1)S(1)}, u32[]{:S(2)}, u32[]{:S(2)}) collective-permute-start(bf16[512,512]{1,0:T(8,128)(2,1)S(1)} %collective-permute-done.3.refs_5_), channel_id=1, source_target_pairs={{0,1},{1,0},{2,3},{3,2},{4,5},{5,4},{6,7},{7,6},{8,9},{9,8},{10,11... | collective-permute-start | bytes 1572872 | tf_op jit(solution)/shard_map/ppermute | solution.py:20
  17.1 27.7 %collective-permute-start.11 = (bf16[512,512]{1,0:T(8,128)(2,1)S(1)}, bf16[512,512]{1,0:T(8,128)(2,1)S(1)}, u32[]{:S(2)}, u32[]{:S(2)}) collective-permute-start(bf16[512,512]{1,0:T(8,128)(2,1)S(1)} %pad_maximum_fusion.1.refs_5_), channel_id=1, source_target_pairs={{0,1},{1,0},{2,3},{3,2},{4,5},{5,4},{6,7},{7,6},{8,9},{9,8},{10,11... | collective-permute-start | bytes 1572872 | tf_op jit(solution)/shard_map/ppermute | solution.py:20
  17.6 9.9 %collective-permute-start.1 = (bf16[128,512]{1,0:T(8,128)(2,1)S(1)}, bf16[128,512]{1,0:T(8,128)(2,1)S(1)}, u32[]{:S(2)}, u32[]{:S(2)}) collective-permute-start(bf16[128,512]{1,0:T(8,128)(2,1)S(1)} %bitcast.3), channel_id=1, source_target_pairs={{0,8},{4,12},{8,0},{12,4},{1,9},{5,13},{9,1},{13,5},{2,10},{6,14},... | collective-permute-start | bytes 393224 | tf_op jit(solution)/shard_map/ppermute | solution.py:20
  27.5 20.0 %collective-permute-start.10 = (bf16[512,512]{1,0:T(8,128)(2,1)S(1)}, bf16[512,512]{1,0:T(8,128)(2,1)S(1)}, u32[]{:S(2)}, u32[]{:S(2)}) collective-permute-start(bf16[512,512]{1,0:T(8,128)(2,1)S(1)} %collective-permute-done.9.refs_5_), channel_id=1, source_target_pairs={{0,1},{1,0},{2,3},{3,2},{4,5},{5,4},{6,7},{7,6},{8,9},{9,8},{10,11... | collective-permute-start | bytes 1572872 | tf_op jit(solution)/shard_map/ppermute | solution.py:20
  27.5 6.0 %collective-permute-start = (bf16[128,512]{1,0:T(8,128)(2,1)S(1)}, bf16[128,512]{1,0:T(8,128)(2,1)S(1)}, u32[]{:S(2)}, u32[]{:S(2)}) collective-permute-start(bf16[128,512]{1,0:T(8,128)(2,1)S(1)} %bitcast.4), channel_id=1, source_target_pairs={{0,4},{4,0},{8,12},{12,8},{1,5},{5,1},{9,13},{13,9},{2,6},{6,2},{1... | collective-permute-start | bytes 393224 | tf_op jit(solution)/shard_map/ppermute | solution.py:20
  33.5 5.2 %collective-permute-start.2 = (bf16[128,512]{1,0:T(8,128)(2,1)S(1)}, bf16[128,512]{1,0:T(8,128)(2,1)S(1)}, u32[]{:S(2)}, u32[]{:S(2)}) collective-permute-start(bf16[128,512]{1,0:T(8,128)(2,1)S(1)} %collective-permute-done.1.refs_3_), channel_id=1, source_target_pairs={{0,4},{4,0},{8,12},{12,8},{1,5},{5,1},{9,13},{13,9},{2,6},{6,2},{1... | collective-permute-start | bytes 393224 | tf_op jit(solution)/shard_map/ppermute | solution.py:20
  43.0 4.0 %copy-start.1 = (f32[128,256]{1,0:T(8,128)}, f32[128,256]{1,0:T(8,128)S(1)}, u32[]{:S(2)}) copy-start(f32[128,256]{1,0:T(8,128)S(1)} %get-tuple-element.25.refs_0_) | copy-start | bytes 393220
  43.0 8.6 %collective-permute-start.7 = (bf16[128,256]{1,0:T(8,128)(2,1)S(1)}, bf16[128,256]{1,0:T(8,128)(2,1)S(1)}, u32[]{:S(2)}, u32[]{:S(2)}) collective-permute-start(bf16[128,256]{1,0:T(8,128)(2,1)S(1)} %get-tuple-element.28), channel_id=1, source_target_pairs={{0,4},{4,0},{8,12},{12,8},{1,5},{5,1},{9,13},{13,9},{2,6},{6,2},{1... | collective-permute-start | bytes 196616 | tf_op jit(solution)/shard_map/ppermute | solution.py:20
  47.0 11.4 %collective-permute-start.6 = (bf16[128,256]{1,0:T(8,128)(2,1)S(1)}, bf16[128,256]{1,0:T(8,128)(2,1)S(1)}, u32[]{:S(2)}, u32[]{:S(2)}) collective-permute-start(bf16[128,256]{1,0:T(8,128)(2,1)S(1)} %get-tuple-element.26), channel_id=1, source_target_pairs={{0,4},{4,0},{8,12},{12,8},{1,5},{5,1},{9,13},{13,9},{2,6},{6,2},{1... | collective-permute-start | bytes 196616 | tf_op jit(solution)/shard_map/ppermute | solution.py:20
  49.5 2.1 %copy-start.2 = (f32[128,256]{1,0:T(8,128)}, f32[128,256]{1,0:T(8,128)S(1)}, u32[]{:S(2)}) copy-start(f32[128,256]{1,0:T(8,128)S(1)} %get-tuple-element.33.refs_3_) | copy-start | bytes 393220
  49.5 8.9 %collective-permute-start.12 = (bf16[128,256]{1,0:T(8,128)(2,1)S(1)}, bf16[128,256]{1,0:T(8,128)(2,1)S(1)}, u32[]{:S(2)}, u32[]{:S(2)}) collective-permute-start(bf16[128,256]{1,0:T(8,128)(2,1)S(1)} %get-tuple-element.34), channel_id=1, source_target_pairs={{0,4},{4,0},{8,12},{12,8},{1,5},{5,1},{9,13},{13,9},{2,6},{6,2},{1... | collective-permute-start | bytes 196616 | tf_op jit(solution)/shard_map/ppermute | solution.py:20
  51.2 4.3 %collective-permute-start.13 = (bf16[128,256]{1,0:T(8,128)(2,1)S(1)}, bf16[128,256]{1,0:T(8,128)(2,1)S(1)}, u32[]{:S(2)}, u32[]{:S(2)}) collective-permute-start(bf16[128,256]{1,0:T(8,128)(2,1)S(1)} %get-tuple-element.36), channel_id=1, source_target_pairs={{0,4},{4,0},{8,12},{12,8},{1,5},{5,1},{9,13},{13,9},{2,6},{6,2},{1... | collective-permute-start | bytes 196616 | tf_op jit(solution)/shard_map/ppermute | solution.py:20
  51.6 7.2 %collective-permute-start.8 = (bf16[128,256]{1,0:T(8,128)(2,1)S(1)}, bf16[128,256]{1,0:T(8,128)(2,1)S(1)}, u32[]{:S(2)}, u32[]{:S(2)}) collective-permute-start(bf16[128,256]{1,0:T(8,128)(2,1)S(1)} %add_convert_fusion.1), channel_id=1, source_target_pairs={{0,8},{4,12},{8,0},{12,4},{1,9},{5,13},{9,1},{13,5},{2,10},{6,14},... | collective-permute-start | bytes 196616 | tf_op jit(solution)/shard_map/ppermute | solution.py:20
  55.5 5.2 %collective-permute-start.14 = (bf16[128,256]{1,0:T(8,128)(2,1)S(1)}, bf16[128,256]{1,0:T(8,128)(2,1)S(1)}, u32[]{:S(2)}, u32[]{:S(2)}) collective-permute-start(bf16[128,256]{1,0:T(8,128)(2,1)S(1)} %add_convert_fusion), channel_id=1, source_target_pairs={{0,8},{4,12},{8,0},{12,4},{1,9},{5,13},{9,1},{13,5},{2,10},{6,14},... | collective-permute-start | bytes 196616 | tf_op jit(solution)/shard_map/ppermute | solution.py:20
  58.4 2.3 %copy-start.4 = (bf16[128,256]{1,0:T(8,128)(2,1)}, bf16[128,256]{1,0:T(8,128)(2,1)S(1)}, u32[]{:S(2)}) copy-start(bf16[128,256]{1,0:T(8,128)(2,1)S(1)} %collective-permute-done.6.refs_1_) | copy-start | bytes 196612
  58.4 2.3 %copy-start.5 = (bf16[128,256]{1,0:T(8,128)(2,1)}, bf16[128,256]{1,0:T(8,128)(2,1)S(1)}, u32[]{:S(2)}) copy-start(bf16[128,256]{1,0:T(8,128)(2,1)S(1)} %collective-permute-done.12.refs_4_) | copy-start | bytes 196612
  58.8 1.9 %copy-start.6 = (bf16[128,256]{1,0:T(8,128)(2,1)}, bf16[128,256]{1,0:T(8,128)(2,1)S(1)}, u32[]{:S(2)}) copy-start(bf16[128,256]{1,0:T(8,128)(2,1)S(1)} %collective-permute-done.8.refs_2_) | copy-start | bytes 196612
  60.7 0.6 copy-start.7

commit v2 on v0

v2 whole, which is shorter than its diff:
```python
import functools

import jax
import jax.numpy as jnp
from jax import lax
from jax.experimental import pallas as pl
from jax.experimental.pallas import tpu as pltpu
from jax.sharding import PartitionSpec as P

HEADS = 4
HEAD_DIM = 128
CAND_BLOCK = 128
HALF_SCALE = 0.5 * HEAD_DIM ** (-0.5)
LONG = 10**10
PAIR = 2 * HEAD_DIM
VMEM_LIMIT = 48 * 1024 * 1024
PARAMS = pltpu.CompilerParams(vmem_limit_bytes=VMEM_LIMIT)
COST = pl.CostEstimate(flops=1, transcendentals=0, bytes_accessed=1)
VMEM = pl.BlockSpec(memory_space=pltpu.VMEM)


def swapped(block, axis, mask):
    size = lax.axis_size(axis)
    return lax.ppermute(block, axis, [(i, i ^ mask) for i in range(size)])


def after(block, *others):
    return lax.optimization_barrier((block, *others))[0]


def pack_kernel(queries, keys, values, *refs):
    outs, sems = refs[:-1], refs[-1]
    kept_queries, sent_queries, kept, sent = outs[0], outs[1], outs[2:6], outs[6:8]
    core = lax.rem(lax.axis_index("blk"), 2)
    count = keys.shape[0]
    copies = []

    def copy(source, target):
        copies.append(pltpu.make_async_copy(source, target, sems.at[len(copies)]))
        copies[-1].start()

    def columns(side, at, width):
        return pl.ds(pl.multiple_of(side * PAIR + at * HEAD_DIM, HEAD_DIM), width)

    copy(queries.at[:, columns(1 - core, 0, PAIR)], sent_queries)
    copy(queries.at[:, columns(core, 0, PAIR)], kept_queries)
    for at in range(2):
        copy(keys.at[:, columns(1 - core, at, HEAD_DIM)], sent[at].at[:count])
        copy(values.at[:, columns(1 - core, at, HEAD_DIM)], sent[at].at[count:])
        copy(keys.at[:, columns(core, at, HEAD_DIM)], kept[2 * at])
        copy(values.at[:, columns(core, at, HEAD_DIM)], kept[2 * at + 1])
    for each in copies:
        each.wait()


def pack(queries, keys, values):
    row_shape = jax.ShapeDtypeStruct((queries.shape[0], PAIR), queries.dtype)
    hist_shape = jax.ShapeDtypeStruct((keys.shape[0], HEAD_DIM), keys.dtype)
    sent_shape = jax.ShapeDtypeStruct((2 * keys.shape[0], HEAD_DIM), keys.dtype)
    return pl.pallas_call(
        pack_kernel,
        out_shape=[row_shape] * 2 + [hist_shape] * 4 + [sent_shape] * 2,
        in_specs=[pl.BlockSpec(memory_space=pltpu.HBM)] * 3,
        out_specs=[VMEM] * 8,
        scratch_shapes=[pltpu.SemaphoreType.DMA((10,))],
        compiler_params=PARAMS,
        cost_estimate=COST,
    )(*(pltpu.with_memory_space_constraint(x, pltpu.HBM) for x in (queries, keys, values)))


def weigh(pattern_ref, queries, keys, places, columns):
    events = keys.shape[0] // len(columns)
    scores = lax.dot_general(
        queries, keys, (((1,), (1,)), ((), ())), preferred_element_type=jnp.float32
    )
    rows = []
    for i, place in enumerate(places):
        weights = []
        for j, column in enumerate(columns):
            scale = pattern_ref[place, column].astype(jnp.float32) * HALF_SCALE
            half = scores[
                i * CAND_BLOCK : (i + 1) * CAND_BLOCK, j * events : (j + 1) * events
            ] * scale
            weights.append((half + half * jnp.tanh(half)).astype(jnp.bfloat16))
        rows.append(jnp.concatenate(weights, axis=1))
    return jnp.concatenate(rows, axis=0)


def mix(weights, values):
    return jnp.dot(weights, values, preferred_element_type=jnp.float32)


def head_rows(refs, head):
    wide = slice(head * HEAD_DIM, (head + 1) * HEAD_DIM)
    return jnp.concatenate([ref[:, wide] for ref in refs], axis=0)


def row_places(masks):
    seq, blk = lax.axis_index("seq"), lax.axis_index("blk")
    return [
        (blk ^ side) * lax.axis_size("seq") + (seq ^ mask) for mask in masks for side in (0, 1)
    ]


def hist_places(masks):
    seq, blk = lax.axis_index("seq"), lax.axis_index("blk")
    return [seq * lax.axis_size("blk") + (blk ^ mask) for mask in masks]


def early_kernel(pattern, own, near, far, *refs):
    for head in range(2):
        keys, values, out = refs[2 * head], refs[2 * head + 1], refs[4 + head]
        weights = weigh(
            pattern, head_rows((own, near, far), head), keys[...], row_places((0, 1, 2)), hist_places((0, 1))
        )
        out[...] = mix(weights, values[...])


def first_kernel(pattern, own, near, far, both, keys, values, far_hist, start, *outs):
    weights = weigh(pattern, head_rows((both,), 0), keys[...], row_places((3,)), hist_places((0, 1)))
    rest = mix(weights, values[...])
    events = keys.shape[0]
    weights = weigh(
        pattern, head_rows((own, near, far, both), 0), far_hist[:events], row_places(range(4)), hist_places((2, 3))
    )
    total = mix(weights, far_hist[events:]) + jnp.concatenate([start[...], rest], axis=0)
    near_own, near_far, sent = outs
    half = near_own.shape[0]
    near_own[...] = total[:half]
    near_far[...] = total[2 * half : 3 * half]
    sent[:half] = total[half : 2 * half].astype(sent.dtype)
    sent[half:] = total[3 * half :].astype(sent.dtype)


def weights_kernel(pattern, own, near, far, both, keys, values, far_next, rest, out):
    weights = weigh(pattern, head_rows((both,), 1), keys[...], row_places((3,)), hist_places((0, 1)))
    rest[...] = mix(weights, values[...])
    out[...] = weigh(
        pattern, head_rows((own, near, far, both), 1), far_next[: keys.shape[0]], row_places(range(4)), hist_places((2, 3))
    )


def second_kernel(weights, far_next, far_last, start, rest, *outs):
    events = far_last.shape[0]
    far_values = jnp.concatenate([far_next[2 * events :], far_last[...]], axis=0)
    total = mix(weights[...], far_values)
    total = total + jnp.concatenate([start[...], rest[...]], axis=0)
    own, others, theirs = outs
    count = own.shape[0]
    own[...] = total[:count]
    for i in range(4):
        at = 2 * i * count
        if i:
            others[(i - 1) * count : i * count] = total[at : at + count].astype(others.dtype)
        theirs[i * count : (i + 1) * count] = total[at + count : at + 2 * count].astype(theirs.dtype)


def call(kernel, outs, *inputs, flops=1):
    return pl.pallas_call(
        kernel,
        out_shape=[jax.ShapeDtypeStruct(shape, kind) for shape, kind in outs],
        in_specs=[
            pl.BlockSpec(memory_space=pltpu.SMEM) if x.dtype == jnp.int32 else VMEM for x in inputs
        ],
        out_specs=[VMEM] * len(outs),
        compiler_params=PARAMS,
        cost_estimate=pl.CostEstimate(flops=flops, transcendentals=0, bytes_accessed=1),
    )(*inputs)


def finish_kernel(gate_ref, first_mine, first_theirs, own, other, *refs):
    passed, out_ref = refs[:-1], refs[-1]
    core = lax.rem(lax.axis_index("blk"), 2)
    mine, theirs = own[...], other[...].astype(jnp.float32)
    for piece in passed:
        mine = mine + piece[:, :HEAD_DIM].astype(jnp.float32)
        theirs = theirs + piece[:, HEAD_DIM:].astype(jnp.float32)
    mine = jnp.concatenate([first_mine[...], mine], axis=1)
    theirs = jnp.concatenate([first_theirs[...], theirs], axis=1)
    squares = jnp.sum(mine * mine, axis=1, keepdims=True)
    squares = squares + jnp.sum(theirs * theirs, axis=1, keepdims=True)
    factor = lax.rsqrt(squares / (HEADS * HEAD_DIM) + 1e-05)
    first = jnp.where(core == 0, mine, theirs) * factor
    second = jnp.where(core == 0, theirs, mine) * factor
    gate = gate_ref[...].astype(jnp.float32)
    out_ref[:, :PAIR] = (first * gate[:, :PAIR]).astype(out_ref.dtype)
    out_ref[:, PAIR:] = (second * gate[:, PAIR:]).astype(out_ref.dtype)


def paired(candidates, gate_values, hist_keys, hist_values, pattern):
    count = CAND_BLOCK
    half = 2 * count
    events = hist_keys.shape[0]
    own, queries, *hists = pack(candidates[0], hist_keys, hist_values)
    beside = [swapped(hist, "blk", 1) for hist in hists[4:]]
    own = jnp.concatenate([own, swapped(queries, "blk", 1)], axis=0)
    keys, values = [], []
    for i in range(2):
        keys.append(jnp.concatenate([hists[2 * i], beside[i][:events]], axis=0))
        values.append(jnp.concatenate([hists[2 * i + 1], beside[i][events:]], axis=0))
    hist = jnp.concatenate([keys[0], values[0]], axis=0)
    far_hist = swapped(hist, "blk", 2)
    hist_next = jnp.concatenate([keys[1], values[1][:events]], axis=0)
    far_next = swapped(hist_next, "blk", 2)
    far_last = swapped(values[1][events:], "blk", 2)
    own = after(own, hist, hist_next)
    far = swapped(own, "seq", 2)
    near = swapped(own, "seq", 1)
    both = swapped(far, "seq", 1)

    f32, b16 = jnp.float32, jnp.bfloat16
    part = ((3 * half, HEAD_DIM), f32)
    early = call(
        early_kernel, [part, part], pattern, own, near, far, keys[0], values[0], keys[1], values[1]
    )
    outs = [((half, HEAD_DIM), f32), ((half, HEAD_DIM), f32), ((2 * half, HEAD_DIM), b16)]
    first = call(
        first_kernel, outs, pattern, own, near, far, both, keys[0], values[0], far_hist, early[0]
    )
    passed = swapped(first[2], "seq", 1)
    left, weights = call(
        weights_kernel,
        [((half, HEAD_DIM), f32), ((4 * half, 2 * events), b16)],
        pattern, own, near, far, both, after(keys[1], first[2]), values[1], far_next,
        flops=LONG,
    )
    folded = after(first[1], left) + passed[half:].astype(f32)
    last = swapped(folded.astype(b16), "seq", 2)
    first = first[0] + passed[:half].astype(f32) + last.astype(f32)
    first_theirs = swapped(first[count:], "blk", 1)

    outs = [((count, HEAD_DIM), f32), ((3 * count, HEAD_DIM), b16), ((4 * count, HEAD_DIM), b16)]
    own, others, theirs = call(second_kernel, outs, weights, far_next, far_last, early[1], left)
    came = swapped(theirs, "blk", 1)
    pieces = []
    for mask in (3, 2, 1):
        mine = others[(mask - 1) * count : mask * count]
        piece = jnp.concatenate([mine, came[mask * count : (mask + 1) * count]], axis=1)
        if mask == 1:
            piece, first_theirs = lax.optimization_barrier((piece, first_theirs))
        pieces.append(swapped(piece, "seq", mask))
    gate = gate_values[0]
    inputs = [gate, first[:count], first_theirs, own, came[:count], *pieces]
    return call(finish_kernel, [(gate.shape, gate.dtype)], *inputs)[0][None]


def general_kernel(places, pattern, rows, *refs):
    hists, out = refs[:-1], refs[-1]
    blk = lax.axis_index("blk")
    total = None
    for at, hist in enumerate(hists):
        weights = weigh(
            pattern, rows[...], hist[:, :HEAD_DIM], places(blk), hist_places((at,))
        )
        mixed = mix(weights, hist[:, HEAD_DIM:])
        total = mixed if total is None else total + mixed
    out[...] = total


def general_finish_kernel(gate_ref, *refs):
    sums, out_ref = refs[:-1], refs[-1]
    summed = jnp.concatenate([ref[...] for ref in sums], axis=1)
    mean_square = jnp.mean(summed * summed, axis=1, keepdims=True)
    normed = summed * lax.rsqrt(mean_square + 1e-05)
    out_ref[...] = (normed * gate_ref[...].astype(jnp.float32)).astype(out_ref.dtype)


def general(candidates, gate_values, hist_keys, hist_values, pattern):
    hists = []
    for head in range(HEADS):
        wide = slice(head * HEAD_DIM, (head + 1) * HEAD_DIM)
        hists.append(jnp.concatenate([hist_keys[:, wide], hist_values[:, wide]], axis=1))
    gathered = lax.all_gather(candidates[0], "seq", axis=0, tiled=True)
    blocks = gathered.shape[0] // CAND_BLOCK
    masks = range(lax.axis_size("blk"))

    def places(blk):
        return [blk * blocks + i for i in range(blocks)]

    sums = []
    for head in range(HEADS):
        wide = slice(head * HEAD_DIM, (head + 1) * HEAD_DIM)
        around = [swapped(hists[head], "blk", mask) if mask else hists[head] for mask in masks]
        outs = [((gathered.shape[0], HEAD_DIM), jnp.float32)]
        kernel = functools.partial(general_kernel, places)
        (total,) = call(kernel, outs, pattern, gathered[:, wide], *around)
        sums.append(lax.psum_scatter(total, "seq", scatter_dimension=0, tiled=True))
    return pl.pallas_call(
        general_finish_kernel,
        out_shape=jax.ShapeDtypeStruct(gate_values[0].shape, gate_values.dtype),
        in_specs=[VMEM] * (1 + HEADS),
        out_specs=VMEM,
    )(gate_values[0], *sums)[None]


def on_device(candidates, *others):
    if lax.axis_size("seq") == 4 and candidates.shape[1] == CAND_BLOCK:
        return paired(candidates, *others)
    return general(candidates, *others)


def solution(mesh):
    in_specs = (
        P(("groups", "blk"), "seq", None),
        P(("groups", "blk"), "seq", None),
        P(("groups", "seq", "blk"), None),
        P(("groups", "seq", "blk"), None),
        P("groups", None),
    )
    out_specs = P(("groups", "blk"), "seq", None)
    return jax.shard_map(
        on_device, mesh=mesh, in_specs=in_specs, out_specs=out_specs, check_vma=False
    )
```

time: 132 us -> 45.8 us (0.35)
  waiting for transfers between devices: 68 us -> 14 us
  starting transfers between devices: 1.84 us -> 21.5 us
  blocking collectives: 16.7 us -> 0 us
  matrix products: 16 us -> 0 us
  between operations: 13.5 us -> 0.18 us
  Pallas kernels: 0 us -> 9.62 us
  local copies, waits for them, and re-layouts: 8.41 us -> 0.08 us
  other arithmetic: 7.29 us -> 0.23 us
    reduce_scatter x1 -> x0, waiting for transfers between devices: 27.4 us -> none  [on_device(): summed = lax.psum_scatter(running, 'seq', scatter_dimension=0, tiled=True)]
    ppermute x7 -> x16, waiting for transfers between devices: 40.6 us -> 14 us  [swapped(): return lax.ppermute(block, axis, [(i, i ^ mask) for i in range(size)])]
    ppermute x7 -> x16, starting transfers between devices: 1.84 us -> 21.5 us  [swapped(): return lax.ppermute(block, axis, [(i, i ^ mask) for i in range(size)])]
    all_gather x1 -> x0, blocking collectives: 16.7 us -> none  [on_device(): queries = lax.all_gather(candidates, 'seq', axis=1, tiled=True)[0]]
    dot_general x4 -> x0, matrix products: 16 us -> none  [attend_block(): jnp.einsum('hqk,khd->qhd', weights, value_heads, preferred_element_type=j...]
    pallas_call x0 -> x6, Pallas kernels: none -> 9.62 us  [the longest x5 8.18 us: call(): pl.pallas_call(kernel, out_shape=[jax.ShapeDtypeStruct(shape, kind) for s...]
    reshape x5 -> x0, local copies, waits for them, and re-layouts: 6.02 us -> none  [the longest x4 4.99 us: attend_block(): return mixed.reshape(row_count, width)]
    add x3 -> x1, other arithmetic: 4.29 us -> 0.03 us  [paired(): first = first[0] + passed[:half].astype(f32) + last.astype(f32)]
  transfers between devices with their start and end apart: 8 -> 16, of which waited for: 8 -> 9; matrix products, arithmetic and copies ran while one was open for 19% -> 1% of each run, Pallas kernels for 0% -> 16%
where the time goes in v2:
time: 45.8 us; the launch traced here: 45.7 us
  starting transfers between devices  21.5 us (47%)
  waiting for transfers between devices  14 us (31%)
  Pallas kernels  9.62 us (21%)
    ppermute x16, starting transfers between devices, swapped(): return lax.ppermute(block, axis, [(i, i ^ mask) for i in range(size)])  21.5 us
    ppermute x16, waiting for transfers between devices, swapped(): return lax.ppermute(block, axis, [(i, i ^ mask) for i in range(size)])  14 us
    pallas_call x5, Pallas kernels, call(): pl.pallas_call(kernel, out_shape=[jax.ShapeDtypeStruct(shape, kind) for s...  8.18 us
    pallas_call x1, Pallas kernels, pack(): pl.pallas_call(pack_kernel, out_shape=[row_shape] * 2 + [hist_shape] * 4...  1.44 us
  transfers between devices with their start and end apart: 16, of which 9 were waited for; matrix products, arithmetic and copies ran while one was open for 1% of the time, Pallas kernels for 16%

profile of v2, /device:TPU:0, one launch (start us, length us, event | category | flops | bytes accessed | tf_op | source)
XLA Modules:
  0.0 45.7 jit_solution(12954540306642021114)
XLA Ops:
  0.0 1.4 %shard_map.55 = (bf16[128,256]{1,0:T(8,128)(2,1)S(1)}, bf16[128,256]{1,0:T(8,128)(2,1)S(1)}, bf16[512,128]{1,0:T(8,128)(2,1)S(1)}, bf16[512,128]{1,0:T(8,128)(2,...) custom-call(bf16[128,512]{1,0:T(8,128)(2,1)} %bitcast.4, ...), custom_call_target="tpu_custom_call" | custom-call | flops 1 | bytes 1 | tf_op jit(solution)/shard_map/pallas_call | solution.py:60
  1.4 0.5 %collective-permute-start.1 = (bf16[1024,128]{1,0:T(8,128)(2,1)S(1)}, bf16[1024,128]{1,0:T(8,128)(2,1)S(1)}, u32[]{:S(2)}, u32[]{:S(2)}) collective-permute-start(bf16[1024,128]{1,0:T(8,128)(2,1)S(1)} %get-tuple-element.31), channel_id=1, source_target_pairs={{0,1},{1,0},{2,3},{3,2},{4,5},{5,4},{6,7},{7,6},{8,9},{9,8},{10,11... | collective-permute-start | bytes 786440 | tf_op jit(solution)/shard_map/ppermute | solution.py:24
  2.0 0.1 collective-permute-start
  2.0 0.4 collective-permute-start.2
  2.5 0.7 %collective-permute-done.1 = bf16[1024,128]{1,0:T(8,128)(2,1)S(1)} collective-permute-done((bf16[1024,128]{1,0:T(8,128)(2,1)S(1)}, bf16[1024,128]{1,0:T(8,128)(2,1)S(1)}, u32[]{:S(2)}, u32[]{:S(2)}) %collective-permute-start.1) | collective-permute-done | bytes 262176 | tf_op jit(solution)/shard_map/ppermute | solution.py:24
  3.2 0.0 copy-start.1
  3.2 2.9 %collective-permute-start.6 = (bf16[2048,128]{1,0:T(8,128)(2,1)S(1)}, bf16[2048,128]{1,0:T(8,128)(2,1)S(1)}, u32[]{:S(2)}, u32[]{:S(2)}) collective-permute-start(bf16[2048,128]{1,0:T(8,128)(2,1)S(1)} %pad_maximum_fusion), channel_id=1, source_target_pairs={{0,2},{1,3},{2,0},{3,1},{4,6},{5,7},{6,4},{7,5},{8,10},{9,11},{10,... | collective-permute-start | bytes 1572872 | tf_op jit(solution)/shard_map/ppermute | solution.py:24
  6.1 0.0 collective-permute-done.2
  6.2 0.4 collective-permute-start.8
  6.6 0.0 collective-permute-done
  6.6 2.8 %collective-permute-start.4 = (bf16[256,256]{1,0:T(8,128)(2,1)S(1)}, bf16[256,256]{1,0:T(8,128)(2,1)S(1)}, u32[]{:S(2)}, u32[]{:S(2)}) collective-permute-start(bf16[256,256]{1,0:T(8,128)(2,1)S(1)} %pad_maximum_fusion.6.own), channel_id=1, source_target_pairs={{0,8},{4,12},{8,0},{12,4},{1,9},{5,13},{9,1},{13,5},{2,10},{6,14},... | collective-permute-start | bytes 393224 | tf_op jit(solution)/shard_map/ppermute | solution.py:24
  9.5 1.6 %collective-permute-start.3 = (bf16[256,256]{1,0:T(8,128)(2,1)S(1)}, bf16[256,256]{1,0:T(8,128)(2,1)S(1)}, u32[]{:S(2)}, u32[]{:S(2)}) collective-permute-start(bf16[256,256]{1,0:T(8,128)(2,1)S(1)} %pad_maximum_fusion.6.own), channel_id=1, source_target_pairs={{0,4},{4,0},{8,12},{12,8},{1,5},{5,1},{9,13},{13,9},{2,6},{6,2},{1... | collective-permute-start | bytes 393224 | tf_op jit(solution)/shard_map/ppermute | solution.py:24
  11.0 1.5 %collective-permute-start.10 = (bf16[512,128]{1,0:T(8,128)(2,1)S(1)}, bf16[512,128]{1,0:T(8,128)(2,1)S(1)}, u32[]{:S(2)}, u32[]{:S(2)}) collective-permute-start(bf16[512,128]{1,0:T(8,128)(2,1)S(1)} %get-tuple-element.51), channel_id=1, source_target_pairs={{0,2},{1,3},{2,0},{3,1},{4,6},{5,7},{6,4},{7,5},{8,10},{9,11},{10,... | collective-permute-start | bytes 393224 | tf_op jit(solution)/shard_map/ppermute | solution.py:24
  12.5 3.2 %collective-permute-done.4.far = bf16[256,256]{1,0:T(8,128)(2,1)S(1)} collective-permute-done((bf16[256,256]{1,0:T(8,128)(2,1)S(1)}, bf16[256,256]{1,0:T(8,128)(2,1)S(1)}, u32[]{:S(2)}, u32[]{:S(2)}) %collective-permute-start.4) | collective-permute-done | bytes 131104 | tf_op jit(solution)/shard_map/ppermute | solution.py:24
  15.8 0.6 %collective-permute-start.5 = (bf16[256,256]{1,0:T(8,128)(2,1)S(1)}, bf16[256,256]{1,0:T(8,128)(2,1)S(1)}, u32[]{:S(2)}, u32[]{:S(2)}) collective-permute-start(bf16[256,256]{1,0:T(8,128)(2,1)S(1)} %collective-permute-done.4.far), channel_id=1, source_target_pairs={{0,4},{4,0},{8,12},{12,8},{1,5},{5,1},{9,13},{13,9},{2,6},{6,2},{1... | collective-permute-start | bytes 393224 | tf_op jit(solution)/shard_map/ppermute | solution.py:24
  16.4 0.0 collective-permute-done.3.near
  16.4 0.0 copy-done.1
  16.4 2.6 %shard_map.56 = (f32[768,128]{1,0:T(8,128)S(1)}, f32[768,128]{1,0:T(8,128)S(1)}) custom-call(s32[16,16]{1,0:T(8,128)S(1)} %copy-done.1, bf16[256,256]{1,0:T(8,128)(2,1)S(1)} %pad_maximum_fusion.6.own, bf16[256,256]{1,0:T(8,128)(2,1)S(1)} %collective-permute-done.3.near, bf16[256,256]{1,0:T(8,128)(2,1)S(1)} %collective-permute-done.4.far, ...), custom_call_target="tpu_custom_call" | custom-call | flops 1 | bytes 1 | tf_op jit(solution)/shard_map/pallas_call | solution.py:159
  19.0 1.7 %collective-permute-done.5.both = bf16[256,256]{1,0:T(8,128)(2,1)S(1)} collective-permute-done((bf16[256,256]{1,0:T(8,128)(2,1)S(1)}, bf16[256,256]{1,0:T(8,128)(2,1)S(1)}, u32[]{:S(2)}, u32[]{:S(2)}) %collective-permute-start.5) | collective-permute-done | bytes 131104 | tf_op jit(solution)/shard_map/ppermute | solution.py:24
  20.7 0.0 collective-permute-done.6.far_hist
  20.7 2.3 %shard_map.57 = (f32[256,128]{1,0:T(8,128)S(1)}, f32[256,128]{1,0:T(8,128)S(1)}, bf16[512,128]{1,0:T(8,128)(2,1)S(1)}) custom-call(s32[16,16]{1,0:T(8,128)S(1)} %copy-done.1, bf16[256,256]{1,0:T(8,128)(2,1)S(1)} %pad_maximum_fusion.6.own, bf16[256,256]{1,0:T(8,128)(2,1)S(1)} %collective-permute-done.3.near, bf16[256,256]{1,0:T(8,128)(2,1)S(1)} %collective-permute-done.4.far, ...), custom_call_target="tpu_custom_call" | custom-call | flops 1 | bytes 1 | tf_op jit(solution)/shard_map/pallas_call | solution.py:159
  23.1 1.1 %collective-permute-start.7 = (bf16[512,128]{1,0:T(8,128)(2,1)S(1)}, bf16[512,128]{1,0:T(8,128)(2,1)S(1)}, u32[]{:S(2)}, u32[]{:S(2)}) collective-permute-start(bf16[512,128]{1,0:T(8,128)(2,1)S(1)} %get-tuple-element.39), channel_id=1, source_target_pairs={{0,4},{4,0},{8,12},{12,8},{1,5},{5,1},{9,13},{13,9},{2,6},{6,2},{1... | collective-permute-start | bytes 393224 | tf_op jit(solution)/shard_map/ppermute | solution.py:24
  24.2 3.1 %collective-permute-done.8.far_next = bf16[1536,128]{1,0:T(8,128)(2,1)S(1)} collective-permute-done((bf16[1536,128]{1,0:T(8,128)(2,1)S(1)}, bf16[1536,128]{1,0:T(8,128)(2,1)S(1)}, u32[]{:S(2)}, u32[]{:S(2)}) %collective-permute-start.8) | collective-permute-done | bytes 393248 | tf_op jit(solution)/shard_map/ppermute | solution.py:24
  27.3 1.8 %shard_map.58 = (f32[256,128]{1,0:T(8,128)S(1)}, bf16[1024,1024]{1,0:T(8,128)(2,1)S(1)}) custom-call(s32[16,16]{1,0:T(8,128)S(1)} %copy-done.1, bf16[256,256]{1,0:T(8,128)(2,1)S(1)} %pad_maximum_fusion.6.own, bf16[256,256]{1,0:T(8,128)(2,1)S(1)} %collective-permute-done.3.near, bf16[256,256]{1,0:T(8,128)(2,1)S(1)} %collective-permute-done.4.far, ...), custom_call_target="tpu_custom_call" | custom-call | flops 10000000000 | bytes 1 | tf_op jit(solution)/shard_map/pallas_call | solution.py:159
  29.0 0.6 %collective-permute-done.10.far_last = bf16[512,128]{1,0:T(8,128)(2,1)S(1)} collective-permute-done((bf16[512,128]{1,0:T(8,128)(2,1)S(1)}, bf16[512,128]{1,0:T(8,128)(2,1)S(1)}, u32[]{:S(2)}, u32[]{:S(2)}) %collective-permute-start.10) | collective-permute-done | bytes 131104 | tf_op jit(solution)/shard_map/ppermute | solution.py:24
  29.6 0.0 copy-start
  29.6 0.7 %shard_map.59 = (f32[128,128]{1,0:T(8,128)S(1)}, bf16[384,128]{1,0:T(8,128)(2,1)S(1)}, bf16[512,128]{1,0:T(8,128)(2,1)S(1)}) custom-call(bf16[1024,1024]{1,0:T(8,128)(2,1)S(1)} %get-tuple-element.44.weights, bf16[1536,128]{1,0:T(8,128)(2,1)S(1)} %collective-permute-done.8.far_next, bf16[512,128]{1,0:T(8,128)(2,1)S(1)} %collective-permute-done.10.far_last, ...), custom_call_target="tpu_custom_call" | custom-call | flops 1 | bytes 1 | tf_op jit(solution)/shard_map/pallas_call | solution.py:159
  30.3 0.1 collective-permute-start.11
  30.4 0.0 collective-permute-done.7
  30.4 2.9 %collective-permute-start.9 = (bf16[256,128]{1,0:T(8,128)(2,1)S(1)}, bf16[256,128]{1,0:T(8,128)(2,1)S(1)}, u32[]{:S(2)}, u32[]{:S(2)}) collective-permute-start(bf16[256,128]{1,0:T(8,128)(2,1)S(1)} %add_convert_fusion), channel_id=1, source_target_pairs={{0,8},{4,12},{8,0},{12,4},{1,9},{5,13},{9,1},{13,5},{2,10},{6,14},... | collective-permute-start | bytes 196616 | tf_op jit(solution)/shard_map/ppermute | solution.py:24
  33.3 0.0 collective-permute-done.11
  33.4 2.3 %collective-permute-start.13 = (bf16[128,256]{1,0:T(8,128)(2,1)S(1)}, bf16[128,256]{1,0:T(8,128)(2,1)S(1)}, u32[]{:S(2)}, u32[]{:S(2)}) collective-permute-start(bf16[128,256]{1,0:T(8,128)(2,1)S(1)} %pad_maximum_fusion.8), channel_id=1, source_target_pairs={{0,12},{4,8},{8,4},{12,0},{1,13},{5,9},{9,5},{13,1},{2,14},{6,10},... | collective-permute-start | bytes 196616 | tf_op jit(solution)/shard_map/ppermute | solution.py:24
  35.7 0.9 %collective-permute-start.14 = (bf16[128,256]{1,0:T(8,128)(2,1)S(1)}, bf16[128,256]{1,0:T(8,128)(2,1)S(1)}, u32[]{:S(2)}, u32[]{:S(2)}) collective-permute-start(bf16[128,256]{1,0:T(8,128)(2,1)S(1)} %pad_maximum_fusion.9), channel_id=1, source_target_pairs={{0,8},{4,12},{8,0},{12,4},{1,9},{5,13},{9,1},{13,5},{2,10},{6,14},... | collective-permute-start | bytes 196616 | tf_op jit(solution)/shard_map/ppermute | solution.py:24
  36.6 1.1 %collective-permute-done.9 = bf16[256,128]{1,0:T(8,128)(2,1)S(1)} collective-permute-done((bf16[256,128]{1,0:T(8,128)(2,1)S(1)}, bf16[256,128]{1,0:T(8,128)(2,1)S(1)}, u32[]{:S(2)}, u32[]{:S(2)}) %collective-permute-start.9) | collective-permute-done | bytes 65568 | tf_op jit(solution)/shard_map/ppermute | solution.py:24
  37.7 0.1 collective-permute-start.12
  37.8 1.2 %collective-permute-done.12.first_theirs = f32[128,128]{1,0:T(8,128)S(1)} collective-permute-done((f32[128,128]{1,0:T(8,128)S(1)}, f32[128,128]{1,0:T(8,128)S(1)}, u32[]{:S(2)}, u32[]{:S(2)}) %collective-permute-start.12) | collective-permute-done | bytes 65568 | tf_op jit(solution)/shard_map/ppermute | solution.py:24
  39.0 3.4 %collective-permute-start.15 = (bf16[128,256]{1,0:T(8,128)(2,1)S(1)}, bf16[128,256]{1,0:T(8,128)(2,1)S(1)}, u32[]{:S(2)}, u32[]{:S(2)}) collective-permute-start(bf16[128,256]{1,0:T(8,128)(2,1)S(1)} %pad_maximum_fusion.7), channel_id=1, source_target_pairs={{0,4},{4,0},{8,12},{12,8},{1,5},{5,1},{9,13},{13,9},{2,6},{6,2},{1... | collective-permute-start | bytes 196616 | tf_op jit(solution)/shard_map/ppermute | solution.py:24
  42.4 0.0 collective-permute-done.13.refs_0_
  42.4 0.7 %collective-permute-done.14.refs_1_ = bf16[128,256]{1,0:T(8,128)(2,1)S(1)} collective-permute-done((bf16[128,256]{1,0:T(8,128)(2,1)S(1)}, bf16[128,256]{1,0:T(8,128)(2,1)S(1)}, u32[]{:S(2)}, u32[]{:S(2)}) %collective-permute-start.14) | collective-permute-done | bytes 65568 | tf_op jit(solution)/shard_map/ppermute | solution.py:24
  43.1 1.7 %collective-permute-done.15.refs_2_ = bf16[128,256]{1,0:T(8,128)(2,1)S(1)} collective-permute-done((bf16[128,256]{1,0:T(8,128)(2,1)S(1)}, bf16[128,256]{1,0:T(8,128)(2,1)S(1)}, u32[]{:S(2)}, u32[]{:S(2)}) %collective-permute-start.15) | collective-permute-done | bytes 65568 | tf_op jit(solution)/shard_map/ppermute | solution.py:24
  44.8 0.0 copy-done
  44.8 0.8 %shard_map.60 = bf16[128,512]{1,0:T(8,128)(2,1)} custom-call(bf16[128,512]{1,0:T(8,128)(2,1)S(1)} %bitcast.3, f32[128,128]{1,0:T(8,128)S(1)} %get-tuple-element.60.first_mine, f32[128,128]{1,0:T(8,128)S(1)} %collective-permute-done.12.first_theirs, f32[128,128]{1,0:T(8,128)S(1)} %get-tuple-element.49.own, bf16[128,128]{1,0:T(8,128)(2,1)S(1)} %get-tuple-element.57.other, ...), custom_call_target="tpu_custom_call" | custom-call | flops 1 | bytes 1 | tf_op jit(solution)/shard_map/pallas_call | solution.py:159
  (15 shorter events, 0.3 us)
Async XLA Ops:
  1.4 1.7 %collective-permute-start.1 = (bf16[1024,128]{1,0:T(8,128)(2,1)S(1)}, bf16[1024,128]{1,0:T(8,128)(2,1)S(1)}, u32[]{:S(2)}, u32[]{:S(2)}) collective-permute-start(bf16[1024,128]{1,0:T(8,128)(2,1)S(1)} %get-tuple-element.31), channel_id=1, source_target_pairs={{0,1},{1,0},{2,3},{3,2},{4,5},{5,4},{6,7},{7,6},{8,9},{9,8},{10,11... | collective-permute-start | bytes 786440 | tf_op jit(solution)/shard_map/ppermute | solution.py:24
  2.0 4.7 %collective-permute-start = (bf16[128,256]{1,0:T(8,128)(2,1)S(1)}, bf16[128,256]{1,0:T(8,128)(2,1)S(1)}, u32[]{:S(2)}, u32[]{:S(2)}) collective-permute-start(bf16[128,256]{1,0:T(8,128)(2,1)S(1)} %get-tuple-element.29), channel_id=1, source_target_pairs={{0,1},{1,0},{2,3},{3,2},{4,5},{5,4},{6,7},{7,6},{8,9},{9,8},{10,11... | collective-permute-start | bytes 196616 | tf_op jit(solution)/shard_map/ppermute | solution.py:24
  2.0 4.1 %collective-permute-start.2 = (bf16[1024,128]{1,0:T(8,128)(2,1)S(1)}, bf16[1024,128]{1,0:T(8,128)(2,1)S(1)}, u32[]{:S(2)}, u32[]{:S(2)}) collective-permute-start(bf16[1024,128]{1,0:T(8,128)(2,1)S(1)} %get-tuple-element.34), channel_id=1, source_target_pairs={{0,1},{1,0},{2,3},{3,2},{4,5},{5,4},{6,7},{7,6},{8,9},{9,8},{10,11... | collective-permute-start | bytes 786440 | tf_op jit(solution)/shard_map/ppermute | solution.py:24
  3.2 13.2 %copy-start.1 = (s32[16,16]{1,0:T(8,128)S(1)}, s32[16,16]{1,0:T(8,128)}, u32[]{:S(2)}) copy-start(s32[16,16]{1,0:T(8,128)} %pattern.5) | copy-start | bytes 3076
  3.2 17.5 %collective-permute-start.6 = (bf16[2048,128]{1,0:T(8,128)(2,1)S(1)}, bf16[2048,128]{1,0:T(8,128)(2,1)S(1)}, u32[]{:S(2)}, u32[]{:S(2)}) collective-permute-start(bf16[2048,128]{1,0:T(8,128)(2,1)S(1)} %pad_maximum_fusion), channel_id=1, source_target_pairs={{0,2},{1,3},{2,0},{3,1},{4,6},{5,7},{6,4},{7,5},{8,10},{9,11},{10,... | collective-permute-start | bytes 1572872 | tf_op jit(solution)/shard_map/ppermute | solution.py:24
  6.2 21.1 %collective-permute-start.8 = (bf16[1536,128]{1,0:T(8,128)(2,1)S(1)}, bf16[1536,128]{1,0:T(8,128)(2,1)S(1)}, u32[]{:S(2)}, u32[]{:S(2)}) collective-permute-start(bf16[1536,128]{1,0:T(8,128)(2,1)S(1)} %pad_maximum_fusion.1), channel_id=1, source_target_pairs={{0,2},{1,3},{2,0},{3,1},{4,6},{5,7},{6,4},{7,5},{8,10},{9,11},{10,... | collective-permute-start | bytes 1179656 | tf_op jit(solution)/shard_map/ppermute | solution.py:24
  6.6 9.1 %collective-permute-start.4 = (bf16[256,256]{1,0:T(8,128)(2,1)S(1)}, bf16[256,256]{1,0:T(8,128)(2,1)S(1)}, u32[]{:S(2)}, u32[]{:S(2)}) collective-permute-start(bf16[256,256]{1,0:T(8,128)(2,1)S(1)} %pad_maximum_fusion.6.own), channel_id=1, source_target_pairs={{0,8},{4,12},{8,0},{12,4},{1,9},{5,13},{9,1},{13,5},{2,10},{6,14},... | collective-permute-start | bytes 393224 | tf_op jit(solution)/shard_map/ppermute | solution.py:24
  9.5 7.0 %collective-permute-start.3 = (bf16[256,256]{1,0:T(8,128)(2,1)S(1)}, bf16[256,256]{1,0:T(8,128)(2,1)S(1)}, u32[]{:S(2)}, u32[]{:S(2)}) collective-permute-start(bf16[256,256]{1,0:T(8,128)(2,1)S(1)} %pad_maximum_fusion.6.own), channel_id=1, source_target_pairs={{0,4},{4,0},{8,12},{12,8},{1,5},{5,1},{9,13},{13,9},{2,6},{6,2},{1... | collective-permute-start | bytes 393224 | tf_op jit(solution)/shard_map/ppermute | solution.py:24
  11.0 18.6 %collective-permute-start.10 = (bf16[512,128]{1,0:T(8,128)(2,1)S(1)}, bf16[512,128]{1,0:T(8,128)(2,1)S(1)}, u32[]{:S(2)}, u32[]{:S(2)}) collective-permute-start(bf16[512,128]{1,0:T(8,128)(2,1)S(1)} %get-tuple-element.51), channel_id=1, source_target_pairs={{0,2},{1,3},{2,0},{3,1},{4,6},{5,7},{6,4},{7,5},{8,10},{9,11},{10,... | collective-permute-start | bytes 393224 | tf_op jit(solution)/shard_map/ppermute | solution.py:24
  15.8 5.0 %collective-permute-start.5 = (bf16[256,256]{1,0:T(8,128)(2,1)S(1)}, bf16[256,256]{1,0:T(8,128)(2,1)S(1)}, u32[]{:S(2)}, u32[]{:S(2)}) collective-permute-start(bf16[256,256]{1,0:T(8,128)(2,1)S(1)} %collective-permute-done.4.far), channel_id=1, source_target_pairs={{0,4},{4,0},{8,12},{12,8},{1,5},{5,1},{9,13},{13,9},{2,6},{6,2},{1... | collective-permute-start | bytes 393224 | tf_op jit(solution)/shard_map/ppermute | solution.py:24
  23.1 7.3 %collective-permute-start.7 = (bf16[512,128]{1,0:T(8,128)(2,1)S(1)}, bf16[512,128]{1,0:T(8,128)(2,1)S(1)}, u32[]{:S(2)}, u32[]{:S(2)}) collective-permute-start(bf16[512,128]{1,0:T(8,128)(2,1)S(1)} %get-tuple-element.39), channel_id=1, source_target_pairs={{0,4},{4,0},{8,12},{12,8},{1,5},{5,1},{9,13},{13,9},{2,6},{6,2},{1... | collective-permute-start | bytes 393224 | tf_op jit(solution)/shard_map/ppermute | solution.py:24
  29.6 15.2 %copy-start = (bf16[1,128,512]{2,1,0:T(8,128)(2,1)S(1)}, bf16[1,128,512]{2,1,0:T(8,128)(2,1)}, u32[]{:S(2)}) copy-start(bf16[1,128,512]{2,1,0:T(8,128)(2,1)} %param.6) | copy-start | bytes 393220
  30.3 3.0 %collective-permute-start.11 = (bf16[512,128]{1,0:T(8,128)(2,1)S(1)}, bf16[512,128]{1,0:T(8,128)(2,1)S(1)}, u32[]{:S(2)}, u32[]{:S(2)}) collective-permute-start(bf16[512,128]{1,0:T(8,128)(2,1)S(1)} %get-tuple-element.47), channel_id=1, source_target_pairs={{0,1},{1,0},{2,3},{3,2},{4,5},{5,4},{6,7},{7,6},{8,9},{9,8},{10,11... | collective-permute-start | bytes 393224 | tf_op jit(solution)/shard_map/ppermute | solution.py:24
  30.4 7.2 %collective-permute-start.9 = (bf16[256,128]{1,0:T(8,128)(2,1)S(1)}, bf16[256,128]{1,0:T(8,128)(2,1)S(1)}, u32[]{:S(2)}, u32[]{:S(2)}) collective-permute-start(bf16[256,128]{1,0:T(8,128)(2,1)S(1)} %add_convert_fusion), channel_id=1, source_target_pairs={{0,8},{4,12},{8,0},{12,4},{1,9},{5,13},{9,1},{13,5},{2,10},{6,14},... | collective-permute-start | bytes 196616 | tf_op jit(solution)/shard_map/ppermute | solution.py:24
  33.4 9.1 %collective-permute-start.13 = (bf16[128,256]{1,0:T(8,128)(2,1)S(1)}, bf16[128,256]{1,0:T(8,128)(2,1)S(1)}, u32[]{:S(2)}, u32[]{:S(2)}) collective-permute-start(bf16[128,256]{1,0:T(8,128)(2,1)S(1)} %pad_maximum_fusion.8), channel_id=1, source_target_pairs={{0,12},{4,8},{8,4},{12,0},{1,13},{5,9},{9,5},{13,1},{2,14},{6,10},... | collective-permute-start | bytes 196616 | tf_op jit(solution)/shard_map/ppermute | solution.py:24
  35.7 7.4 %collective-permute-start.14 = (bf16[128,256]{1,0:T(8,128)(2,1)S(1)}, bf16[128,256]{1,0:T(8,128)(2,1)S(1)}, u32[]{:S(2)}, u32[]{:S(2)}) collective-permute-start(bf16[128,256]{1,0:T(8,128)(2,1)S(1)} %pad_maximum_fusion.9), channel_id=1, source_target_pairs={{0,8},{4,12},{8,0},{12,4},{1,9},{5,13},{9,1},{13,5},{2,10},{6,14},... | collective-permute-start | bytes 196616 | tf_op jit(solution)/shard_map/ppermute | solution.py:24
  37.7 1.3 %collective-permute-start.12 = (f32[128,128]{1,0:T(8,128)S(1)}, f32[128,128]{1,0:T(8,128)S(1)}, u32[]{:S(2)}, u32[]{:S(2)}) collective-permute-start(f32[128,128]{1,0:T(8,128)S(1)} %get-tuple-element.59), channel_id=1, source_target_pairs={{0,1},{1,0},{2,3},{3,2},{4,5},{5,4},{6,7},{7,6},{8,9},{9,8},{10,11... | collective-permute-start | bytes 196616 | tf_op jit(solution)/shard_map/ppermute | solution.py:24
  39.0 5.8 %collective-permute-start.15 = (bf16[128,256]{1,0:T(8,128)(2,1)S(1)}, bf16[128,256]{1,0:T(8,128)(2,1)S(1)}, u32[]{:S(2)}, u32[]{:S(2)}) collective-permute-start(bf16[128,256]{1,0:T(8,128)(2,1)S(1)} %pad_maximum_fusion.7), channel_id=1, source_target_pairs={{0,4},{4,0},{8,12},{12,8},{1,5},{5,1},{9,13},{13,9},{2,6},{6,2},{1... | collective-permute-start | bytes 196616 | tf_op jit(solution)/shard_map/ppermute | solution.py:24

commit v3 on v2

--- a/solution.py
+++ b/solution.py
@@ -30,7 +30,7 @@
 
 def pack_kernel(queries, keys, values, *refs):
     outs, sems = refs[:-1], refs[-1]
-    kept_queries, sent_queries, kept, sent = outs[0], outs[1], outs[2:6], outs[6:8]
+    kept_queries, sent_queries, kept, sent = outs[0], outs[1], outs[2:4], outs[4:]
     core = lax.rem(lax.axis_index("blk"), 2)
     count = keys.shape[0]
     copies = []
@@ -44,24 +44,24 @@
 
     copy(queries.at[:, columns(1 - core, 0, PAIR)], sent_queries)
     copy(queries.at[:, columns(core, 0, PAIR)], kept_queries)
+    targets = [part for block in sent for part in (block.at[:count], block.at[count:])]
     for at in range(2):
-        copy(keys.at[:, columns(1 - core, at, HEAD_DIM)], sent[at].at[:count])
-        copy(values.at[:, columns(1 - core, at, HEAD_DIM)], sent[at].at[count:])
-        copy(keys.at[:, columns(core, at, HEAD_DIM)], kept[2 * at])
-        copy(values.at[:, columns(core, at, HEAD_DIM)], kept[2 * at + 1])
+        copy(keys.at[:, columns(core, at, HEAD_DIM)], kept[at].at[:count])
+        copy(values.at[:, columns(core, at, HEAD_DIM)], kept[at].at[count:])
+        copy(keys.at[:, columns(1 - core, at, HEAD_DIM)], targets[2 * at])
+        copy(values.at[:, columns(1 - core, at, HEAD_DIM)], targets[2 * at + 1])
     for each in copies:
         each.wait()
 
 
 def pack(queries, keys, values):
     row_shape = jax.ShapeDtypeStruct((queries.shape[0], PAIR), queries.dtype)
-    hist_shape = jax.ShapeDtypeStruct((keys.shape[0], HEAD_DIM), keys.dtype)
-    sent_shape = jax.ShapeDtypeStruct((2 * keys.shape[0], HEAD_DIM), keys.dtype)
+    both_shape = jax.ShapeDtypeStruct((2 * keys.shape[0], HEAD_DIM), keys.dtype)
     return pl.pallas_call(
         pack_kernel,
-        out_shape=[row_shape] * 2 + [hist_shape] * 4 + [sent_shape] * 2,
+        out_shape=[row_shape] * 2 + [both_shape] * 4,
         in_specs=[pl.BlockSpec(memory_space=pltpu.HBM)] * 3,
-        out_specs=[VMEM] * 8,
+        out_specs=[VMEM] * 6,
         scratch_shapes=[pltpu.SemaphoreType.DMA((10,))],
         compiler_params=PARAMS,
         cost_estimate=COST,
@@ -107,44 +107,51 @@
     return [seq * lax.axis_size("blk") + (blk ^ mask) for mask in masks]
 
 
-def early_kernel(pattern, own, near, far, *refs):
-    for head in range(2):
-        keys, values, out = refs[2 * head], refs[2 * head + 1], refs[4 + head]
-        weights = weigh(
-            pattern, head_rows((own, near, far), head), keys[...], row_places((0, 1, 2)), hist_places((0, 1))
-        )
-        out[...] = mix(weights, values[...])
-
-
-def first_kernel(pattern, own, near, far, both, keys, values, far_hist, start, *outs):
-    weights = weigh(pattern, head_rows((both,), 0), keys[...], row_places((3,)), hist_places((0, 1)))
-    rest = mix(weights, values[...])
-    events = keys.shape[0]
+def joined(hists):
+    events = hists[0].shape[0] // 2
+    keys = jnp.concatenate([hist[:events] for hist in hists], axis=0)
+    return keys, jnp.concatenate([hist[events:] for hist in hists], axis=0)
+
+
+def sums_kernel(head, row_masks, hist_masks, pattern, *refs):
+    rows, refs = refs[: len(row_masks)], refs[len(row_masks) :]
+    hists, refs = refs[: len(hist_masks)], refs[len(hist_masks) :]
+    keys, values = joined(hists)
     weights = weigh(
-        pattern, head_rows((own, near, far, both), 0), far_hist[:events], row_places(range(4)), hist_places((2, 3))
-    )
-    total = mix(weights, far_hist[events:]) + jnp.concatenate([start[...], rest], axis=0)
-    near_own, near_far, sent = outs
-    half = near_own.shape[0]
-    near_own[...] = total[:half]
-    near_far[...] = total[2 * half : 3 * half]
-    sent[:half] = total[half : 2 * half].astype(sent.dtype)
-    sent[half:] = total[3 * half :].astype(sent.dtype)
-
-
-def weights_kernel(pattern, own, near, far, both, keys, values, far_next, rest, out):
-    weights = weigh(pattern, head_rows((both,), 1), keys[...], row_places((3,)), hist_places((0, 1)))
-    rest[...] = mix(weights, values[...])
-    out[...] = weigh(
-        pattern, head_rows((own, near, far, both), 1), far_next[: keys.shape[0]], row_places(range(4)), hist_places((2, 3))
-    )
-
-
-def second_kernel(weights, far_next, far_last, start, rest, *outs):
-    events = far_last.shape[0]
-    far_values = jnp.concatenate([far_next[2 * events :], far_last[...]], axis=0)
-    total = mix(weights[...], far_values)
-    total = total + jnp.concatenate([start[...], rest[...]], axis=0)
+        pattern, head_rows(rows, head), keys, row_places(row_masks), hist_places(hist_masks)
+    )
+    total = mix(weights, values)
+    if refs[0].shape == total.shape and len(refs) > 1:
+        total, refs = total + refs[0][...], refs[1:]
+    done = 0
+    for out in refs:
+        out[...] = total[done : done + out.shape[0]].astype(out.dtype)
+        done += out.shape[0]
+
+
+def both_kernel(pattern, both, kept, beside, straight, diagonal, far_sums, out):
+    half = far_sums.shape[0]
+    keys, values = joined((kept, beside, straight, diagonal))
+    weights = weigh(pattern, head_rows((both,), 0), keys, row_places((3,)), hist_places(range(4)))
+    out[:half] = far_sums[...]
+    out[half:] = mix(weights, values).astype(out.dtype)
+
+
+def weights_kernel(pattern, own, near, far, both, kept, beside, straight, start, out):
+    rows = head_rows((own, near, far, both), 1)
+    keys, values = joined((kept, beside))
+    weights = weigh(pattern, rows, keys, row_places(range(4)), hist_places((0, 1)))
+    start[...] = mix(weights, values)
+    events = straight.shape[0] // 2
+    out[...] = weigh(pattern, rows, straight[:events], row_places(range(4)), hist_places((2,)))
+
+
+def second_kernel(pattern, own, near, far, both, straight, diagonal, weights, start, *outs):
+    rows = head_rows((own, near, far, both), 1)
+    events = straight.shape[0] // 2
+    late = weigh(pattern, rows, diagonal[:events], row_places(range(4)), hist_places((3,)))
+    values = jnp.concatenate([straight[events:], diagonal[events:]], axis=0)
+    total = mix(jnp.concatenate([weights[...], late], axis=1), values) + start[...]
     own, others, theirs = outs
     count = own.shape[0]
     own[...] = total[:count]
@@ -192,52 +199,55 @@
     half = 2 * count
     events = hist_keys.shape[0]
     own, queries, *hists = pack(candidates[0], hist_keys, hist_values)
-    beside = [swapped(hist, "blk", 1) for hist in hists[4:]]
+    kept, sent = hists[:2], hists[2:]
+    straight = [swapped(x, "blk", 2) for x in kept]
+    diagonal = [swapped(x, "blk", 3) for x in sent]
     own = jnp.concatenate([own, swapped(queries, "blk", 1)], axis=0)
-    keys, values = [], []
-    for i in range(2):
-        keys.append(jnp.concatenate([hists[2 * i], beside[i][:events]], axis=0))
-        values.append(jnp.concatenate([hists[2 * i + 1], beside[i][events:]], axis=0))
-    hist = jnp.concatenate([keys[0], values[0]], axis=0)
-    far_hist = swapped(hist, "blk", 2)
-    hist_next = jnp.concatenate([keys[1], values[1][:events]], axis=0)
-    far_next = swapped(hist_next, "blk", 2)
-    far_last = swapped(values[1][events:], "blk", 2)
-    own = after(own, hist, hist_next)
+    beside = [swapped(x, "blk", 1) for x in sent]
+    own = after(own, *beside)
     far = swapped(own, "seq", 2)
     near = swapped(own, "seq", 1)
     both = swapped(far, "seq", 1)
 
     f32, b16 = jnp.float32, jnp.bfloat16
-    part = ((3 * half, HEAD_DIM), f32)
+    rows, three = (own, near, far, both), (own, near, far)
+    part = ((half, HEAD_DIM), f32)
     early = call(
-        early_kernel, [part, part], pattern, own, near, far, keys[0], values[0], keys[1], values[1]
-    )
-    outs = [((half, HEAD_DIM), f32), ((half, HEAD_DIM), f32), ((2 * half, HEAD_DIM), b16)]
-    first = call(
-        first_kernel, outs, pattern, own, near, far, both, keys[0], values[0], far_hist, early[0]
-    )
-    passed = swapped(first[2], "seq", 1)
-    left, weights = call(
+        functools.partial(sums_kernel, 0, (0, 1, 2), (0, 1)),
+        [((3 * half, HEAD_DIM), f32)],
+        pattern, *three, kept[0], beside[0],
+    )
+    first, first_near, sums = call(
+        functools.partial(sums_kernel, 0, (0, 1, 2), (2, 3)),
+        [part, part, ((half, HEAD_DIM), b16)],
+        pattern, *three, straight[0], diagonal[0], *early,
+    )
+    (sums,) = call(
+        both_kernel,
+        [((2 * half, HEAD_DIM), b16)],
+        pattern, both, kept[0], beside[0], straight[0], diagonal[0], sums,
+    )
+    passed = swapped(sums, "seq", 2)
+    start, weights = call(
         weights_kernel,
-        [((half, HEAD_DIM), f32), ((4 * half, 2 * events), b16)],
-        pattern, own, near, far, both, after(keys[1], first[2]), values[1], far_next,
+        [((4 * half, HEAD_DIM), f32), ((4 * half, events), b16)],
+        pattern, *rows, after(kept[1], sums), beside[1], straight[1],
         flops=LONG,
     )
-    folded = after(first[1], left) + passed[half:].astype(f32)
-    last = swapped(folded.astype(b16), "seq", 2)
-    first = first[0] + passed[:half].astype(f32) + last.astype(f32)
+    folded = first_near + passed[half:].astype(f32)
+    last = swapped(folded.astype(b16), "seq", 1)
+    first = first + passed[:half].astype(f32) + last.astype(f32)
     first_theirs = swapped(first[count:], "blk", 1)
 
     outs = [((count, HEAD_DIM), f32), ((3 * count, HEAD_DIM), b16), ((4 * count, HEAD_DIM), b16)]
-    own, others, theirs = call(second_kernel, outs, weights, far_next, far_last, early[1], left)
+    own, others, theirs = call(
+        second_kernel, outs, pattern, *rows, straight[1], diagonal[1], weights, start, flops=LONG
+    )
     came = swapped(theirs, "blk", 1)
     pieces = []
-    for mask in (3, 2, 1):
+    for mask in (2, 3, 1):
         mine = others[(mask - 1) * count : mask * count]
         piece = jnp.concatenate([mine, came[mask * count : (mask + 1) * count]], axis=1)
-        if mask == 1:
-            piece, first_theirs = lax.optimization_barrier((piece, first_theirs))
         pieces.append(swapped(piece, "seq", mask))
     gate = gate_values[0]
     inputs = [gate, first[:count], first_theirs, own, came[:count], *pieces]

time: 45.8 us -> 42.4 us (0.926)
  starting transfers between devices: 21.5 us -> 19.2 us
  waiting for transfers between devices: 14 us -> 11.7 us
  Pallas kernels: 9.62 us -> 11.1 us
    ppermute x16 -> x17, starting transfers between devices: 21.5 us -> 19.2 us  [swapped(): return lax.ppermute(block, axis, [(i, i ^ mask) for i in range(size)])]
    ppermute x16 -> x17, waiting for transfers between devices: 14 us -> 11.7 us  [swapped(): return lax.ppermute(block, axis, [(i, i ^ mask) for i in range(size)])]
    pallas_call x5 -> x6, Pallas kernels: 8.18 us -> 9.68 us  [call(): pl.pallas_call(kernel, out_shape=[jax.ShapeDtypeStruct(shape, kind) for s...]
  transfers between devices with their start and end apart: 16 -> 17, of which waited for: 9 -> 7; matrix products, arithmetic and copies ran while one was open for 1% -> 0% of each run, Pallas kernels for 16% -> 21%
where the time goes in v3:
time: 42.4 us; the launch traced here: 42.3 us
  starting transfers between devices  19.2 us (45%)
  waiting for transfers between devices  11.7 us (28%)
  Pallas kernels  11.1 us (26%)
    ppermute x17, starting transfers between devices, swapped(): return lax.ppermute(block, axis, [(i, i ^ mask) for i in range(size)])  19.2 us
    ppermute x17, waiting for transfers between devices, swapped(): return lax.ppermute(block, axis, [(i, i ^ mask) for i in range(size)])  11.7 us
    pallas_call x6, Pallas kernels, call(): pl.pallas_call(kernel, out_shape=[jax.ShapeDtypeStruct(shape, kind) for s...  9.68 us
    pallas_call x1, Pallas kernels, pack(): pl.pallas_call(pack_kernel, out_shape=[row_shape] * 2 + [both_shape] * 4,...  1.44 us
  transfers between devices with their start and end apart: 17, of which 7 were waited for; matrix products, arithmetic and copies ran while one was open for 0% of the time, Pallas kernels for 21%

profile of v3, /device:TPU:0, one launch (start us, length us, event | category | flops | bytes accessed | tf_op | source)
XLA Modules:
  0.0 42.3 jit_solution(2094310178946227070)
XLA Ops:
  0.0 1.4 %shard_map.55 = (bf16[128,256]{1,0:T(8,128)(2,1)S(1)}, bf16[128,256]{1,0:T(8,128)(2,1)S(1)}, bf16[1024,128]{1,0:T(8,128)(2,1)S(1)}, bf16[1024,128]{1,0:T(8,128)(...) custom-call(bf16[128,512]{1,0:T(8,128)(2,1)} %bitcast.4, bf16[512,512]{1,0:T(8,128)(2,1)} %keys.1, ...), custom_call_target="tpu_custom_call" | custom-call | flops 1 | bytes 1 | tf_op jit(solution)/shard_map/pallas_call | solution.py:60
  1.4 0.5 %collective-permute-start.1 = (bf16[1024,128]{1,0:T(8,128)(2,1)S(1)}, bf16[1024,128]{1,0:T(8,128)(2,1)S(1)}, u32[]{:S(2)}, u32[]{:S(2)}) collective-permute-start(bf16[1024,128]{1,0:T(8,128)(2,1)S(1)} %get-tuple-element.23), channel_id=1, source_target_pairs={{0,1},{1,0},{2,3},{3,2},{4,5},{5,4},{6,7},{7,6},{8,9},{9,8},{10,11... | collective-permute-start | bytes 786440 | tf_op jit(solution)/shard_map/ppermute | solution.py:24
  2.0 0.1 collective-permute-start.2
  2.0 0.4 %collective-permute-start = (bf16[128,256]{1,0:T(8,128)(2,1)S(1)}, bf16[128,256]{1,0:T(8,128)(2,1)S(1)}, u32[]{:S(2)}, u32[]{:S(2)}) collective-permute-start(bf16[128,256]{1,0:T(8,128)(2,1)S(1)} %get-tuple-element.22), channel_id=1, source_target_pairs={{0,1},{1,0},{2,3},{3,2},{4,5},{5,4},{6,7},{7,6},{8,9},{9,8},{10,11... | collective-permute-start | bytes 196616 | tf_op jit(solution)/shard_map/ppermute | solution.py:24
  2.5 2.6 %collective-permute-start.6 = (bf16[1024,128]{1,0:T(8,128)(2,1)S(1)}, bf16[1024,128]{1,0:T(8,128)(2,1)S(1)}, u32[]{:S(2)}, u32[]{:S(2)}) collective-permute-start(bf16[1024,128]{1,0:T(8,128)(2,1)S(1)} %get-tuple-element.23), channel_id=1, source_target_pairs={{0,3},{1,2},{2,1},{3,0},{4,7},{5,6},{6,5},{7,4},{8,11},{9,10},{10,... | collective-permute-start | bytes 786440 | tf_op jit(solution)/shard_map/ppermute | solution.py:24
  5.1 0.0 collective-permute-start.5
  5.1 0.0 collective-permute-done
  5.1 0.0 copy-start.1
  5.1 0.0 collective-permute-done.1.refs_4_.beside
  5.1 0.0 collective-permute-done.2.beside
  5.1 3.2 %collective-permute-start.4 = (bf16[256,256]{1,0:T(8,128)(2,1)S(1)}, bf16[256,256]{1,0:T(8,128)(2,1)S(1)}, u32[]{:S(2)}, u32[]{:S(2)}) collective-permute-start(bf16[256,256]{1,0:T(8,128)(2,1)S(1)} %pad_maximum_fusion.refs_0_.own), channel_id=1, source_target_pairs={{0,8},{4,12},{8,0},{12,4},{1,9},{5,13},{9,1},{13,5},{2,10},{6,14},... | collective-permute-start | bytes 393224 | tf_op jit(solution)/shard_map/ppermute | solution.py:24
  8.3 1.5 %collective-permute-start.11 = (bf16[1024,128]{1,0:T(8,128)(2,1)S(1)}, bf16[1024,128]{1,0:T(8,128)(2,1)S(1)}, u32[]{:S(2)}, u32[]{:S(2)}) collective-permute-start(bf16[1024,128]{1,0:T(8,128)(2,1)S(1)} %get-tuple-element.31.kept), channel_id=1, source_target_pairs={{0,2},{1,3},{2,0},{3,1},{4,6},{5,7},{6,4},{7,5},{8,10},{9,11},{10,... | collective-permute-start | bytes 786440 | tf_op jit(solution)/shard_map/ppermute | solution.py:24
  9.8 1.6 %collective-permute-start.3 = (bf16[256,256]{1,0:T(8,128)(2,1)S(1)}, bf16[256,256]{1,0:T(8,128)(2,1)S(1)}, u32[]{:S(2)}, u32[]{:S(2)}) collective-permute-start(bf16[256,256]{1,0:T(8,128)(2,1)S(1)} %pad_maximum_fusion.refs_0_.own), channel_id=1, source_target_pairs={{0,4},{4,0},{8,12},{12,8},{1,5},{5,1},{9,13},{13,9},{2,6},{6,2},{1... | collective-permute-start | bytes 393224 | tf_op jit(solution)/shard_map/ppermute | solution.py:24
  11.4 3.3 %collective-permute-done.4.refs_2_.far = bf16[256,256]{1,0:T(8,128)(2,1)S(1)} collective-permute-done((bf16[256,256]{1,0:T(8,128)(2,1)S(1)}, bf16[256,256]{1,0:T(8,128)(2,1)S(1)}, u32[]{:S(2)}, u32[]{:S(2)}) %collective-permute-start.4) | collective-permute-done | bytes 131104 | tf_op jit(solution)/shard_map/ppermute | solution.py:24
  14.7 0.7 %collective-permute-start.7 = (bf16[256,256]{1,0:T(8,128)(2,1)S(1)}, bf16[256,256]{1,0:T(8,128)(2,1)S(1)}, u32[]{:S(2)}, u32[]{:S(2)}) collective-permute-start(bf16[256,256]{1,0:T(8,128)(2,1)S(1)} %collective-permute-done.4.refs_2_.far), channel_id=1, source_target_pairs={{0,4},{4,0},{8,12},{12,8},{1,5},{5,1},{9,13},{13,9},{2,6},{6,2},{1... | collective-permute-start | bytes 393224 | tf_op jit(solution)/shard_map/ppermute | solution.py:24
  15.3 0.7 %collective-permute-done.3.refs_1_.near = bf16[256,256]{1,0:T(8,128)(2,1)S(1)} collective-permute-done((bf16[256,256]{1,0:T(8,128)(2,1)S(1)}, bf16[256,256]{1,0:T(8,128)(2,1)S(1)}, u32[]{:S(2)}, u32[]{:S(2)}) %collective-permute-start.3) | collective-permute-done | bytes 131104 | tf_op jit(solution)/shard_map/ppermute | solution.py:24
  16.1 0.1 collective-permute-start.12
  16.1 0.0 copy-done.1
  16.1 1.7 %shard_map.56.refs_5_ = f32[768,128]{1,0:T(8,128)S(1)} custom-call(s32[16,16]{1,0:T(8,128)S(1)} %copy-done.1, bf16[256,256]{1,0:T(8,128)(2,1)S(1)} %pad_maximum_fusion.refs_0_.own, bf16[256,256]{1,0:T(8,128)(2,1)S(1)} %collective-permute-done.3.refs_1_.near, bf16[256,256]{1,0:T(8,128)(2,1)S(1)} %collective-permute-done.4.refs_2_.far, ...), custom_call_target="tpu_custom_call" | custom-call | flops 1 | bytes 1 | tf_op jit(solution)/shard_map/pallas_call | solution.py:166
  17.9 0.0 collective-permute-done.5.refs_3_.straight
  17.9 0.0 collective-permute-done.6.refs_4_.diagonal
  17.9 1.8 %shard_map.57 = (f32[256,128]{1,0:T(8,128)S(1)}, f32[256,128]{1,0:T(8,128)S(1)}, bf16[256,128]{1,0:T(8,128)(2,1)S(1)}) custom-call(s32[16,16]{1,0:T(8,128)S(1)} %copy-done.1, bf16[256,256]{1,0:T(8,128)(2,1)S(1)} %pad_maximum_fusion.refs_0_.own, bf16[256,256]{1,0:T(8,128)(2,1)S(1)} %collective-permute-done.3.refs_1_.near, ...), custom_call_target="tpu_custom_call" | custom-call | flops 1 | bytes 1 | tf_op jit(solution)/shard_map/pallas_call | solution.py:166
  19.7 0.0 collective-permute-done.7.both
  19.7 1.4 %shard_map.58 = bf16[512,128]{1,0:T(8,128)(2,1)S(1)} custom-call(s32[16,16]{1,0:T(8,128)S(1)} %copy-done.1, bf16[256,256]{1,0:T(8,128)(2,1)S(1)} %collective-permute-done.7.both, bf16[1024,128]{1,0:T(8,128)(2,1)S(1)} %get-tuple-element.26.refs_3_.kept, bf16[1024,128]{1,0:T(8,128)(2,1)S(1)} %collective-permute-done.1.refs_4_.beside, ...), custom_call_target="tpu_custom_call" | custom-call | flops 1 | bytes 1 | tf_op jit(solution)/shard_map/pallas_call | solution.py:166
  21.1 3.4 %collective-permute-start.8 = (bf16[512,128]{1,0:T(8,128)(2,1)S(1)}, bf16[512,128]{1,0:T(8,128)(2,1)S(1)}, u32[]{:S(2)}, u32[]{:S(2)}) collective-permute-start(bf16[512,128]{1,0:T(8,128)(2,1)S(1)} %shard_map.58), channel_id=1, source_target_pairs={{0,8},{4,12},{8,0},{12,4},{1,9},{5,13},{9,1},{13,5},{2,10},{6,14},... | collective-permute-start | bytes 393224 | tf_op jit(solution)/shard_map/ppermute | solution.py:24
  24.6 0.0 collective-permute-done.11.straight
  24.6 2.3 %shard_map.59 = (f32[1024,128]{1,0:T(8,128)S(1)}, bf16[1024,512]{1,0:T(8,128)(2,1)S(1)}) custom-call(s32[16,16]{1,0:T(8,128)S(1)} %copy-done.1, bf16[256,256]{1,0:T(8,128)(2,1)S(1)} %pad_maximum_fusion.refs_0_.own, bf16[256,256]{1,0:T(8,128)(2,1)S(1)} %collective-permute-done.3.refs_1_.near, bf16[256,256]{1,0:T(8,128)(2,1)S(1)} %collective-permute-done.4.refs_2_.far, ...), custom_call_target="tpu_custom_call" | custom-call | flops 10000000000 | bytes 1 | tf_op jit(solution)/shard_map/pallas_call | solution.py:166
  26.9 1.7 %collective-permute-done.12.diagonal = bf16[1024,128]{1,0:T(8,128)(2,1)S(1)} collective-permute-done((bf16[1024,128]{1,0:T(8,128)(2,1)S(1)}, bf16[1024,128]{1,0:T(8,128)(2,1)S(1)}, u32[]{:S(2)}, u32[]{:S(2)}) %collective-permute-start.12) | collective-permute-done | bytes 262176 | tf_op jit(solution)/shard_map/ppermute | solution.py:24
  28.5 1.7 %shard_map.60 = (f32[128,128]{1,0:T(8,128)S(1)}, bf16[384,128]{1,0:T(8,128)(2,1)S(1)}, bf16[512,128]{1,0:T(8,128)(2,1)S(1)}) custom-call(s32[16,16]{1,0:T(8,128)S(1)} %copy-done.1, bf16[256,256]{1,0:T(8,128)(2,1)S(1)} %pad_maximum_fusion.refs_0_.own, bf16[256,256]{1,0:T(8,128)(2,1)S(1)} %collective-permute-done.3.refs_1_.near, ...), custom_call_target="tpu_custom_call" | custom-call | flops 10000000000 | bytes 1 | tf_op jit(solution)/shard_map/pallas_call | solution.py:166
  30.2 0.4 %collective-permute-start.13 = (bf16[512,128]{1,0:T(8,128)(2,1)S(1)}, bf16[512,128]{1,0:T(8,128)(2,1)S(1)}, u32[]{:S(2)}, u32[]{:S(2)}) collective-permute-start(bf16[512,128]{1,0:T(8,128)(2,1)S(1)} %get-tuple-element.35), channel_id=1, source_target_pairs={{0,1},{1,0},{2,3},{3,2},{4,5},{5,4},{6,7},{7,6},{8,9},{9,8},{10,11... | collective-permute-start | bytes 393224 | tf_op jit(solution)/shard_map/ppermute | solution.py:24
  30.6 1.0 %collective-permute-done.8 = bf16[512,128]{1,0:T(8,128)(2,1)S(1)} collective-permute-done((bf16[512,128]{1,0:T(8,128)(2,1)S(1)}, bf16[512,128]{1,0:T(8,128)(2,1)S(1)}, u32[]{:S(2)}, u32[]{:S(2)}) %collective-permute-start.8) | collective-permute-done | bytes 131104 | tf_op jit(solution)/shard_map/ppermute | solution.py:24
  31.7 0.6 %collective-permute-start.9 = (bf16[256,128]{1,0:T(8,128)(2,1)S(1)}, bf16[256,128]{1,0:T(8,128)(2,1)S(1)}, u32[]{:S(2)}, u32[]{:S(2)}) collective-permute-start(bf16[256,128]{1,0:T(8,128)(2,1)S(1)} %add_convert_fusion), channel_id=1, source_target_pairs={{0,4},{4,0},{8,12},{12,8},{1,5},{5,1},{9,13},{13,9},{2,6},{6,2},{1... | collective-permute-start | bytes 196616 | tf_op jit(solution)/shard_map/ppermute | solution.py:24
  32.2 0.0 collective-permute-done.13
  32.3 2.9 %collective-permute-start.14 = (bf16[128,256]{1,0:T(8,128)(2,1)S(1)}, bf16[128,256]{1,0:T(8,128)(2,1)S(1)}, u32[]{:S(2)}, u32[]{:S(2)}) collective-permute-start(bf16[128,256]{1,0:T(8,128)(2,1)S(1)} %pad_maximum_fusion.1), channel_id=1, source_target_pairs={{0,8},{4,12},{8,0},{12,4},{1,9},{5,13},{9,1},{13,5},{2,10},{6,14},... | collective-permute-start | bytes 196616 | tf_op jit(solution)/shard_map/ppermute | solution.py:24
  35.2 1.1 %collective-permute-start.15 = (bf16[128,256]{1,0:T(8,128)(2,1)S(1)}, bf16[128,256]{1,0:T(8,128)(2,1)S(1)}, u32[]{:S(2)}, u32[]{:S(2)}) collective-permute-start(bf16[128,256]{1,0:T(8,128)(2,1)S(1)} %pad_maximum_fusion.2), channel_id=1, source_target_pairs={{0,12},{4,8},{8,4},{12,0},{1,13},{5,9},{9,5},{13,1},{2,14},{6,10},... | collective-permute-start | bytes 196616 | tf_op jit(solution)/shard_map/ppermute | solution.py:24
  36.3 0.1 collective-permute-start.16
  36.4 0.3 collective-permute-done.9
  36.7 0.0 copy-start
  36.8 0.1 collective-permute-start.10
  36.8 2.1 %collective-permute-done.14.refs_0_ = bf16[128,256]{1,0:T(8,128)(2,1)S(1)} collective-permute-done((bf16[128,256]{1,0:T(8,128)(2,1)S(1)}, bf16[128,256]{1,0:T(8,128)(2,1)S(1)}, u32[]{:S(2)}, u32[]{:S(2)}) %collective-permute-start.14) | collective-permute-done | bytes 65568 | tf_op jit(solution)/shard_map/ppermute | solution.py:24
  39.0 2.5 %collective-permute-done.15.refs_1_ = bf16[128,256]{1,0:T(8,128)(2,1)S(1)} collective-permute-done((bf16[128,256]{1,0:T(8,128)(2,1)S(1)}, bf16[128,256]{1,0:T(8,128)(2,1)S(1)}, u32[]{:S(2)}, u32[]{:S(2)}) %collective-permute-start.15) | collective-permute-done | bytes 65568 | tf_op jit(solution)/shard_map/ppermute | solution.py:24
  41.5 0.0 collective-permute-done.16.refs_2_
  41.5 0.0 collective-permute-done.10.first_theirs
  41.5 0.0 copy-done
  41.5 0.8 %shard_map.61 = bf16[128,512]{1,0:T(8,128)(2,1)} custom-call(bf16[128,512]{1,0:T(8,128)(2,1)S(1)} %bitcast.3, f32[128,128]{1,0:T(8,128)S(1)} %get-tuple-element.42.first_mine, f32[128,128]{1,0:T(8,128)S(1)} %collective-permute-done.10.first_theirs, f32[128,128]{1,0:T(8,128)S(1)} %get-tuple-element.34.own, bf16[128,128]{1,0:T(8,128)(2,1)S(1)} %get-tuple-element.40.other, ...), custom_call_target="tpu_custom_call" | custom-call | flops 1 | bytes 1 | tf_op jit(solution)/shard_map/pallas_call | solution.py:166
  (9 shorter events, 0.1 us)
Async XLA Ops:
  1.4 3.7 %collective-permute-start.1 = (bf16[1024,128]{1,0:T(8,128)(2,1)S(1)}, bf16[1024,128]{1,0:T(8,128)(2,1)S(1)}, u32[]{:S(2)}, u32[]{:S(2)}) collective-permute-start(bf16[1024,128]{1,0:T(8,128)(2,1)S(1)} %get-tuple-element.23), channel_id=1, source_target_pairs={{0,1},{1,0},{2,3},{3,2},{4,5},{5,4},{6,7},{7,6},{8,9},{9,8},{10,11... | collective-permute-start | bytes 786440 | tf_op jit(solution)/shard_map/ppermute | solution.py:24
  2.0 3.2 %collective-permute-start.2 = (bf16[1024,128]{1,0:T(8,128)(2,1)S(1)}, bf16[1024,128]{1,0:T(8,128)(2,1)S(1)}, u32[]{:S(2)}, u32[]{:S(2)}) collective-permute-start(bf16[1024,128]{1,0:T(8,128)(2,1)S(1)} %get-tuple-element.24), channel_id=1, source_target_pairs={{0,1},{1,0},{2,3},{3,2},{4,5},{5,4},{6,7},{7,6},{8,9},{9,8},{10,11... | collective-permute-start | bytes 786440 | tf_op jit(solution)/shard_map/ppermute | solution.py:24
  2.0 3.1 %collective-permute-start = (bf16[128,256]{1,0:T(8,128)(2,1)S(1)}, bf16[128,256]{1,0:T(8,128)(2,1)S(1)}, u32[]{:S(2)}, u32[]{:S(2)}) collective-permute-start(bf16[128,256]{1,0:T(8,128)(2,1)S(1)} %get-tuple-element.22), channel_id=1, source_target_pairs={{0,1},{1,0},{2,3},{3,2},{4,5},{5,4},{6,7},{7,6},{8,9},{9,8},{10,11... | collective-permute-start | bytes 196616 | tf_op jit(solution)/shard_map/ppermute | solution.py:24
  2.5 15.4 %collective-permute-start.6 = (bf16[1024,128]{1,0:T(8,128)(2,1)S(1)}, bf16[1024,128]{1,0:T(8,128)(2,1)S(1)}, u32[]{:S(2)}, u32[]{:S(2)}) collective-permute-start(bf16[1024,128]{1,0:T(8,128)(2,1)S(1)} %get-tuple-element.23), channel_id=1, source_target_pairs={{0,3},{1,2},{2,1},{3,0},{4,7},{5,6},{6,5},{7,4},{8,11},{9,10},{10,... | collective-permute-start | bytes 786440 | tf_op jit(solution)/shard_map/ppermute | solution.py:24
  5.1 12.8 %collective-permute-start.5 = (bf16[1024,128]{1,0:T(8,128)(2,1)S(1)}, bf16[1024,128]{1,0:T(8,128)(2,1)S(1)}, u32[]{:S(2)}, u32[]{:S(2)}) collective-permute-start(bf16[1024,128]{1,0:T(8,128)(2,1)S(1)} %get-tuple-element.26.refs_3_.kept), channel_id=1, source_target_pairs={{0,2},{1,3},{2,0},{3,1},{4,6},{5,7},{6,4},{7,5},{8,10},{9,11},{10,... | collective-permute-start | bytes 786440 | tf_op jit(solution)/shard_map/ppermute | solution.py:24
  5.1 11.0 %copy-start.1 = (s32[16,16]{1,0:T(8,128)S(1)}, s32[16,16]{1,0:T(8,128)}, u32[]{:S(2)}) copy-start(s32[16,16]{1,0:T(8,128)} %pattern.9) | copy-start | bytes 3076
  5.1 9.5 %collective-permute-start.4 = (bf16[256,256]{1,0:T(8,128)(2,1)S(1)}, bf16[256,256]{1,0:T(8,128)(2,1)S(1)}, u32[]{:S(2)}, u32[]{:S(2)}) collective-permute-start(bf16[256,256]{1,0:T(8,128)(2,1)S(1)} %pad_maximum_fusion.refs_0_.own), channel_id=1, source_target_pairs={{0,8},{4,12},{8,0},{12,4},{1,9},{5,13},{9,1},{13,5},{2,10},{6,14},... | collective-permute-start | bytes 393224 | tf_op jit(solution)/shard_map/ppermute | solution.py:24
  8.3 16.3 %collective-permute-start.11 = (bf16[1024,128]{1,0:T(8,128)(2,1)S(1)}, bf16[1024,128]{1,0:T(8,128)(2,1)S(1)}, u32[]{:S(2)}, u32[]{:S(2)}) collective-permute-start(bf16[1024,128]{1,0:T(8,128)(2,1)S(1)} %get-tuple-element.31.kept), channel_id=1, source_target_pairs={{0,2},{1,3},{2,0},{3,1},{4,6},{5,7},{6,4},{7,5},{8,10},{9,11},{10,... | collective-permute-start | bytes 786440 | tf_op jit(solution)/shard_map/ppermute | solution.py:24
  9.8 6.3 %collective-permute-start.3 = (bf16[256,256]{1,0:T(8,128)(2,1)S(1)}, bf16[256,256]{1,0:T(8,128)(2,1)S(1)}, u32[]{:S(2)}, u32[]{:S(2)}) collective-permute-start(bf16[256,256]{1,0:T(8,128)(2,1)S(1)} %pad_maximum_fusion.refs_0_.own), channel_id=1, source_target_pairs={{0,4},{4,0},{8,12},{12,8},{1,5},{5,1},{9,13},{13,9},{2,6},{6,2},{1... | collective-permute-start | bytes 393224 | tf_op jit(solution)/shard_map/ppermute | solution.py:24
  14.7 5.0 %collective-permute-start.7 = (bf16[256,256]{1,0:T(8,128)(2,1)S(1)}, bf16[256,256]{1,0:T(8,128)(2,1)S(1)}, u32[]{:S(2)}, u32[]{:S(2)}) collective-permute-start(bf16[256,256]{1,0:T(8,128)(2,1)S(1)} %collective-permute-done.4.refs_2_.far), channel_id=1, source_target_pairs={{0,4},{4,0},{8,12},{12,8},{1,5},{5,1},{9,13},{13,9},{2,6},{6,2},{1... | collective-permute-start | bytes 393224 | tf_op jit(solution)/shard_map/ppermute | solution.py:24
  16.1 12.4 %collective-permute-start.12 = (bf16[1024,128]{1,0:T(8,128)(2,1)S(1)}, bf16[1024,128]{1,0:T(8,128)(2,1)S(1)}, u32[]{:S(2)}, u32[]{:S(2)}) collective-permute-start(bf16[1024,128]{1,0:T(8,128)(2,1)S(1)} %get-tuple-element.24), channel_id=1, source_target_pairs={{0,3},{1,2},{2,1},{3,0},{4,7},{5,6},{6,5},{7,4},{8,11},{9,10},{10,... | collective-permute-start | bytes 786440 | tf_op jit(solution)/shard_map/ppermute | solution.py:24
  21.1 10.5 %collective-permute-start.8 = (bf16[512,128]{1,0:T(8,128)(2,1)S(1)}, bf16[512,128]{1,0:T(8,128)(2,1)S(1)}, u32[]{:S(2)}, u32[]{:S(2)}) collective-permute-start(bf16[512,128]{1,0:T(8,128)(2,1)S(1)} %shard_map.58), channel_id=1, source_target_pairs={{0,8},{4,12},{8,0},{12,4},{1,9},{5,13},{9,1},{13,5},{2,10},{6,14},... | collective-permute-start | bytes 393224 | tf_op jit(solution)/shard_map/ppermute | solution.py:24
  30.2 2.0 %collective-permute-start.13 = (bf16[512,128]{1,0:T(8,128)(2,1)S(1)}, bf16[512,128]{1,0:T(8,128)(2,1)S(1)}, u32[]{:S(2)}, u32[]{:S(2)}) collective-permute-start(bf16[512,128]{1,0:T(8,128)(2,1)S(1)} %get-tuple-element.35), channel_id=1, source_target_pairs={{0,1},{1,0},{2,3},{3,2},{4,5},{5,4},{6,7},{7,6},{8,9},{9,8},{10,11... | collective-permute-start | bytes 393224 | tf_op jit(solution)/shard_map/ppermute | solution.py:24
  31.7 5.0 %collective-permute-start.9 = (bf16[256,128]{1,0:T(8,128)(2,1)S(1)}, bf16[256,128]{1,0:T(8,128)(2,1)S(1)}, u32[]{:S(2)}, u32[]{:S(2)}) collective-permute-start(bf16[256,128]{1,0:T(8,128)(2,1)S(1)} %add_convert_fusion), channel_id=1, source_target_pairs={{0,4},{4,0},{8,12},{12,8},{1,5},{5,1},{9,13},{13,9},{2,6},{6,2},{1... | collective-permute-start | bytes 196616 | tf_op jit(solution)/shard_map/ppermute | solution.py:24
  32.3 6.7 %collective-permute-start.14 = (bf16[128,256]{1,0:T(8,128)(2,1)S(1)}, bf16[128,256]{1,0:T(8,128)(2,1)S(1)}, u32[]{:S(2)}, u32[]{:S(2)}) collective-permute-start(bf16[128,256]{1,0:T(8,128)(2,1)S(1)} %pad_maximum_fusion.1), channel_id=1, source_target_pairs={{0,8},{4,12},{8,0},{12,4},{1,9},{5,13},{9,1},{13,5},{2,10},{6,14},... | collective-permute-start | bytes 196616 | tf_op jit(solution)/shard_map/ppermute | solution.py:24
  35.2 6.2 %collective-permute-start.15 = (bf16[128,256]{1,0:T(8,128)(2,1)S(1)}, bf16[128,256]{1,0:T(8,128)(2,1)S(1)}, u32[]{:S(2)}, u32[]{:S(2)}) collective-permute-start(bf16[128,256]{1,0:T(8,128)(2,1)S(1)} %pad_maximum_fusion.2), channel_id=1, source_target_pairs={{0,12},{4,8},{8,4},{12,0},{1,13},{5,9},{9,5},{13,1},{2,14},{6,10},... | collective-permute-start | bytes 196616 | tf_op jit(solution)/shard_map/ppermute | solution.py:24
  36.3 5.2 %collective-permute-start.16 = (bf16[128,256]{1,0:T(8,128)(2,1)S(1)}, bf16[128,256]{1,0:T(8,128)(2,1)S(1)}, u32[]{:S(2)}, u32[]{:S(2)}) collective-permute-start(bf16[128,256]{1,0:T(8,128)(2,1)S(1)} %pad_maximum_fusion.3), channel_id=1, source_target_pairs={{0,4},{4,0},{8,12},{12,8},{1,5},{5,1},{9,13},{13,9},{2,6},{6,2},{1... | collective-permute-start | bytes 196616 | tf_op jit(solution)/shard_map/ppermute | solution.py:24
  36.7 4.7 %copy-start = (bf16[1,128,512]{2,1,0:T(8,128)(2,1)S(1)}, bf16[1,128,512]{2,1,0:T(8,128)(2,1)}, u32[]{:S(2)}) copy-start(bf16[1,128,512]{2,1,0:T(8,128)(2,1)} %param.6) | copy-start | bytes 393220
  36.8 4.7 %collective-permute-start.10 = (f32[128,128]{1,0:T(8,128)S(1)}, f32[128,128]{1,0:T(8,128)S(1)}, u32[]{:S(2)}, u32[]{:S(2)}) collective-permute-start(f32[128,128]{1,0:T(8,128)S(1)} %get-tuple-element.41), channel_id=1, source_target_pairs={{0,1},{1,0},{2,3},{3,2},{4,5},{5,4},{6,7},{7,6},{8,9},{9,8},{10,11... | collective-permute-start | bytes 196616 | tf_op jit(solution)/shard_map/ppermute | solution.py:24

commit v4 on v3

--- a/solution.py
+++ b/solution.py
@@ -13,6 +13,11 @@
 HALF_SCALE = 0.5 * HEAD_DIM ** (-0.5)
 LONG = 10**10
 PAIR = 2 * HEAD_DIM
+ALONG = ((0, 0), (1, 0), (2, 0), (3, 0))
+SQUARE = ((0, 0), (0, 2), (2, 0), (2, 2))
+PAIRED = ((0, 0), (0, 1))
+ACROSS = ((0, 2), (0, 3))
+BESIDE = ((1, 0), (1, 1))
 VMEM_LIMIT = 48 * 1024 * 1024
 PARAMS = pltpu.CompilerParams(vmem_limit_bytes=VMEM_LIMIT)
 COST = pl.CostEstimate(flops=1, transcendentals=0, bytes_accessed=1)
@@ -92,74 +97,63 @@
 
 def head_rows(refs, head):
     wide = slice(head * HEAD_DIM, (head + 1) * HEAD_DIM)
-    return jnp.concatenate([ref[:, wide] for ref in refs], axis=0)
-
-
-def row_places(masks):
+    return jnp.concatenate(
+        [ref[...] if ref.shape[1] == HEAD_DIM else ref[:, wide] for ref in refs], axis=0
+    )
+
+
+def row_places(places, sides=(0, 1)):
     seq, blk = lax.axis_index("seq"), lax.axis_index("blk")
-    return [
-        (blk ^ side) * lax.axis_size("seq") + (seq ^ mask) for mask in masks for side in (0, 1)
-    ]
-
-
-def hist_places(masks):
+    size = lax.axis_size("seq")
+    return [(blk ^ across ^ side) * size + (seq ^ near) for near, across in places for side in sides]
+
+
+def hist_places(places):
     seq, blk = lax.axis_index("seq"), lax.axis_index("blk")
-    return [seq * lax.axis_size("blk") + (blk ^ mask) for mask in masks]
-
-
-def joined(hists):
-    events = hists[0].shape[0] // 2
-    keys = jnp.concatenate([hist[:events] for hist in hists], axis=0)
-    return keys, jnp.concatenate([hist[events:] for hist in hists], axis=0)
-
-
-def sums_kernel(head, row_masks, hist_masks, pattern, *refs):
-    rows, refs = refs[: len(row_masks)], refs[len(row_masks) :]
-    hists, refs = refs[: len(hist_masks)], refs[len(hist_masks) :]
-    keys, values = joined(hists)
-    weights = weigh(
-        pattern, head_rows(rows, head), keys, row_places(row_masks), hist_places(hist_masks)
-    )
-    total = mix(weights, values)
-    if refs[0].shape == total.shape and len(refs) > 1:
-        total, refs = total + refs[0][...], refs[1:]
-    done = 0
-    for out in refs:
-        out[...] = total[done : done + out.shape[0]].astype(out.dtype)
-        done += out.shape[0]
-
-
-def both_kernel(pattern, both, kept, beside, straight, diagonal, far_sums, out):
-    half = far_sums.shape[0]
-    keys, values = joined((kept, beside, straight, diagonal))
-    weights = weigh(pattern, head_rows((both,), 0), keys, row_places((3,)), hist_places(range(4)))
-    out[:half] = far_sums[...]
-    out[half:] = mix(weights, values).astype(out.dtype)
-
-
-def weights_kernel(pattern, own, near, far, both, kept, beside, straight, start, out):
-    rows = head_rows((own, near, far, both), 1)
-    keys, values = joined((kept, beside))
-    weights = weigh(pattern, rows, keys, row_places(range(4)), hist_places((0, 1)))
-    start[...] = mix(weights, values)
-    events = straight.shape[0] // 2
-    out[...] = weigh(pattern, rows, straight[:events], row_places(range(4)), hist_places((2,)))
-
-
-def second_kernel(pattern, own, near, far, both, straight, diagonal, weights, start, *outs):
-    rows = head_rows((own, near, far, both), 1)
-    events = straight.shape[0] // 2
-    late = weigh(pattern, rows, diagonal[:events], row_places(range(4)), hist_places((3,)))
-    values = jnp.concatenate([straight[events:], diagonal[events:]], axis=0)
-    total = mix(jnp.concatenate([weights[...], late], axis=1), values) + start[...]
-    own, others, theirs = outs
-    count = own.shape[0]
-    own[...] = total[:count]
-    for i in range(4):
-        at = 2 * i * count
-        if i:
-            others[(i - 1) * count : i * count] = total[at : at + count].astype(others.dtype)
-        theirs[i * count : (i + 1) * count] = total[at + count : at + 2 * count].astype(theirs.dtype)
+    return [(seq ^ near) * lax.axis_size("blk") + (blk ^ across) for near, across in places]
+
+
+def early_kernel(pattern, own, far, keys, values, out):
+    rows = head_rows((own, far), 0)
+    weights = weigh(pattern, rows, keys[...], row_places(ALONG[::2]), hist_places(PAIRED))
+    out[...] = mix(weights, values[...])
+
+
+def first_kernel(pattern, own, far, far_hist, start, own_out, far_out):
+    half = own.shape[0]
+    events = far_hist.shape[0] // 2
+    rows = head_rows((own, far), 0)
+    weights = weigh(pattern, rows, far_hist[:events], row_places(ALONG[::2]), hist_places(ACROSS))
+    total = mix(weights, far_hist[events:]) + start[...]
+    own_out[...] = total[:half]
+    far_out[...] = total[half:]
+
+
+def rest_kernel(pattern, near_pack, both, keys, values, far_hist, out):
+    half = both.shape[0]
+    events = keys.shape[0]
+    rows = head_rows((near_pack.at[:half], both), 0)
+    weights = weigh(pattern, rows, keys[...], row_places(ALONG[1::2]), hist_places(PAIRED))
+    total = mix(weights, values[...])
+    weights = weigh(pattern, rows, far_hist[:events], row_places(ALONG[1::2]), hist_places(ACROSS))
+    out[...] = (total + mix(weights, far_hist[events:])).astype(out.dtype)
+
+
+def weights_kernel(pattern, own, crosses, far, keys, values, near_pack, start, out):
+    half = own.shape[0]
+    rows = head_rows((own, crosses.at[:half], far, crosses.at[half:]), 1)
+    weights = weigh(pattern, rows, keys[...], row_places(SQUARE), hist_places(PAIRED))
+    start[...] = mix(weights, values[...])
+    out[...] = weigh(pattern, rows, near_pack[half:], row_places(SQUARE), hist_places(BESIDE))
+
+
+def second_kernel(weights, near_values, start, own, far, others):
+    total = mix(weights[...], near_values[...]) + start[...]
+    half = own.shape[0]
+    own[...] = total[:half]
+    far[...] = total[2 * half : 3 * half]
+    others[:half] = total[half : 2 * half].astype(others.dtype)
+    others[half:] = total[3 * half :].astype(others.dtype)
 
 
 def call(kernel, outs, *inputs, flops=1):
@@ -175,15 +169,10 @@
     )(*inputs)
 
 
-def finish_kernel(gate_ref, first_mine, first_theirs, own, other, *refs):
-    passed, out_ref = refs[:-1], refs[-1]
+def finish_kernel(gate_ref, first_mine, first_theirs, second_mine, second_theirs, out_ref):
     core = lax.rem(lax.axis_index("blk"), 2)
-    mine, theirs = own[...], other[...].astype(jnp.float32)
-    for piece in passed:
-        mine = mine + piece[:, :HEAD_DIM].astype(jnp.float32)
-        theirs = theirs + piece[:, HEAD_DIM:].astype(jnp.float32)
-    mine = jnp.concatenate([first_mine[...], mine], axis=1)
-    theirs = jnp.concatenate([first_theirs[...], theirs], axis=1)
+    mine = jnp.concatenate([first_mine[...], second_mine[...]], axis=1)
+    theirs = jnp.concatenate([first_theirs[...], second_theirs[...]], axis=1)
     squares = jnp.sum(mine * mine, axis=1, keepdims=True)
     squares = squares + jnp.sum(theirs * theirs, axis=1, keepdims=True)
     factor = lax.rsqrt(squares / (HEADS * HEAD_DIM) + 1e-05)
@@ -194,63 +183,57 @@
     out_ref[:, PAIR:] = (second * gate[:, PAIR:]).astype(out_ref.dtype)
 
 
+def reduced(own, far, others, axis, mask):
+    half = own.shape[0]
+    passed = swapped(others, axis, mask).astype(jnp.float32)
+    last = swapped((far + passed[half:]).astype(others.dtype), "seq", 2)
+    return own + passed[:half] + last.astype(jnp.float32)
+
+
 def paired(candidates, gate_values, hist_keys, hist_values, pattern):
     count = CAND_BLOCK
     half = 2 * count
     events = hist_keys.shape[0]
     own, queries, *hists = pack(candidates[0], hist_keys, hist_values)
     kept, sent = hists[:2], hists[2:]
-    straight = [swapped(x, "blk", 2) for x in kept]
-    diagonal = [swapped(x, "blk", 3) for x in sent]
     own = jnp.concatenate([own, swapped(queries, "blk", 1)], axis=0)
     beside = [swapped(x, "blk", 1) for x in sent]
-    own = after(own, *beside)
+    keys = [jnp.concatenate([x[:events], y[:events]], axis=0) for x, y in zip(kept, beside)]
+    values = [jnp.concatenate([x[events:], y[events:]], axis=0) for x, y in zip(kept, beside)]
+    hist = jnp.concatenate([keys[0], values[0]], axis=0)
+    own = after(own, hist)
     far = swapped(own, "seq", 2)
-    near = swapped(own, "seq", 1)
-    both = swapped(far, "seq", 1)
+    far_hist = swapped(hist, "blk", 2)
+    near_pack = swapped(jnp.concatenate([own[:, :HEAD_DIM], keys[1]], axis=0), "seq", 1)
+    both = swapped(far[:, :HEAD_DIM], "seq", 1)
+    near_values = swapped(after(values[1], far), "seq", 1)
+    crosses = swapped(jnp.concatenate([own[:, HEAD_DIM:], far[:, HEAD_DIM:]], axis=0), "blk", 2)
 
     f32, b16 = jnp.float32, jnp.bfloat16
-    rows, three = (own, near, far, both), (own, near, far)
     part = ((half, HEAD_DIM), f32)
-    early = call(
-        functools.partial(sums_kernel, 0, (0, 1, 2), (0, 1)),
-        [((3 * half, HEAD_DIM), f32)],
-        pattern, *three, kept[0], beside[0],
-    )
-    first, first_near, sums = call(
-        functools.partial(sums_kernel, 0, (0, 1, 2), (2, 3)),
-        [part, part, ((half, HEAD_DIM), b16)],
-        pattern, *three, straight[0], diagonal[0], *early,
-    )
-    (sums,) = call(
-        both_kernel,
-        [((2 * half, HEAD_DIM), b16)],
-        pattern, both, kept[0], beside[0], straight[0], diagonal[0], sums,
-    )
-    passed = swapped(sums, "seq", 2)
+    (early,) = call(early_kernel, [((2 * half, HEAD_DIM), f32)], pattern, own, far, keys[0], values[0])
+    first, first_far = call(first_kernel, [part, part], pattern, own, far, far_hist, early)
     start, weights = call(
         weights_kernel,
-        [((4 * half, HEAD_DIM), f32), ((4 * half, events), b16)],
-        pattern, *rows, after(kept[1], sums), beside[1], straight[1],
+        [((4 * half, HEAD_DIM), f32), ((4 * half, 2 * events), b16)],
+        pattern, own, crosses, far, after(keys[1], first), values[1], near_pack,
         flops=LONG,
     )
-    folded = first_near + passed[half:].astype(f32)
-    last = swapped(folded.astype(b16), "seq", 1)
-    first = first + passed[:half].astype(f32) + last.astype(f32)
-    first_theirs = swapped(first[count:], "blk", 1)
-
-    outs = [((count, HEAD_DIM), f32), ((3 * count, HEAD_DIM), b16), ((4 * count, HEAD_DIM), b16)]
-    own, others, theirs = call(
-        second_kernel, outs, pattern, *rows, straight[1], diagonal[1], weights, start, flops=LONG
-    )
-    came = swapped(theirs, "blk", 1)
+    (sums,) = call(
+        rest_kernel,
+        [((2 * half, HEAD_DIM), b16)],
+        pattern, near_pack, both, after(keys[0], start), values[0], far_hist,
+    )
+    outs = [part, part, ((2 * half, HEAD_DIM), b16)]
+    second, second_far, others = call(second_kernel, outs, weights, near_values, start)
+    first, second = (
+        reduced(*x) for x in ((first, first_far, sums, "seq", 1), (second, second_far, others, "blk", 2))
+    )
     pieces = []
-    for mask in (2, 3, 1):
-        mine = others[(mask - 1) * count : mask * count]
-        piece = jnp.concatenate([mine, came[mask * count : (mask + 1) * count]], axis=1)
-        pieces.append(swapped(piece, "seq", mask))
+    for x in (first, second):
+        pieces += [x[:count], swapped(x[count:], "blk", 1)]
     gate = gate_values[0]
-    inputs = [gate, first[:count], first_theirs, own, came[:count], *pieces]
+    inputs = [gate, *pieces]
     return call(finish_kernel, [(gate.shape, gate.dtype)], *inputs)[0][None]
 
 
@@ -260,7 +243,7 @@
     total = None
     for at, hist in enumerate(hists):
         weights = weigh(
-            pattern, rows[...], hist[:, :HEAD_DIM], places(blk), hist_places((at,))
+            pattern, rows[...], hist[:, :HEAD_DIM], places(blk), hist_places(((0, at),))
         )
         mixed = mix(weights, hist[:, HEAD_DIM:])
         total = mixed if total is None else total + mixed

time: 42.4 us -> 42.2 us (level)
  waiting for transfers between devices: 11.7 us -> 11.1 us
    ppermute x17 -> x15, waiting for transfers between devices: 11.7 us -> 11.1 us  [swapped(): return lax.ppermute(block, axis, [(i, i ^ mask) for i in range(size)])]
    ppermute x17 -> x15, starting transfers between devices: 19.2 us -> 19.3 us  [swapped(): return lax.ppermute(block, axis, [(i, i ^ mask) for i in range(size)])]
  transfers between devices with their start and end apart: 17 -> 15, of which waited for: 7 -> 9; matrix products, arithmetic and copies ran while one was open for 0% -> 1% of each run, Pallas kernels for 21% -> 21%
where the time goes in v4:
time: 42.2 us; the launch traced here: 42.1 us
  starting transfers between devices  19.3 us (46%)
  waiting for transfers between devices  11.1 us (26%)
  Pallas kernels  11 us (26%)
    ppermute x15, starting transfers between devices, swapped(): return lax.ppermute(block, axis, [(i, i ^ mask) for i in range(size)])  19.3 us
    ppermute x15, waiting for transfers between devices, swapped(): return lax.ppermute(block, axis, [(i, i ^ mask) for i in range(size)])  11.1 us
    pallas_call x6, Pallas kernels, call(): pl.pallas_call(kernel, out_shape=[jax.ShapeDtypeStruct(shape, kind) for s...  9.56 us
    pallas_call x1, Pallas kernels, pack(): pl.pallas_call(pack_kernel, out_shape=[row_shape] * 2 + [both_shape] * 4,...  1.44 us
  transfers between devices with their start and end apart: 15, of which 9 were waited for; matrix products, arithmetic and copies ran while one was open for 1% of the time, Pallas kernels for 21%

profile of v4, /device:TPU:0, one launch (start us, length us, event | category | flops | bytes accessed | tf_op | source)
XLA Modules:
  0.0 42.1 jit_solution(15683351085025664788)
XLA Ops:
  0.0 1.4 %shard_map.55 = (bf16[128,256]{1,0:T(8,128)(2,1)S(1)}, bf16[128,256]{1,0:T(8,128)(2,1)S(1)}, bf16[1024,128]{1,0:T(8,128)(2,1)S(1)}, bf16[1024,128]{1,0:T(8,128)(...) custom-call(bf16[128,512]{1,0:T(8,128)(2,1)} %bitcast.4, bf16[512,512]{1,0:T(8,128)(2,1)} %keys.1, ...), custom_call_target="tpu_custom_call" | custom-call | flops 1 | bytes 1 | tf_op jit(solution)/shard_map/pallas_call | solution.py:65
  1.4 0.5 %collective-permute-start = (bf16[128,256]{1,0:T(8,128)(2,1)S(1)}, bf16[128,256]{1,0:T(8,128)(2,1)S(1)}, u32[]{:S(2)}, u32[]{:S(2)}) collective-permute-start(bf16[128,256]{1,0:T(8,128)(2,1)S(1)} %get-tuple-element.23), channel_id=1, source_target_pairs={{0,1},{1,0},{2,3},{3,2},{4,5},{5,4},{6,7},{7,6},{8,9},{9,8},{10,11... | collective-permute-start | bytes 196616 | tf_op jit(solution)/shard_map/ppermute | solution.py:29
  2.0 0.1 collective-permute-start.1
  2.0 0.4 %collective-permute-start.4 = (bf16[1024,128]{1,0:T(8,128)(2,1)S(1)}, bf16[1024,128]{1,0:T(8,128)(2,1)S(1)}, u32[]{:S(2)}, u32[]{:S(2)}) collective-permute-start(bf16[1024,128]{1,0:T(8,128)(2,1)S(1)} %get-tuple-element.29), channel_id=1, source_target_pairs={{0,1},{1,0},{2,3},{3,2},{4,5},{5,4},{6,7},{7,6},{8,9},{9,8},{10,11... | collective-permute-start | bytes 786440 | tf_op jit(solution)/shard_map/ppermute | solution.py:29
  2.5 0.4 collective-permute-done
  2.9 0.6 %collective-permute-done.1 = bf16[1024,128]{1,0:T(8,128)(2,1)S(1)} collective-permute-done((bf16[1024,128]{1,0:T(8,128)(2,1)S(1)}, bf16[1024,128]{1,0:T(8,128)(2,1)S(1)}, u32[]{:S(2)}, u32[]{:S(2)}) %collective-permute-start.1) | collective-permute-done | bytes 262176 | tf_op jit(solution)/shard_map/ppermute | solution.py:29
  3.6 0.0 copy-start.1
  3.6 2.7 %collective-permute-start.3 = (bf16[2048,128]{1,0:T(8,128)(2,1)S(1)}, bf16[2048,128]{1,0:T(8,128)(2,1)S(1)}, u32[]{:S(2)}, u32[]{:S(2)}) collective-permute-start(bf16[2048,128]{1,0:T(8,128)(2,1)S(1)} %pad_maximum_fusion), channel_id=1, source_target_pairs={{0,2},{1,3},{2,0},{3,1},{4,6},{5,7},{6,4},{7,5},{8,10},{9,11},{10,... | collective-permute-start | bytes 1572872 | tf_op jit(solution)/shard_map/ppermute | solution.py:29
  6.3 2.6 %collective-permute-start.2 = (bf16[256,256]{1,0:T(8,128)(2,1)S(1)}, bf16[256,256]{1,0:T(8,128)(2,1)S(1)}, u32[]{:S(2)}, u32[]{:S(2)}) collective-permute-start(bf16[256,256]{1,0:T(8,128)(2,1)S(1)} %pad_maximum_fusion.6.own), channel_id=1, source_target_pairs={{0,8},{4,12},{8,0},{12,4},{1,9},{5,13},{9,1},{13,5},{2,10},{6,14},... | collective-permute-start | bytes 393224 | tf_op jit(solution)/shard_map/ppermute | solution.py:29
  8.9 0.0 collective-permute-done.4
  9.0 1.6 %collective-permute-start.5 = (bf16[1280,128]{1,0:T(8,128)(2,1)S(1)}, bf16[1280,128]{1,0:T(8,128)(2,1)S(1)}, u32[]{:S(2)}, u32[]{:S(2)}) collective-permute-start(bf16[1280,128]{1,0:T(8,128)(2,1)S(1)} %pad_maximum_fusion.1), channel_id=1, source_target_pairs={{0,4},{4,0},{8,12},{12,8},{1,5},{5,1},{9,13},{13,9},{2,6},{6,2},{1... | collective-permute-start | bytes 983048 | tf_op jit(solution)/shard_map/ppermute | solution.py:29
  10.6 4.9 %collective-permute-done.2.far = bf16[256,256]{1,0:T(8,128)(2,1)S(1)} collective-permute-done((bf16[256,256]{1,0:T(8,128)(2,1)S(1)}, bf16[256,256]{1,0:T(8,128)(2,1)S(1)}, u32[]{:S(2)}, u32[]{:S(2)}) %collective-permute-start.2) | collective-permute-done | bytes 131104 | tf_op jit(solution)/shard_map/ppermute | solution.py:29
  15.6 0.6 %collective-permute-start.7 = (bf16[512,128]{1,0:T(8,128)(2,1)S(1)}, bf16[512,128]{1,0:T(8,128)(2,1)S(1)}, u32[]{:S(2)}, u32[]{:S(2)}) collective-permute-start(bf16[512,128]{1,0:T(8,128)(2,1)S(1)} %pad_maximum_fusion.7), channel_id=1, source_target_pairs={{0,2},{1,3},{2,0},{3,1},{4,6},{5,7},{6,4},{7,5},{8,10},{9,11},{10,... | collective-permute-start | bytes 393224 | tf_op jit(solution)/shard_map/ppermute | solution.py:29
  16.2 0.7 %collective-permute-start.6 = (bf16[256,128]{1,0:T(8,128)(2,1)S(1)}, bf16[256,128]{1,0:T(8,128)(2,1)S(1)}, u32[]{:S(2)}, u32[]{:S(2)}) collective-permute-start(bf16[256,128]{1,0:T(8,128)(2,1)S(1)} %get-tuple-element.54), channel_id=1, source_target_pairs={{0,4},{4,0},{8,12},{12,8},{1,5},{5,1},{9,13},{13,9},{2,6},{6,2},{1... | collective-permute-start | bytes 196616 | tf_op jit(solution)/shard_map/ppermute | solution.py:29
  16.9 1.4 %collective-permute-start.11 = (bf16[1024,128]{1,0:T(8,128)(2,1)S(1)}, bf16[1024,128]{1,0:T(8,128)(2,1)S(1)}, u32[]{:S(2)}, u32[]{:S(2)}) collective-permute-start(bf16[1024,128]{1,0:T(8,128)(2,1)S(1)} %pad_maximum_fusion.5.values), channel_id=1, source_target_pairs={{0,4},{4,0},{8,12},{12,8},{1,5},{5,1},{9,13},{13,9},{2,6},{6,2},{1... | collective-permute-start | bytes 786440 | tf_op jit(solution)/shard_map/ppermute | solution.py:29
  18.3 0.0 copy-done.1
  18.3 1.5 %shard_map.56.start = f32[512,128]{1,0:T(8,128)S(1)} custom-call(s32[16,16]{1,0:T(8,128)S(1)} %copy-done.1, bf16[256,256]{1,0:T(8,128)(2,1)S(1)} %pad_maximum_fusion.6.own, bf16[256,256]{1,0:T(8,128)(2,1)S(1)} %collective-permute-done.2.far, bf16[1024,128]{1,0:T(8,128)(2,1)S(1)} %pad_maximum_fusion.2.keys, bf16[1024,128]{1,0:T(8,128)(2,1)S(1)} %pad_maximum_fusion.3.values), custom_call_target="tpu_custom_call" | custom-call | flops 1 | bytes 1 | tf_op jit(solution)/shard_map/pallas_call | solution.py:160
  19.8 0.0 collective-permute-done.3.far_hist
  19.8 1.5 %shard_map.57 = (f32[256,128]{1,0:T(8,128)S(1)}, f32[256,128]{1,0:T(8,128)S(1)}) custom-call(s32[16,16]{1,0:T(8,128)S(1)} %copy-done.1, bf16[256,256]{1,0:T(8,128)(2,1)S(1)} %pad_maximum_fusion.6.own, bf16[256,256]{1,0:T(8,128)(2,1)S(1)} %collective-permute-done.2.far, bf16[2048,128]{1,0:T(8,128)(2,1)S(1)} %collective-permute-done.3.far_hist, ...), custom_call_target="tpu_custom_call" | custom-call | flops 1 | bytes 1 | tf_op jit(solution)/shard_map/pallas_call | solution.py:160
  21.3 0.3 collective-permute-done.7.crosses
  21.5 0.0 collective-permute-done.5.near_pack
  21.5 2.5 %shard_map.58 = (f32[1024,128]{1,0:T(8,128)S(1)}, bf16[1024,1024]{1,0:T(8,128)(2,1)S(1)}) custom-call(s32[16,16]{1,0:T(8,128)S(1)} %copy-done.1, bf16[256,256]{1,0:T(8,128)(2,1)S(1)} %pad_maximum_fusion.6.own, bf16[512,128]{1,0:T(8,128)(2,1)S(1)} %collective-permute-done.7.crosses, bf16[256,256]{1,0:T(8,128)(2,1)S(1)} %collective-permute-done.2.far, ...), custom_call_target="tpu_custom_call" | custom-call | flops 10000000000 | bytes 1 | tf_op jit(solution)/shard_map/pallas_call | solution.py:160
  24.1 0.0 collective-permute-done.6.both
  24.1 2.6 %shard_map.59 = bf16[512,128]{1,0:T(8,128)(2,1)S(1)} custom-call(s32[16,16]{1,0:T(8,128)S(1)} %copy-done.1, bf16[1280,128]{1,0:T(8,128)(2,1)S(1)} %collective-permute-done.5.near_pack, bf16[256,128]{1,0:T(8,128)(2,1)S(1)} %collective-permute-done.6.both, bf16[1024,128]{1,0:T(8,128)(2,1)S(1)} %pad_maximum_fusion.2.keys, ...), custom_call_target="tpu_custom_call" | custom-call | flops 1 | bytes 1 | tf_op jit(solution)/shard_map/pallas_call | solution.py:160
  26.7 1.9 %collective-permute-start.8 = (bf16[512,128]{1,0:T(8,128)(2,1)S(1)}, bf16[512,128]{1,0:T(8,128)(2,1)S(1)}, u32[]{:S(2)}, u32[]{:S(2)}) collective-permute-start(bf16[512,128]{1,0:T(8,128)(2,1)S(1)} %shard_map.59), channel_id=1, source_target_pairs={{0,4},{4,0},{8,12},{12,8},{1,5},{5,1},{9,13},{13,9},{2,6},{6,2},{1... | collective-permute-start | bytes 393224 | tf_op jit(solution)/shard_map/ppermute | solution.py:29
  28.6 0.0 collective-permute-done.11.near_values
  28.6 0.7 %shard_map.60 = (f32[256,128]{1,0:T(8,128)S(1)}, f32[256,128]{1,0:T(8,128)S(1)}, bf16[512,128]{1,0:T(8,128)(2,1)S(1)}) custom-call(bf16[1024,1024]{1,0:T(8,128)(2,1)S(1)} %get-tuple-element.34.weights, bf16[1024,128]{1,0:T(8,128)(2,1)S(1)} %collective-permute-done.11.near_values, f32[1024,128]{1,0:T(8,128)S(1)} %get-tuple-element.31.start), custom_call_target="tpu_custom_call" | custom-call | flops 1 | bytes 1 | tf_op jit(solution)/shard_map/pallas_call | solution.py:160
  29.3 0.0 copy-start
  29.3 1.6 %collective-permute-start.12 = (bf16[512,128]{1,0:T(8,128)(2,1)S(1)}, bf16[512,128]{1,0:T(8,128)(2,1)S(1)}, u32[]{:S(2)}, u32[]{:S(2)}) collective-permute-start(bf16[512,128]{1,0:T(8,128)(2,1)S(1)} %get-tuple-element.37), channel_id=1, source_target_pairs={{0,2},{1,3},{2,0},{3,1},{4,6},{5,7},{6,4},{7,5},{8,10},{9,11},{10,... | collective-permute-start | bytes 393224 | tf_op jit(solution)/shard_map/ppermute | solution.py:29
  30.8 0.9 %collective-permute-done.8 = bf16[512,128]{1,0:T(8,128)(2,1)S(1)} collective-permute-done((bf16[512,128]{1,0:T(8,128)(2,1)S(1)}, bf16[512,128]{1,0:T(8,128)(2,1)S(1)}, u32[]{:S(2)}, u32[]{:S(2)}) %collective-permute-start.8) | collective-permute-done | bytes 131104 | tf_op jit(solution)/shard_map/ppermute | solution.py:29
  31.8 2.8 %collective-permute-start.9 = (bf16[256,128]{1,0:T(8,128)(2,1)S(1)}, bf16[256,128]{1,0:T(8,128)(2,1)S(1)}, u32[]{:S(2)}, u32[]{:S(2)}) collective-permute-start(bf16[256,128]{1,0:T(8,128)(2,1)S(1)} %fusion.2), channel_id=1, source_target_pairs={{0,8},{4,12},{8,0},{12,4},{1,9},{5,13},{9,1},{13,5},{2,10},{6,14},... | collective-permute-start | bytes 196616 | tf_op jit(solution)/shard_map/ppermute | solution.py:29
  34.7 0.0 collective-permute-done.12
  34.7 2.3 %collective-permute-start.13 = (bf16[256,128]{1,0:T(8,128)(2,1)S(1)}, bf16[256,128]{1,0:T(8,128)(2,1)S(1)}, u32[]{:S(2)}, u32[]{:S(2)}) collective-permute-start(bf16[256,128]{1,0:T(8,128)(2,1)S(1)} %fusion), channel_id=1, source_target_pairs={{0,8},{4,12},{8,0},{12,4},{1,9},{5,13},{9,1},{13,5},{2,10},{6,14},... | collective-permute-start | bytes 196616 | tf_op jit(solution)/shard_map/ppermute | solution.py:29
  37.0 2.1 %collective-permute-done.9 = bf16[256,128]{1,0:T(8,128)(2,1)S(1)} collective-permute-done((bf16[256,128]{1,0:T(8,128)(2,1)S(1)}, bf16[256,128]{1,0:T(8,128)(2,1)S(1)}, u32[]{:S(2)}, u32[]{:S(2)}) %collective-permute-start.9) | collective-permute-done | bytes 65568 | tf_op jit(solution)/shard_map/ppermute | solution.py:29
  39.2 0.1 collective-permute-start.10
  39.2 0.7 %collective-permute-done.13 = bf16[256,128]{1,0:T(8,128)(2,1)S(1)} collective-permute-done((bf16[256,128]{1,0:T(8,128)(2,1)S(1)}, bf16[256,128]{1,0:T(8,128)(2,1)S(1)}, u32[]{:S(2)}, u32[]{:S(2)}) %collective-permute-start.13) | collective-permute-done | bytes 65568 | tf_op jit(solution)/shard_map/ppermute | solution.py:29
  40.0 0.1 collective-permute-start.14
  40.1 0.4 %collective-permute-done.10.first_theirs = f32[128,128]{1,0:T(8,128)S(1)} collective-permute-done((f32[128,128]{1,0:T(8,128)S(1)}, f32[128,128]{1,0:T(8,128)S(1)}, u32[]{:S(2)}, u32[]{:S(2)}) %collective-permute-start.10) | collective-permute-done | bytes 65568 | tf_op jit(solution)/shard_map/ppermute | solution.py:29
  40.5 0.8 %collective-permute-done.14.second_theirs = f32[128,128]{1,0:T(8,128)S(1)} collective-permute-done((f32[128,128]{1,0:T(8,128)S(1)}, f32[128,128]{1,0:T(8,128)S(1)}, u32[]{:S(2)}, u32[]{:S(2)}) %collective-permute-start.14) | collective-permute-done | bytes 65568 | tf_op jit(solution)/shard_map/ppermute | solution.py:29
  41.3 0.0 copy-done
  41.3 0.8 %shard_map.61 = bf16[128,512]{1,0:T(8,128)(2,1)} custom-call(bf16[128,512]{1,0:T(8,128)(2,1)S(1)} %bitcast.3, f32[128,128]{1,0:T(8,128)S(1)} %get-tuple-element.50.first_mine, f32[128,128]{1,0:T(8,128)S(1)} %collective-permute-done.10.first_theirs, f32[128,128]{1,0:T(8,128)S(1)} %get-tuple-element.48.second_mine, ...), custom_call_target="tpu_custom_call" | custom-call | flops 1 | bytes 1 | tf_op jit(solution)/shard_map/pallas_call | solution.py:160
  (21 shorter events, 0.4 us)
Async XLA Ops:
  1.4 1.4 %collective-permute-start = (bf16[128,256]{1,0:T(8,128)(2,1)S(1)}, bf16[128,256]{1,0:T(8,128)(2,1)S(1)}, u32[]{:S(2)}, u32[]{:S(2)}) collective-permute-start(bf16[128,256]{1,0:T(8,128)(2,1)S(1)} %get-tuple-element.23), channel_id=1, source_target_pairs={{0,1},{1,0},{2,3},{3,2},{4,5},{5,4},{6,7},{7,6},{8,9},{9,8},{10,11... | collective-permute-start | bytes 196616 | tf_op jit(solution)/shard_map/ppermute | solution.py:29
  2.0 1.5 %collective-permute-start.1 = (bf16[1024,128]{1,0:T(8,128)(2,1)S(1)}, bf16[1024,128]{1,0:T(8,128)(2,1)S(1)}, u32[]{:S(2)}, u32[]{:S(2)}) collective-permute-start(bf16[1024,128]{1,0:T(8,128)(2,1)S(1)} %get-tuple-element.25), channel_id=1, source_target_pairs={{0,1},{1,0},{2,3},{3,2},{4,5},{5,4},{6,7},{7,6},{8,9},{9,8},{10,11... | collective-permute-start | bytes 786440 | tf_op jit(solution)/shard_map/ppermute | solution.py:29
  2.0 6.8 %collective-permute-start.4 = (bf16[1024,128]{1,0:T(8,128)(2,1)S(1)}, bf16[1024,128]{1,0:T(8,128)(2,1)S(1)}, u32[]{:S(2)}, u32[]{:S(2)}) collective-permute-start(bf16[1024,128]{1,0:T(8,128)(2,1)S(1)} %get-tuple-element.29), channel_id=1, source_target_pairs={{0,1},{1,0},{2,3},{3,2},{4,5},{5,4},{6,7},{7,6},{8,9},{9,8},{10,11... | collective-permute-start | bytes 786440 | tf_op jit(solution)/shard_map/ppermute | solution.py:29
  3.6 14.7 %copy-start.1 = (s32[16,16]{1,0:T(8,128)S(1)}, s32[16,16]{1,0:T(8,128)}, u32[]{:S(2)}) copy-start(s32[16,16]{1,0:T(8,128)} %pattern.7) | copy-start | bytes 3076
  3.6 16.2 %collective-permute-start.3 = (bf16[2048,128]{1,0:T(8,128)(2,1)S(1)}, bf16[2048,128]{1,0:T(8,128)(2,1)S(1)}, u32[]{:S(2)}, u32[]{:S(2)}) collective-permute-start(bf16[2048,128]{1,0:T(8,128)(2,1)S(1)} %pad_maximum_fusion), channel_id=1, source_target_pairs={{0,2},{1,3},{2,0},{3,1},{4,6},{5,7},{6,4},{7,5},{8,10},{9,11},{10,... | collective-permute-start | bytes 1572872 | tf_op jit(solution)/shard_map/ppermute | solution.py:29
  6.3 9.3 %collective-permute-start.2 = (bf16[256,256]{1,0:T(8,128)(2,1)S(1)}, bf16[256,256]{1,0:T(8,128)(2,1)S(1)}, u32[]{:S(2)}, u32[]{:S(2)}) collective-permute-start(bf16[256,256]{1,0:T(8,128)(2,1)S(1)} %pad_maximum_fusion.6.own), channel_id=1, source_target_pairs={{0,8},{4,12},{8,0},{12,4},{1,9},{5,13},{9,1},{13,5},{2,10},{6,14},... | collective-permute-start | bytes 393224 | tf_op jit(solution)/shard_map/ppermute | solution.py:29
  9.0 12.6 %collective-permute-start.5 = (bf16[1280,128]{1,0:T(8,128)(2,1)S(1)}, bf16[1280,128]{1,0:T(8,128)(2,1)S(1)}, u32[]{:S(2)}, u32[]{:S(2)}) collective-permute-start(bf16[1280,128]{1,0:T(8,128)(2,1)S(1)} %pad_maximum_fusion.1), channel_id=1, source_target_pairs={{0,4},{4,0},{8,12},{12,8},{1,5},{5,1},{9,13},{13,9},{2,6},{6,2},{1... | collective-permute-start | bytes 983048 | tf_op jit(solution)/shard_map/ppermute | solution.py:29
  15.6 5.9 %collective-permute-start.7 = (bf16[512,128]{1,0:T(8,128)(2,1)S(1)}, bf16[512,128]{1,0:T(8,128)(2,1)S(1)}, u32[]{:S(2)}, u32[]{:S(2)}) collective-permute-start(bf16[512,128]{1,0:T(8,128)(2,1)S(1)} %pad_maximum_fusion.7), channel_id=1, source_target_pairs={{0,2},{1,3},{2,0},{3,1},{4,6},{5,7},{6,4},{7,5},{8,10},{9,11},{10,... | collective-permute-start | bytes 393224 | tf_op jit(solution)/shard_map/ppermute | solution.py:29
  16.2 7.9 %collective-permute-start.6 = (bf16[256,128]{1,0:T(8,128)(2,1)S(1)}, bf16[256,128]{1,0:T(8,128)(2,1)S(1)}, u32[]{:S(2)}, u32[]{:S(2)}) collective-permute-start(bf16[256,128]{1,0:T(8,128)(2,1)S(1)} %get-tuple-element.54), channel_id=1, source_target_pairs={{0,4},{4,0},{8,12},{12,8},{1,5},{5,1},{9,13},{13,9},{2,6},{6,2},{1... | collective-permute-start | bytes 196616 | tf_op jit(solution)/shard_map/ppermute | solution.py:29
  16.9 11.6 %collective-permute-start.11 = (bf16[1024,128]{1,0:T(8,128)(2,1)S(1)}, bf16[1024,128]{1,0:T(8,128)(2,1)S(1)}, u32[]{:S(2)}, u32[]{:S(2)}) collective-permute-start(bf16[1024,128]{1,0:T(8,128)(2,1)S(1)} %pad_maximum_fusion.5.values), channel_id=1, source_target_pairs={{0,4},{4,0},{8,12},{12,8},{1,5},{5,1},{9,13},{13,9},{2,6},{6,2},{1... | collective-permute-start | bytes 786440 | tf_op jit(solution)/shard_map/ppermute | solution.py:29
  26.7 5.1 %collective-permute-start.8 = (bf16[512,128]{1,0:T(8,128)(2,1)S(1)}, bf16[512,128]{1,0:T(8,128)(2,1)S(1)}, u32[]{:S(2)}, u32[]{:S(2)}) collective-permute-start(bf16[512,128]{1,0:T(8,128)(2,1)S(1)} %shard_map.59), channel_id=1, source_target_pairs={{0,4},{4,0},{8,12},{12,8},{1,5},{5,1},{9,13},{13,9},{2,6},{6,2},{1... | collective-permute-start | bytes 393224 | tf_op jit(solution)/shard_map/ppermute | solution.py:29
  29.3 12.0 %copy-start = (bf16[1,128,512]{2,1,0:T(8,128)(2,1)S(1)}, bf16[1,128,512]{2,1,0:T(8,128)(2,1)}, u32[]{:S(2)}) copy-start(bf16[1,128,512]{2,1,0:T(8,128)(2,1)} %param.6) | copy-start | bytes 393220
  29.3 5.4 %collective-permute-start.12 = (bf16[512,128]{1,0:T(8,128)(2,1)S(1)}, bf16[512,128]{1,0:T(8,128)(2,1)S(1)}, u32[]{:S(2)}, u32[]{:S(2)}) collective-permute-start(bf16[512,128]{1,0:T(8,128)(2,1)S(1)} %get-tuple-element.37), channel_id=1, source_target_pairs={{0,2},{1,3},{2,0},{3,1},{4,6},{5,7},{6,4},{7,5},{8,10},{9,11},{10,... | collective-permute-start | bytes 393224 | tf_op jit(solution)/shard_map/ppermute | solution.py:29
  31.8 7.3 %collective-permute-start.9 = (bf16[256,128]{1,0:T(8,128)(2,1)S(1)}, bf16[256,128]{1,0:T(8,128)(2,1)S(1)}, u32[]{:S(2)}, u32[]{:S(2)}) collective-permute-start(bf16[256,128]{1,0:T(8,128)(2,1)S(1)} %fusion.2), channel_id=1, source_target_pairs={{0,8},{4,12},{8,0},{12,4},{1,9},{5,13},{9,1},{13,5},{2,10},{6,14},... | collective-permute-start | bytes 196616 | tf_op jit(solution)/shard_map/ppermute | solution.py:29
  34.7 5.2 %collective-permute-start.13 = (bf16[256,128]{1,0:T(8,128)(2,1)S(1)}, bf16[256,128]{1,0:T(8,128)(2,1)S(1)}, u32[]{:S(2)}, u32[]{:S(2)}) collective-permute-start(bf16[256,128]{1,0:T(8,128)(2,1)S(1)} %fusion), channel_id=1, source_target_pairs={{0,8},{4,12},{8,0},{12,4},{1,9},{5,13},{9,1},{13,5},{2,10},{6,14},... | collective-permute-start | bytes 196616 | tf_op jit(solution)/shard_map/ppermute | solution.py:29
  39.2 1.3 %collective-permute-start.10 = (f32[128,128]{1,0:T(8,128)S(1)}, f32[128,128]{1,0:T(8,128)S(1)}, u32[]{:S(2)}, u32[]{:S(2)}) collective-permute-start(f32[128,128]{1,0:T(8,128)S(1)} %get-tuple-element.49), channel_id=1, source_target_pairs={{0,1},{1,0},{2,3},{3,2},{4,5},{5,4},{6,7},{7,6},{8,9},{9,8},{10,11... | collective-permute-start | bytes 196616 | tf_op jit(solution)/shard_map/ppermute | solution.py:29
  40.0 1.3 %collective-permute-start.14 = (f32[128,128]{1,0:T(8,128)S(1)}, f32[128,128]{1,0:T(8,128)S(1)}, u32[]{:S(2)}, u32[]{:S(2)}) collective-permute-start(f32[128,128]{1,0:T(8,128)S(1)} %get-tuple-element.47), channel_id=1, source_target_pairs={{0,1},{1,0},{2,3},{3,2},{4,5},{5,4},{6,7},{7,6},{8,9},{9,8},{10,11... | collective-permute-start | bytes 196616 | tf_op jit(solution)/shard_map/ppermute | solution.py:29

commit v5 on v4

--- a/solution.py
+++ b/solution.py
@@ -145,6 +145,11 @@
     weights = weigh(pattern, rows, keys[...], row_places(SQUARE), hist_places(PAIRED))
     start[...] = mix(weights, values[...])
     out[...] = weigh(pattern, rows, near_pack[half:], row_places(SQUARE), hist_places(BESIDE))
+
+
+def work_kernel(pattern, own, crosses, far, keys, values, near_pack, both, first_keys, first_values, far_hist, start, weights, out):
+    weights_kernel(pattern, own, crosses, far, keys, values, near_pack, start, weights)
+    rest_kernel(pattern, near_pack, both, first_keys, first_values, far_hist, out)
 
 
 def second_kernel(weights, near_values, start, own, far, others):
@@ -213,19 +218,14 @@
     part = ((half, HEAD_DIM), f32)
     (early,) = call(early_kernel, [((2 * half, HEAD_DIM), f32)], pattern, own, far, keys[0], values[0])
     first, first_far = call(first_kernel, [part, part], pattern, own, far, far_hist, early)
-    start, weights = call(
-        weights_kernel,
-        [((4 * half, HEAD_DIM), f32), ((4 * half, 2 * events), b16)],
-        pattern, own, crosses, far, after(keys[1], first), values[1], near_pack,
+    start, weights, sums = call(
+        work_kernel,
+        [((4 * half, HEAD_DIM), f32), ((4 * half, 2 * events), b16), ((2 * half, HEAD_DIM), b16)],
+        pattern, own, crosses, far, after(keys[1], first), values[1], near_pack, both, keys[0], values[0], far_hist,
         flops=LONG,
     )
-    (sums,) = call(
-        rest_kernel,
-        [((2 * half, HEAD_DIM), b16)],
-        pattern, near_pack, both, after(keys[0], start), values[0], far_hist,
-    )
     outs = [part, part, ((2 * half, HEAD_DIM), b16)]
-    second, second_far, others = call(second_kernel, outs, weights, near_values, start)
+    second, second_far, others = call(second_kernel, outs, weights, near_values, start, flops=LONG)
     first, second = (
         reduced(*x) for x in ((first, first_far, sums, "seq", 1), (second, second_far, others, "blk", 2))
     )

time: 42.2 us -> 42 us (level)
  waiting for transfers between devices: 11.1 us -> 14.7 us
  starting transfers between devices: 19.3 us -> 16.3 us
  Pallas kernels: 11 us -> 10.3 us
    ppermute x15, waiting for transfers between devices: 11.1 us -> 14.7 us  [swapped(): return lax.ppermute(block, axis, [(i, i ^ mask) for i in range(size)])]
    ppermute x15, starting transfers between devices: 19.3 us -> 16.3 us  [swapped(): return lax.ppermute(block, axis, [(i, i ^ mask) for i in range(size)])]
    pallas_call x6 -> x5, Pallas kernels: 9.56 us -> 8.82 us  [call(): pl.pallas_call(kernel, out_shape=[jax.ShapeDtypeStruct(shape, kind) for s...]
  transfers between devices with their start and end apart: 15 -> 15, of which waited for: 9 -> 8; matrix products, arithmetic and copies ran while one was open for 1% -> 1% of each run, Pallas kernels for 21% -> 17%
where the time goes in v5:
time: 42 us; the launch traced here: 41.9 us
  starting transfers between devices  16.3 us (39%)
  waiting for transfers between devices  14.7 us (35%)
  Pallas kernels  10.3 us (25%)
    ppermute x15, starting transfers between devices, swapped(): return lax.ppermute(block, axis, [(i, i ^ mask) for i in range(size)])  16.3 us
    ppermute x15, waiting for transfers between devices, swapped(): return lax.ppermute(block, axis, [(i, i ^ mask) for i in range(size)])  14.7 us
    pallas_call x5, Pallas kernels, call(): pl.pallas_call(kernel, out_shape=[jax.ShapeDtypeStruct(shape, kind) for s...  8.82 us
    pallas_call x1, Pallas kernels, pack(): pl.pallas_call(pack_kernel, out_shape=[row_shape] * 2 + [both_shape] * 4,...  1.44 us
  transfers between devices with their start and end apart: 15, of which 8 were waited for; matrix products, arithmetic and copies ran while one was open for 1% of the time, Pallas kernels for 17%

profile of v5, /device:TPU:0, one launch (start us, length us, event | category | flops | bytes accessed | tf_op | source)
XLA Modules:
  0.0 41.9 jit_solution(14105618086352970549)
XLA Ops:
  0.0 1.4 %shard_map.55 = (bf16[128,256]{1,0:T(8,128)(2,1)S(1)}, bf16[128,256]{1,0:T(8,128)(2,1)S(1)}, bf16[1024,128]{1,0:T(8,128)(2,1)S(1)}, bf16[1024,128]{1,0:T(8,128)(...) custom-call(bf16[128,512]{1,0:T(8,128)(2,1)} %bitcast.4, bf16[512,512]{1,0:T(8,128)(2,1)} %keys.1, ...), custom_call_target="tpu_custom_call" | custom-call | flops 1 | bytes 1 | tf_op jit(solution)/shard_map/pallas_call | solution.py:65
  1.4 0.5 %collective-permute-start.1 = (bf16[1024,128]{1,0:T(8,128)(2,1)S(1)}, bf16[1024,128]{1,0:T(8,128)(2,1)S(1)}, u32[]{:S(2)}, u32[]{:S(2)}) collective-permute-start(bf16[1024,128]{1,0:T(8,128)(2,1)S(1)} %get-tuple-element.25), channel_id=1, source_target_pairs={{0,1},{1,0},{2,3},{3,2},{4,5},{5,4},{6,7},{7,6},{8,9},{9,8},{10,11... | collective-permute-start | bytes 786440 | tf_op jit(solution)/shard_map/ppermute | solution.py:29
  2.0 0.1 collective-permute-start
  2.0 0.4 %collective-permute-start.5 = (bf16[1024,128]{1,0:T(8,128)(2,1)S(1)}, bf16[1024,128]{1,0:T(8,128)(2,1)S(1)}, u32[]{:S(2)}, u32[]{:S(2)}) collective-permute-start(bf16[1024,128]{1,0:T(8,128)(2,1)S(1)} %get-tuple-element.29), channel_id=1, source_target_pairs={{0,1},{1,0},{2,3},{3,2},{4,5},{5,4},{6,7},{7,6},{8,9},{9,8},{10,11... | collective-permute-start | bytes 786440 | tf_op jit(solution)/shard_map/ppermute | solution.py:29
  2.5 0.7 %collective-permute-done = bf16[128,256]{1,0:T(8,128)(2,1)S(1)} collective-permute-done((bf16[128,256]{1,0:T(8,128)(2,1)S(1)}, bf16[128,256]{1,0:T(8,128)(2,1)S(1)}, u32[]{:S(2)}, u32[]{:S(2)}) %collective-permute-start) | collective-permute-done | bytes 65568 | tf_op jit(solution)/shard_map/ppermute | solution.py:29
  3.2 0.0 collective-permute-done.1
  3.3 0.0 copy-start.1
  3.4 2.9 %collective-permute-start.3 = (bf16[2048,128]{1,0:T(8,128)(2,1)S(1)}, bf16[2048,128]{1,0:T(8,128)(2,1)S(1)}, u32[]{:S(2)}, u32[]{:S(2)}) collective-permute-start(bf16[2048,128]{1,0:T(8,128)(2,1)S(1)} %pad_maximum_fusion), channel_id=1, source_target_pairs={{0,2},{1,3},{2,0},{3,1},{4,6},{5,7},{6,4},{7,5},{8,10},{9,11},{10,... | collective-permute-start | bytes 1572872 | tf_op jit(solution)/shard_map/ppermute | solution.py:29
  6.3 2.6 %collective-permute-start.2 = (bf16[256,256]{1,0:T(8,128)(2,1)S(1)}, bf16[256,256]{1,0:T(8,128)(2,1)S(1)}, u32[]{:S(2)}, u32[]{:S(2)}) collective-permute-start(bf16[256,256]{1,0:T(8,128)(2,1)S(1)} %pad_maximum_fusion.6.own), channel_id=1, source_target_pairs={{0,8},{4,12},{8,0},{12,4},{1,9},{5,13},{9,1},{13,5},{2,10},{6,14},... | collective-permute-start | bytes 393224 | tf_op jit(solution)/shard_map/ppermute | solution.py:29
  8.9 0.0 collective-permute-done.5
  9.0 1.6 %collective-permute-start.6 = (bf16[1280,128]{1,0:T(8,128)(2,1)S(1)}, bf16[1280,128]{1,0:T(8,128)(2,1)S(1)}, u32[]{:S(2)}, u32[]{:S(2)}) collective-permute-start(bf16[1280,128]{1,0:T(8,128)(2,1)S(1)} %pad_maximum_fusion.1), channel_id=1, source_target_pairs={{0,4},{4,0},{8,12},{12,8},{1,5},{5,1},{9,13},{13,9},{2,6},{6,2},{1... | collective-permute-start | bytes 983048 | tf_op jit(solution)/shard_map/ppermute | solution.py:29
  10.6 4.7 %collective-permute-done.2.far = bf16[256,256]{1,0:T(8,128)(2,1)S(1)} collective-permute-done((bf16[256,256]{1,0:T(8,128)(2,1)S(1)}, bf16[256,256]{1,0:T(8,128)(2,1)S(1)}, u32[]{:S(2)}, u32[]{:S(2)}) %collective-permute-start.2) | collective-permute-done | bytes 131104 | tf_op jit(solution)/shard_map/ppermute | solution.py:29
  15.4 0.6 %collective-permute-start.4 = (bf16[512,128]{1,0:T(8,128)(2,1)S(1)}, bf16[512,128]{1,0:T(8,128)(2,1)S(1)}, u32[]{:S(2)}, u32[]{:S(2)}) collective-permute-start(bf16[512,128]{1,0:T(8,128)(2,1)S(1)} %pad_maximum_fusion.7), channel_id=1, source_target_pairs={{0,2},{1,3},{2,0},{3,1},{4,6},{5,7},{6,4},{7,5},{8,10},{9,11},{10,... | collective-permute-start | bytes 393224 | tf_op jit(solution)/shard_map/ppermute | solution.py:29
  16.0 0.7 %collective-permute-start.7 = (bf16[256,128]{1,0:T(8,128)(2,1)S(1)}, bf16[256,128]{1,0:T(8,128)(2,1)S(1)}, u32[]{:S(2)}, u32[]{:S(2)}) collective-permute-start(bf16[256,128]{1,0:T(8,128)(2,1)S(1)} %get-tuple-element.51), channel_id=1, source_target_pairs={{0,4},{4,0},{8,12},{12,8},{1,5},{5,1},{9,13},{13,9},{2,6},{6,2},{1... | collective-permute-start | bytes 196616 | tf_op jit(solution)/shard_map/ppermute | solution.py:29
  16.7 1.4 %collective-permute-start.11 = (bf16[1024,128]{1,0:T(8,128)(2,1)S(1)}, bf16[1024,128]{1,0:T(8,128)(2,1)S(1)}, u32[]{:S(2)}, u32[]{:S(2)}) collective-permute-start(bf16[1024,128]{1,0:T(8,128)(2,1)S(1)} %pad_maximum_fusion.5.values), channel_id=1, source_target_pairs={{0,4},{4,0},{8,12},{12,8},{1,5},{5,1},{9,13},{13,9},{2,6},{6,2},{1... | collective-permute-start | bytes 786440 | tf_op jit(solution)/shard_map/ppermute | solution.py:29
  18.1 0.0 copy-done.1
  18.1 1.5 %shard_map.56.start = f32[512,128]{1,0:T(8,128)S(1)} custom-call(s32[16,16]{1,0:T(8,128)S(1)} %copy-done.1, bf16[256,256]{1,0:T(8,128)(2,1)S(1)} %pad_maximum_fusion.6.own, bf16[256,256]{1,0:T(8,128)(2,1)S(1)} %collective-permute-done.2.far, bf16[1024,128]{1,0:T(8,128)(2,1)S(1)} %pad_maximum_fusion.2.keys.first_keys, ...), custom_call_target="tpu_custom_call" | custom-call | flops 1 | bytes 1 | tf_op jit(solution)/shard_map/pallas_call | solution.py:165
  19.6 0.0 collective-permute-done.3.far_hist
  19.6 1.5 %shard_map.57 = (f32[256,128]{1,0:T(8,128)S(1)}, f32[256,128]{1,0:T(8,128)S(1)}) custom-call(s32[16,16]{1,0:T(8,128)S(1)} %copy-done.1, bf16[256,256]{1,0:T(8,128)(2,1)S(1)} %pad_maximum_fusion.6.own, bf16[256,256]{1,0:T(8,128)(2,1)S(1)} %collective-permute-done.2.far, bf16[2048,128]{1,0:T(8,128)(2,1)S(1)} %collective-permute-done.3.far_hist, ...), custom_call_target="tpu_custom_call" | custom-call | flops 1 | bytes 1 | tf_op jit(solution)/shard_map/pallas_call | solution.py:165
  21.1 1.6 %collective-permute-done.7.both = bf16[256,128]{1,0:T(8,128)(2,1)S(1)} collective-permute-done((bf16[256,128]{1,0:T(8,128)(2,1)S(1)}, bf16[256,128]{1,0:T(8,128)(2,1)S(1)}, u32[]{:S(2)}, u32[]{:S(2)}) %collective-permute-start.7) | collective-permute-done | bytes 65568 | tf_op jit(solution)/shard_map/ppermute | solution.py:29
  22.7 0.0 collective-permute-done.4.crosses
  22.7 0.0 collective-permute-done.6.near_pack
  22.7 4.4 %shard_map.58 = (f32[1024,128]{1,0:T(8,128)S(1)}, bf16[1024,1024]{1,0:T(8,128)(2,1)S(1)}, bf16[512,128]{1,0:T(8,128)(2,1)S(1)}) custom-call(s32[16,16]{1,0:T(8,128)S(1)} %copy-done.1, bf16[256,256]{1,0:T(8,128)(2,1)S(1)} %pad_maximum_fusion.6.own, bf16[512,128]{1,0:T(8,128)(2,1)S(1)} %collective-permute-done.4.crosses, ...), custom_call_target="tpu_custom_call" | custom-call | flops 10000000000 | bytes 1 | tf_op jit(solution)/shard_map/pallas_call | solution.py:165
  27.1 0.0 collective-permute-done.11.near_values
  27.1 0.7 %shard_map.59 = (f32[256,128]{1,0:T(8,128)S(1)}, f32[256,128]{1,0:T(8,128)S(1)}, bf16[512,128]{1,0:T(8,128)(2,1)S(1)}) custom-call(bf16[1024,1024]{1,0:T(8,128)(2,1)S(1)} %get-tuple-element.33.weights, bf16[1024,128]{1,0:T(8,128)(2,1)S(1)} %collective-permute-done.11.near_values, f32[1024,128]{1,0:T(8,128)S(1)} %get-tuple-element.35.start), custom_call_target="tpu_custom_call" | custom-call | flops 10000000000 | bytes 1 | tf_op jit(solution)/shard_map/pallas_call | solution.py:165
  27.8 0.0 copy-start
  27.8 0.5 %collective-permute-start.12 = (bf16[512,128]{1,0:T(8,128)(2,1)S(1)}, bf16[512,128]{1,0:T(8,128)(2,1)S(1)}, u32[]{:S(2)}, u32[]{:S(2)}) collective-permute-start(bf16[512,128]{1,0:T(8,128)(2,1)S(1)} %get-tuple-element.37), channel_id=1, source_target_pairs={{0,2},{1,3},{2,0},{3,1},{4,6},{5,7},{6,4},{7,5},{8,10},{9,11},{10,... | collective-permute-start | bytes 393224 | tf_op jit(solution)/shard_map/ppermute | solution.py:29
  28.4 1.4 %collective-permute-start.8 = (bf16[512,128]{1,0:T(8,128)(2,1)S(1)}, bf16[512,128]{1,0:T(8,128)(2,1)S(1)}, u32[]{:S(2)}, u32[]{:S(2)}) collective-permute-start(bf16[512,128]{1,0:T(8,128)(2,1)S(1)} %get-tuple-element.31), channel_id=1, source_target_pairs={{0,4},{4,0},{8,12},{12,8},{1,5},{5,1},{9,13},{13,9},{2,6},{6,2},{1... | collective-permute-start | bytes 393224 | tf_op jit(solution)/shard_map/ppermute | solution.py:29
  29.8 3.1 %collective-permute-done.12 = bf16[512,128]{1,0:T(8,128)(2,1)S(1)} collective-permute-done((bf16[512,128]{1,0:T(8,128)(2,1)S(1)}, bf16[512,128]{1,0:T(8,128)(2,1)S(1)}, u32[]{:S(2)}, u32[]{:S(2)}) %collective-permute-start.12) | collective-permute-done | bytes 131104 | tf_op jit(solution)/shard_map/ppermute | solution.py:29
  32.9 1.5 %collective-permute-start.13 = (bf16[256,128]{1,0:T(8,128)(2,1)S(1)}, bf16[256,128]{1,0:T(8,128)(2,1)S(1)}, u32[]{:S(2)}, u32[]{:S(2)}) collective-permute-start(bf16[256,128]{1,0:T(8,128)(2,1)S(1)} %fusion), channel_id=1, source_target_pairs={{0,8},{4,12},{8,0},{12,4},{1,9},{5,13},{9,1},{13,5},{2,10},{6,14},... | collective-permute-start | bytes 196616 | tf_op jit(solution)/shard_map/ppermute | solution.py:29
  34.4 0.0 collective-permute-done.8
  34.5 1.8 %collective-permute-start.9 = (bf16[256,128]{1,0:T(8,128)(2,1)S(1)}, bf16[256,128]{1,0:T(8,128)(2,1)S(1)}, u32[]{:S(2)}, u32[]{:S(2)}) collective-permute-start(bf16[256,128]{1,0:T(8,128)(2,1)S(1)} %fusion.2), channel_id=1, source_target_pairs={{0,8},{4,12},{8,0},{12,4},{1,9},{5,13},{9,1},{13,5},{2,10},{6,14},... | collective-permute-start | bytes 196616 | tf_op jit(solution)/shard_map/ppermute | solution.py:29
  36.3 2.7 %collective-permute-done.13 = bf16[256,128]{1,0:T(8,128)(2,1)S(1)} collective-permute-done((bf16[256,128]{1,0:T(8,128)(2,1)S(1)}, bf16[256,128]{1,0:T(8,128)(2,1)S(1)}, u32[]{:S(2)}, u32[]{:S(2)}) %collective-permute-start.13) | collective-permute-done | bytes 65568 | tf_op jit(solution)/shard_map/ppermute | solution.py:29
  39.1 0.1 collective-permute-start.14
  39.1 0.6 %collective-permute-done.9 = bf16[256,128]{1,0:T(8,128)(2,1)S(1)} collective-permute-done((bf16[256,128]{1,0:T(8,128)(2,1)S(1)}, bf16[256,128]{1,0:T(8,128)(2,1)S(1)}, u32[]{:S(2)}, u32[]{:S(2)}) %collective-permute-start.9) | collective-permute-done | bytes 65568 | tf_op jit(solution)/shard_map/ppermute | solution.py:29
  39.8 0.1 collective-permute-start.10
  39.8 0.5 %collective-permute-done.14.second_theirs = f32[128,128]{1,0:T(8,128)S(1)} collective-permute-done((f32[128,128]{1,0:T(8,128)S(1)}, f32[128,128]{1,0:T(8,128)S(1)}, u32[]{:S(2)}, u32[]{:S(2)}) %collective-permute-start.14) | collective-permute-done | bytes 65568 | tf_op jit(solution)/shard_map/ppermute | solution.py:29
  40.4 0.7 %collective-permute-done.10.first_theirs = f32[128,128]{1,0:T(8,128)S(1)} collective-permute-done((f32[128,128]{1,0:T(8,128)S(1)}, f32[128,128]{1,0:T(8,128)S(1)}, u32[]{:S(2)}, u32[]{:S(2)}) %collective-permute-start.10) | collective-permute-done | bytes 65568 | tf_op jit(solution)/shard_map/ppermute | solution.py:29
  41.1 0.0 copy-done
  41.1 0.8 %shard_map.60 = bf16[128,512]{1,0:T(8,128)(2,1)} custom-call(bf16[128,512]{1,0:T(8,128)(2,1)S(1)} %bitcast.3, f32[128,128]{1,0:T(8,128)S(1)} %get-tuple-element.50.first_mine, f32[128,128]{1,0:T(8,128)S(1)} %collective-permute-done.10.first_theirs, f32[128,128]{1,0:T(8,128)S(1)} %get-tuple-element.48.second_mine, ...), custom_call_target="tpu_custom_call" | custom-call | flops 1 | bytes 1 | tf_op jit(solution)/shard_map/pallas_call | solution.py:165
  (21 shorter events, 0.4 us)
Async XLA Ops:
  1.4 1.8 %collective-permute-start.1 = (bf16[1024,128]{1,0:T(8,128)(2,1)S(1)}, bf16[1024,128]{1,0:T(8,128)(2,1)S(1)}, u32[]{:S(2)}, u32[]{:S(2)}) collective-permute-start(bf16[1024,128]{1,0:T(8,128)(2,1)S(1)} %get-tuple-element.25), channel_id=1, source_target_pairs={{0,1},{1,0},{2,3},{3,2},{4,5},{5,4},{6,7},{7,6},{8,9},{9,8},{10,11... | collective-permute-start | bytes 786440 | tf_op jit(solution)/shard_map/ppermute | solution.py:29
  2.0 1.3 %collective-permute-start = (bf16[128,256]{1,0:T(8,128)(2,1)S(1)}, bf16[128,256]{1,0:T(8,128)(2,1)S(1)}, u32[]{:S(2)}, u32[]{:S(2)}) collective-permute-start(bf16[128,256]{1,0:T(8,128)(2,1)S(1)} %get-tuple-element.23), channel_id=1, source_target_pairs={{0,1},{1,0},{2,3},{3,2},{4,5},{5,4},{6,7},{7,6},{8,9},{9,8},{10,11... | collective-permute-start | bytes 196616 | tf_op jit(solution)/shard_map/ppermute | solution.py:29
  2.0 6.8 %collective-permute-start.5 = (bf16[1024,128]{1,0:T(8,128)(2,1)S(1)}, bf16[1024,128]{1,0:T(8,128)(2,1)S(1)}, u32[]{:S(2)}, u32[]{:S(2)}) collective-permute-start(bf16[1024,128]{1,0:T(8,128)(2,1)S(1)} %get-tuple-element.29), channel_id=1, source_target_pairs={{0,1},{1,0},{2,3},{3,2},{4,5},{5,4},{6,7},{7,6},{8,9},{9,8},{10,11... | collective-permute-start | bytes 786440 | tf_op jit(solution)/shard_map/ppermute | solution.py:29
  3.3 14.8 %copy-start.1 = (s32[16,16]{1,0:T(8,128)S(1)}, s32[16,16]{1,0:T(8,128)}, u32[]{:S(2)}) copy-start(s32[16,16]{1,0:T(8,128)} %pattern.5) | copy-start | bytes 3076
  3.4 16.3 %collective-permute-start.3 = (bf16[2048,128]{1,0:T(8,128)(2,1)S(1)}, bf16[2048,128]{1,0:T(8,128)(2,1)S(1)}, u32[]{:S(2)}, u32[]{:S(2)}) collective-permute-start(bf16[2048,128]{1,0:T(8,128)(2,1)S(1)} %pad_maximum_fusion), channel_id=1, source_target_pairs={{0,2},{1,3},{2,0},{3,1},{4,6},{5,7},{6,4},{7,5},{8,10},{9,11},{10,... | collective-permute-start | bytes 1572872 | tf_op jit(solution)/shard_map/ppermute | solution.py:29
  6.3 9.1 %collective-permute-start.2 = (bf16[256,256]{1,0:T(8,128)(2,1)S(1)}, bf16[256,256]{1,0:T(8,128)(2,1)S(1)}, u32[]{:S(2)}, u32[]{:S(2)}) collective-permute-start(bf16[256,256]{1,0:T(8,128)(2,1)S(1)} %pad_maximum_fusion.6.own), channel_id=1, source_target_pairs={{0,8},{4,12},{8,0},{12,4},{1,9},{5,13},{9,1},{13,5},{2,10},{6,14},... | collective-permute-start | bytes 393224 | tf_op jit(solution)/shard_map/ppermute | solution.py:29
  9.0 13.8 %collective-permute-start.6 = (bf16[1280,128]{1,0:T(8,128)(2,1)S(1)}, bf16[1280,128]{1,0:T(8,128)(2,1)S(1)}, u32[]{:S(2)}, u32[]{:S(2)}) collective-permute-start(bf16[1280,128]{1,0:T(8,128)(2,1)S(1)} %pad_maximum_fusion.1), channel_id=1, source_target_pairs={{0,4},{4,0},{8,12},{12,8},{1,5},{5,1},{9,13},{13,9},{2,6},{6,2},{1... | collective-permute-start | bytes 983048 | tf_op jit(solution)/shard_map/ppermute | solution.py:29
  15.4 7.3 %collective-permute-start.4 = (bf16[512,128]{1,0:T(8,128)(2,1)S(1)}, bf16[512,128]{1,0:T(8,128)(2,1)S(1)}, u32[]{:S(2)}, u32[]{:S(2)}) collective-permute-start(bf16[512,128]{1,0:T(8,128)(2,1)S(1)} %pad_maximum_fusion.7), channel_id=1, source_target_pairs={{0,2},{1,3},{2,0},{3,1},{4,6},{5,7},{6,4},{7,5},{8,10},{9,11},{10,... | collective-permute-start | bytes 393224 | tf_op jit(solution)/shard_map/ppermute | solution.py:29
  16.0 6.8 %collective-permute-start.7 = (bf16[256,128]{1,0:T(8,128)(2,1)S(1)}, bf16[256,128]{1,0:T(8,128)(2,1)S(1)}, u32[]{:S(2)}, u32[]{:S(2)}) collective-permute-start(bf16[256,128]{1,0:T(8,128)(2,1)S(1)} %get-tuple-element.51), channel_id=1, source_target_pairs={{0,4},{4,0},{8,12},{12,8},{1,5},{5,1},{9,13},{13,9},{2,6},{6,2},{1... | collective-permute-start | bytes 196616 | tf_op jit(solution)/shard_map/ppermute | solution.py:29
  16.7 10.4 %collective-permute-start.11 = (bf16[1024,128]{1,0:T(8,128)(2,1)S(1)}, bf16[1024,128]{1,0:T(8,128)(2,1)S(1)}, u32[]{:S(2)}, u32[]{:S(2)}) collective-permute-start(bf16[1024,128]{1,0:T(8,128)(2,1)S(1)} %pad_maximum_fusion.5.values), channel_id=1, source_target_pairs={{0,4},{4,0},{8,12},{12,8},{1,5},{5,1},{9,13},{13,9},{2,6},{6,2},{1... | collective-permute-start | bytes 786440 | tf_op jit(solution)/shard_map/ppermute | solution.py:29
  27.8 13.3 %copy-start = (bf16[1,128,512]{2,1,0:T(8,128)(2,1)S(1)}, bf16[1,128,512]{2,1,0:T(8,128)(2,1)}, u32[]{:S(2)}) copy-start(bf16[1,128,512]{2,1,0:T(8,128)(2,1)} %param.6) | copy-start | bytes 393220
  27.8 5.0 %collective-permute-start.12 = (bf16[512,128]{1,0:T(8,128)(2,1)S(1)}, bf16[512,128]{1,0:T(8,128)(2,1)S(1)}, u32[]{:S(2)}, u32[]{:S(2)}) collective-permute-start(bf16[512,128]{1,0:T(8,128)(2,1)S(1)} %get-tuple-element.37), channel_id=1, source_target_pairs={{0,2},{1,3},{2,0},{3,1},{4,6},{5,7},{6,4},{7,5},{8,10},{9,11},{10,... | collective-permute-start | bytes 393224 | tf_op jit(solution)/shard_map/ppermute | solution.py:29
  28.4 6.0 %collective-permute-start.8 = (bf16[512,128]{1,0:T(8,128)(2,1)S(1)}, bf16[512,128]{1,0:T(8,128)(2,1)S(1)}, u32[]{:S(2)}, u32[]{:S(2)}) collective-permute-start(bf16[512,128]{1,0:T(8,128)(2,1)S(1)} %get-tuple-element.31), channel_id=1, source_target_pairs={{0,4},{4,0},{8,12},{12,8},{1,5},{5,1},{9,13},{13,9},{2,6},{6,2},{1... | collective-permute-start | bytes 393224 | tf_op jit(solution)/shard_map/ppermute | solution.py:29
  32.9 6.1 %collective-permute-start.13 = (bf16[256,128]{1,0:T(8,128)(2,1)S(1)}, bf16[256,128]{1,0:T(8,128)(2,1)S(1)}, u32[]{:S(2)}, u32[]{:S(2)}) collective-permute-start(bf16[256,128]{1,0:T(8,128)(2,1)S(1)} %fusion), channel_id=1, source_target_pairs={{0,8},{4,12},{8,0},{12,4},{1,9},{5,13},{9,1},{13,5},{2,10},{6,14},... | collective-permute-start | bytes 196616 | tf_op jit(solution)/shard_map/ppermute | solution.py:29
  34.5 5.3 %collective-permute-start.9 = (bf16[256,128]{1,0:T(8,128)(2,1)S(1)}, bf16[256,128]{1,0:T(8,128)(2,1)S(1)}, u32[]{:S(2)}, u32[]{:S(2)}) collective-permute-start(bf16[256,128]{1,0:T(8,128)(2,1)S(1)} %fusion.2), channel_id=1, source_target_pairs={{0,8},{4,12},{8,0},{12,4},{1,9},{5,13},{9,1},{13,5},{2,10},{6,14},... | collective-permute-start | bytes 196616 | tf_op jit(solution)/shard_map/ppermute | solution.py:29
  39.1 1.3 %collective-permute-start.14 = (f32[128,128]{1,0:T(8,128)S(1)}, f32[128,128]{1,0:T(8,128)S(1)}, u32[]{:S(2)}, u32[]{:S(2)}) collective-permute-start(f32[128,128]{1,0:T(8,128)S(1)} %get-tuple-element.47), channel_id=1, source_target_pairs={{0,1},{1,0},{2,3},{3,2},{4,5},{5,4},{6,7},{7,6},{8,9},{9,8},{10,11... | collective-permute-start | bytes 196616 | tf_op jit(solution)/shard_map/ppermute | solution.py:29
  39.8 1.3 %collective-permute-start.10 = (f32[128,128]{1,0:T(8,128)S(1)}, f32[128,128]{1,0:T(8,128)S(1)}, u32[]{:S(2)}, u32[]{:S(2)}) collective-permute-start(f32[128,128]{1,0:T(8,128)S(1)} %get-tuple-element.49), channel_id=1, source_target_pairs={{0,1},{1,0},{2,3},{3,2},{4,5},{5,4},{6,7},{7,6},{8,9},{9,8},{10,11... | collective-permute-start | bytes 196616 | tf_op jit(solution)/shard_map/ppermute | solution.py:29

commit v6 on v5

--- a/solution.py
+++ b/solution.py
@@ -211,7 +211,7 @@
     far_hist = swapped(hist, "blk", 2)
     near_pack = swapped(jnp.concatenate([own[:, :HEAD_DIM], keys[1]], axis=0), "seq", 1)
     both = swapped(far[:, :HEAD_DIM], "seq", 1)
-    near_values = swapped(after(values[1], far), "seq", 1)
+    near_values = swapped(after(values[1], near_pack), "seq", 1)
     crosses = swapped(jnp.concatenate([own[:, HEAD_DIM:], far[:, HEAD_DIM:]], axis=0), "blk", 2)
 
     f32, b16 = jnp.float32, jnp.bfloat16

time: 42 us -> 42 us (level)
  starting transfers between devices: 16.3 us -> 15.4 us
  waiting for transfers between devices: 14.7 us -> 15.6 us
    ppermute x15, starting transfers between devices: 16.3 us -> 15.4 us  [swapped(): return lax.ppermute(block, axis, [(i, i ^ mask) for i in range(size)])]
    ppermute x15, waiting for transfers between devices: 14.7 us -> 15.6 us  [swapped(): return lax.ppermute(block, axis, [(i, i ^ mask) for i in range(size)])]
  transfers between devices with their start and end apart: 15 -> 15, of which waited for: 8 -> 8; matrix products, arithmetic and copies ran while one was open for 1% -> 1% of each run, Pallas kernels for 17% -> 19%
where the time goes in v6:
time: 42 us; the launch traced here: 41.9 us
  waiting for transfers between devices  15.6 us (37%)
  starting transfers between devices  15.4 us (37%)
  Pallas kernels  10.3 us (25%)
    ppermute x15, waiting for transfers between devices, swapped(): return lax.ppermute(block, axis, [(i, i ^ mask) for i in range(size)])  15.6 us
    ppermute x15, starting transfers between devices, swapped(): return lax.ppermute(block, axis, [(i, i ^ mask) for i in range(size)])  15.4 us
    pallas_call x5, Pallas kernels, call(): pl.pallas_call(kernel, out_shape=[jax.ShapeDtypeStruct(shape, kind) for s...  8.83 us
    pallas_call x1, Pallas kernels, pack(): pl.pallas_call(pack_kernel, out_shape=[row_shape] * 2 + [both_shape] * 4,...  1.44 us
  transfers between devices with their start and end apart: 15, of which 8 were waited for; matrix products, arithmetic and copies ran while one was open for 1% of the time, Pallas kernels for 19%

profile of v6, /device:TPU:0, one launch (start us, length us, event | category | flops | bytes accessed | tf_op | source)
XLA Modules:
  0.0 41.9 jit_solution(8754884999988621671)
XLA Ops:
  0.0 1.4 %shard_map.55 = (bf16[128,256]{1,0:T(8,128)(2,1)S(1)}, bf16[128,256]{1,0:T(8,128)(2,1)S(1)}, bf16[1024,128]{1,0:T(8,128)(2,1)S(1)}, bf16[1024,128]{1,0:T(8,128)(...) custom-call(bf16[128,512]{1,0:T(8,128)(2,1)} %bitcast.4, bf16[512,512]{1,0:T(8,128)(2,1)} %keys.1, ...), custom_call_target="tpu_custom_call" | custom-call | flops 1 | bytes 1 | tf_op jit(solution)/shard_map/pallas_call | solution.py:65
  1.4 0.5 %collective-permute-start.1 = (bf16[1024,128]{1,0:T(8,128)(2,1)S(1)}, bf16[1024,128]{1,0:T(8,128)(2,1)S(1)}, u32[]{:S(2)}, u32[]{:S(2)}) collective-permute-start(bf16[1024,128]{1,0:T(8,128)(2,1)S(1)} %get-tuple-element.25), channel_id=1, source_target_pairs={{0,1},{1,0},{2,3},{3,2},{4,5},{5,4},{6,7},{7,6},{8,9},{9,8},{10,11... | collective-permute-start | bytes 786440 | tf_op jit(solution)/shard_map/ppermute | solution.py:29
  2.0 0.1 collective-permute-start
  2.0 0.4 %collective-permute-start.5 = (bf16[1024,128]{1,0:T(8,128)(2,1)S(1)}, bf16[1024,128]{1,0:T(8,128)(2,1)S(1)}, u32[]{:S(2)}, u32[]{:S(2)}) collective-permute-start(bf16[1024,128]{1,0:T(8,128)(2,1)S(1)} %get-tuple-element.29), channel_id=1, source_target_pairs={{0,1},{1,0},{2,3},{3,2},{4,5},{5,4},{6,7},{7,6},{8,9},{9,8},{10,11... | collective-permute-start | bytes 786440 | tf_op jit(solution)/shard_map/ppermute | solution.py:29
  2.5 0.7 %collective-permute-done = bf16[128,256]{1,0:T(8,128)(2,1)S(1)} collective-permute-done((bf16[128,256]{1,0:T(8,128)(2,1)S(1)}, bf16[128,256]{1,0:T(8,128)(2,1)S(1)}, u32[]{:S(2)}, u32[]{:S(2)}) %collective-permute-start) | collective-permute-done | bytes 65568 | tf_op jit(solution)/shard_map/ppermute | solution.py:29
  3.2 0.0 collective-permute-done.1
  3.3 0.0 copy-start.1
  3.4 2.9 %collective-permute-start.3 = (bf16[2048,128]{1,0:T(8,128)(2,1)S(1)}, bf16[2048,128]{1,0:T(8,128)(2,1)S(1)}, u32[]{:S(2)}, u32[]{:S(2)}) collective-permute-start(bf16[2048,128]{1,0:T(8,128)(2,1)S(1)} %pad_maximum_fusion), channel_id=1, source_target_pairs={{0,2},{1,3},{2,0},{3,1},{4,6},{5,7},{6,4},{7,5},{8,10},{9,11},{10,... | collective-permute-start | bytes 1572872 | tf_op jit(solution)/shard_map/ppermute | solution.py:29
  6.3 2.6 %collective-permute-start.2 = (bf16[256,256]{1,0:T(8,128)(2,1)S(1)}, bf16[256,256]{1,0:T(8,128)(2,1)S(1)}, u32[]{:S(2)}, u32[]{:S(2)}) collective-permute-start(bf16[256,256]{1,0:T(8,128)(2,1)S(1)} %pad_maximum_fusion.6.own), channel_id=1, source_target_pairs={{0,8},{4,12},{8,0},{12,4},{1,9},{5,13},{9,1},{13,5},{2,10},{6,14},... | collective-permute-start | bytes 393224 | tf_op jit(solution)/shard_map/ppermute | solution.py:29
  8.9 0.0 collective-permute-done.5
  9.0 1.6 %collective-permute-start.6 = (bf16[1280,128]{1,0:T(8,128)(2,1)S(1)}, bf16[1280,128]{1,0:T(8,128)(2,1)S(1)}, u32[]{:S(2)}, u32[]{:S(2)}) collective-permute-start(bf16[1280,128]{1,0:T(8,128)(2,1)S(1)} %pad_maximum_fusion.1), channel_id=1, source_target_pairs={{0,4},{4,0},{8,12},{12,8},{1,5},{5,1},{9,13},{13,9},{2,6},{6,2},{1... | collective-permute-start | bytes 983048 | tf_op jit(solution)/shard_map/ppermute | solution.py:29
  10.6 4.7 %collective-permute-done.2.far = bf16[256,256]{1,0:T(8,128)(2,1)S(1)} collective-permute-done((bf16[256,256]{1,0:T(8,128)(2,1)S(1)}, bf16[256,256]{1,0:T(8,128)(2,1)S(1)}, u32[]{:S(2)}, u32[]{:S(2)}) %collective-permute-start.2) | collective-permute-done | bytes 131104 | tf_op jit(solution)/shard_map/ppermute | solution.py:29
  15.4 0.6 %collective-permute-start.4 = (bf16[512,128]{1,0:T(8,128)(2,1)S(1)}, bf16[512,128]{1,0:T(8,128)(2,1)S(1)}, u32[]{:S(2)}, u32[]{:S(2)}) collective-permute-start(bf16[512,128]{1,0:T(8,128)(2,1)S(1)} %pad_maximum_fusion.7), channel_id=1, source_target_pairs={{0,2},{1,3},{2,0},{3,1},{4,6},{5,7},{6,4},{7,5},{8,10},{9,11},{10,... | collective-permute-start | bytes 393224 | tf_op jit(solution)/shard_map/ppermute | solution.py:29
  16.0 0.7 %collective-permute-start.7 = (bf16[256,128]{1,0:T(8,128)(2,1)S(1)}, bf16[256,128]{1,0:T(8,128)(2,1)S(1)}, u32[]{:S(2)}, u32[]{:S(2)}) collective-permute-start(bf16[256,128]{1,0:T(8,128)(2,1)S(1)} %get-tuple-element.51), channel_id=1, source_target_pairs={{0,4},{4,0},{8,12},{12,8},{1,5},{5,1},{9,13},{13,9},{2,6},{6,2},{1... | collective-permute-start | bytes 196616 | tf_op jit(solution)/shard_map/ppermute | solution.py:29
  16.7 0.0 copy-done.1
  16.7 1.5 %shard_map.56.start = f32[512,128]{1,0:T(8,128)S(1)} custom-call(s32[16,16]{1,0:T(8,128)S(1)} %copy-done.1, bf16[256,256]{1,0:T(8,128)(2,1)S(1)} %pad_maximum_fusion.6.own, bf16[256,256]{1,0:T(8,128)(2,1)S(1)} %collective-permute-done.2.far, bf16[1024,128]{1,0:T(8,128)(2,1)S(1)} %pad_maximum_fusion.2.keys.first_keys, ...), custom_call_target="tpu_custom_call" | custom-call | flops 1 | bytes 1 | tf_op jit(solution)/shard_map/pallas_call | solution.py:165
  18.2 2.4 %collective-permute-done.6.near_pack = bf16[1280,128]{1,0:T(8,128)(2,1)S(1)} collective-permute-done((bf16[1280,128]{1,0:T(8,128)(2,1)S(1)}, bf16[1280,128]{1,0:T(8,128)(2,1)S(1)}, u32[]{:S(2)}, u32[]{:S(2)}) %collective-permute-start.6) | collective-permute-done | bytes 327712 | tf_op jit(solution)/shard_map/ppermute | solution.py:29
  20.6 1.3 %collective-permute-start.11 = (bf16[1024,128]{1,0:T(8,128)(2,1)S(1)}, bf16[1024,128]{1,0:T(8,128)(2,1)S(1)}, u32[]{:S(2)}, u32[]{:S(2)}) collective-permute-start(bf16[1024,128]{1,0:T(8,128)(2,1)S(1)} %pad_maximum_fusion.5.values), channel_id=1, source_target_pairs={{0,4},{4,0},{8,12},{12,8},{1,5},{5,1},{9,13},{13,9},{2,6},{6,2},{1... | collective-permute-start | bytes 786440 | tf_op jit(solution)/shard_map/ppermute | solution.py:29
  21.9 0.0 collective-permute-done.3.far_hist
  21.9 1.5 %shard_map.57 = (f32[256,128]{1,0:T(8,128)S(1)}, f32[256,128]{1,0:T(8,128)S(1)}) custom-call(s32[16,16]{1,0:T(8,128)S(1)} %copy-done.1, bf16[256,256]{1,0:T(8,128)(2,1)S(1)} %pad_maximum_fusion.6.own, bf16[256,256]{1,0:T(8,128)(2,1)S(1)} %collective-permute-done.2.far, bf16[2048,128]{1,0:T(8,128)(2,1)S(1)} %collective-permute-done.3.far_hist, ...), custom_call_target="tpu_custom_call" | custom-call | flops 1 | bytes 1 | tf_op jit(solution)/shard_map/pallas_call | solution.py:165
  23.4 0.0 collective-permute-done.7.both
  23.4 0.0 collective-permute-done.4.crosses
  23.4 4.4 %shard_map.58 = (f32[1024,128]{1,0:T(8,128)S(1)}, bf16[1024,1024]{1,0:T(8,128)(2,1)S(1)}, bf16[512,128]{1,0:T(8,128)(2,1)S(1)}) custom-call(s32[16,16]{1,0:T(8,128)S(1)} %copy-done.1, bf16[256,256]{1,0:T(8,128)(2,1)S(1)} %pad_maximum_fusion.6.own, bf16[512,128]{1,0:T(8,128)(2,1)S(1)} %collective-permute-done.4.crosses, ...), custom_call_target="tpu_custom_call" | custom-call | flops 10000000000 | bytes 1 | tf_op jit(solution)/shard_map/pallas_call | solution.py:165
  27.7 0.8 %collective-permute-start.8 = (bf16[512,128]{1,0:T(8,128)(2,1)S(1)}, bf16[512,128]{1,0:T(8,128)(2,1)S(1)}, u32[]{:S(2)}, u32[]{:S(2)}) collective-permute-start(bf16[512,128]{1,0:T(8,128)(2,1)S(1)} %get-tuple-element.31), channel_id=1, source_target_pairs={{0,4},{4,0},{8,12},{12,8},{1,5},{5,1},{9,13},{13,9},{2,6},{6,2},{1... | collective-permute-start | bytes 393224 | tf_op jit(solution)/shard_map/ppermute | solution.py:29
  28.6 0.0 collective-permute-done.11.near_values
  28.6 0.7 %shard_map.59 = (f32[256,128]{1,0:T(8,128)S(1)}, f32[256,128]{1,0:T(8,128)S(1)}, bf16[512,128]{1,0:T(8,128)(2,1)S(1)}) custom-call(bf16[1024,1024]{1,0:T(8,128)(2,1)S(1)} %get-tuple-element.33.weights, bf16[1024,128]{1,0:T(8,128)(2,1)S(1)} %collective-permute-done.11.near_values, f32[1024,128]{1,0:T(8,128)S(1)} %get-tuple-element.35.start), custom_call_target="tpu_custom_call" | custom-call | flops 10000000000 | bytes 1 | tf_op jit(solution)/shard_map/pallas_call | solution.py:165
  29.3 0.0 copy-start
  29.3 0.5 %collective-permute-start.12 = (bf16[512,128]{1,0:T(8,128)(2,1)S(1)}, bf16[512,128]{1,0:T(8,128)(2,1)S(1)}, u32[]{:S(2)}, u32[]{:S(2)}) collective-permute-start(bf16[512,128]{1,0:T(8,128)(2,1)S(1)} %get-tuple-element.37), channel_id=1, source_target_pairs={{0,2},{1,3},{2,0},{3,1},{4,6},{5,7},{6,4},{7,5},{8,10},{9,11},{10,... | collective-permute-start | bytes 393224 | tf_op jit(solution)/shard_map/ppermute | solution.py:29
  29.9 2.9 %collective-permute-done.8 = bf16[512,128]{1,0:T(8,128)(2,1)S(1)} collective-permute-done((bf16[512,128]{1,0:T(8,128)(2,1)S(1)}, bf16[512,128]{1,0:T(8,128)(2,1)S(1)}, u32[]{:S(2)}, u32[]{:S(2)}) %collective-permute-start.8) | collective-permute-done | bytes 131104 | tf_op jit(solution)/shard_map/ppermute | solution.py:29
  32.8 1.6 %collective-permute-start.9 = (bf16[256,128]{1,0:T(8,128)(2,1)S(1)}, bf16[256,128]{1,0:T(8,128)(2,1)S(1)}, u32[]{:S(2)}, u32[]{:S(2)}) collective-permute-start(bf16[256,128]{1,0:T(8,128)(2,1)S(1)} %fusion.2), channel_id=1, source_target_pairs={{0,8},{4,12},{8,0},{12,4},{1,9},{5,13},{9,1},{13,5},{2,10},{6,14},... | collective-permute-start | bytes 196616 | tf_op jit(solution)/shard_map/ppermute | solution.py:29
  34.4 0.0 collective-permute-done.12
  34.5 1.6 %collective-permute-start.13 = (bf16[256,128]{1,0:T(8,128)(2,1)S(1)}, bf16[256,128]{1,0:T(8,128)(2,1)S(1)}, u32[]{:S(2)}, u32[]{:S(2)}) collective-permute-start(bf16[256,128]{1,0:T(8,128)(2,1)S(1)} %fusion), channel_id=1, source_target_pairs={{0,8},{4,12},{8,0},{12,4},{1,9},{5,13},{9,1},{13,5},{2,10},{6,14},... | collective-permute-start | bytes 196616 | tf_op jit(solution)/shard_map/ppermute | solution.py:29
  36.0 2.7 %collective-permute-done.9 = bf16[256,128]{1,0:T(8,128)(2,1)S(1)} collective-permute-done((bf16[256,128]{1,0:T(8,128)(2,1)S(1)}, bf16[256,128]{1,0:T(8,128)(2,1)S(1)}, u32[]{:S(2)}, u32[]{:S(2)}) %collective-permute-start.9) | collective-permute-done | bytes 65568 | tf_op jit(solution)/shard_map/ppermute | solution.py:29
  38.8 0.1 collective-permute-start.10
  38.9 0.8 %collective-permute-done.13 = bf16[256,128]{1,0:T(8,128)(2,1)S(1)} collective-permute-done((bf16[256,128]{1,0:T(8,128)(2,1)S(1)}, bf16[256,128]{1,0:T(8,128)(2,1)S(1)}, u32[]{:S(2)}, u32[]{:S(2)}) %collective-permute-start.13) | collective-permute-done | bytes 65568 | tf_op jit(solution)/shard_map/ppermute | solution.py:29
  39.8 0.1 collective-permute-start.14
  39.8 0.3 collective-permute-done.10.first_theirs
  40.1 1.0 %collective-permute-done.14.second_theirs = f32[128,128]{1,0:T(8,128)S(1)} collective-permute-done((f32[128,128]{1,0:T(8,128)S(1)}, f32[128,128]{1,0:T(8,128)S(1)}, u32[]{:S(2)}, u32[]{:S(2)}) %collective-permute-start.14) | collective-permute-done | bytes 65568 | tf_op jit(solution)/shard_map/ppermute | solution.py:29
  41.1 0.0 copy-done
  41.1 0.8 %shard_map.60 = bf16[128,512]{1,0:T(8,128)(2,1)} custom-call(bf16[128,512]{1,0:T(8,128)(2,1)S(1)} %bitcast.3, f32[128,128]{1,0:T(8,128)S(1)} %get-tuple-element.50.first_mine, f32[128,128]{1,0:T(8,128)S(1)} %collective-permute-done.10.first_theirs, f32[128,128]{1,0:T(8,128)S(1)} %get-tuple-element.48.second_mine, ...), custom_call_target="tpu_custom_call" | custom-call | flops 1 | bytes 1 | tf_op jit(solution)/shard_map/pallas_call | solution.py:165
  (21 shorter events, 0.4 us)
Async XLA Ops:
  1.4 1.8 %collective-permute-start.1 = (bf16[1024,128]{1,0:T(8,128)(2,1)S(1)}, bf16[1024,128]{1,0:T(8,128)(2,1)S(1)}, u32[]{:S(2)}, u32[]{:S(2)}) collective-permute-start(bf16[1024,128]{1,0:T(8,128)(2,1)S(1)} %get-tuple-element.25), channel_id=1, source_target_pairs={{0,1},{1,0},{2,3},{3,2},{4,5},{5,4},{6,7},{7,6},{8,9},{9,8},{10,11... | collective-permute-start | bytes 786440 | tf_op jit(solution)/shard_map/ppermute | solution.py:29
  2.0 1.3 %collective-permute-start = (bf16[128,256]{1,0:T(8,128)(2,1)S(1)}, bf16[128,256]{1,0:T(8,128)(2,1)S(1)}, u32[]{:S(2)}, u32[]{:S(2)}) collective-permute-start(bf16[128,256]{1,0:T(8,128)(2,1)S(1)} %get-tuple-element.23), channel_id=1, source_target_pairs={{0,1},{1,0},{2,3},{3,2},{4,5},{5,4},{6,7},{7,6},{8,9},{9,8},{10,11... | collective-permute-start | bytes 196616 | tf_op jit(solution)/shard_map/ppermute | solution.py:29
  2.0 6.8 %collective-permute-start.5 = (bf16[1024,128]{1,0:T(8,128)(2,1)S(1)}, bf16[1024,128]{1,0:T(8,128)(2,1)S(1)}, u32[]{:S(2)}, u32[]{:S(2)}) collective-permute-start(bf16[1024,128]{1,0:T(8,128)(2,1)S(1)} %get-tuple-element.29), channel_id=1, source_target_pairs={{0,1},{1,0},{2,3},{3,2},{4,5},{5,4},{6,7},{7,6},{8,9},{9,8},{10,11... | collective-permute-start | bytes 786440 | tf_op jit(solution)/shard_map/ppermute | solution.py:29
  3.3 13.4 %copy-start.1 = (s32[16,16]{1,0:T(8,128)S(1)}, s32[16,16]{1,0:T(8,128)}, u32[]{:S(2)}) copy-start(s32[16,16]{1,0:T(8,128)} %pattern.5) | copy-start | bytes 3076
  3.4 18.5 %collective-permute-start.3 = (bf16[2048,128]{1,0:T(8,128)(2,1)S(1)}, bf16[2048,128]{1,0:T(8,128)(2,1)S(1)}, u32[]{:S(2)}, u32[]{:S(2)}) collective-permute-start(bf16[2048,128]{1,0:T(8,128)(2,1)S(1)} %pad_maximum_fusion), channel_id=1, source_target_pairs={{0,2},{1,3},{2,0},{3,1},{4,6},{5,7},{6,4},{7,5},{8,10},{9,11},{10,... | collective-permute-start | bytes 1572872 | tf_op jit(solution)/shard_map/ppermute | solution.py:29
  6.3 9.1 %collective-permute-start.2 = (bf16[256,256]{1,0:T(8,128)(2,1)S(1)}, bf16[256,256]{1,0:T(8,128)(2,1)S(1)}, u32[]{:S(2)}, u32[]{:S(2)}) collective-permute-start(bf16[256,256]{1,0:T(8,128)(2,1)S(1)} %pad_maximum_fusion.6.own), channel_id=1, source_target_pairs={{0,8},{4,12},{8,0},{12,4},{1,9},{5,13},{9,1},{13,5},{2,10},{6,14},... | collective-permute-start | bytes 393224 | tf_op jit(solution)/shard_map/ppermute | solution.py:29
  9.0 11.7 %collective-permute-start.6 = (bf16[1280,128]{1,0:T(8,128)(2,1)S(1)}, bf16[1280,128]{1,0:T(8,128)(2,1)S(1)}, u32[]{:S(2)}, u32[]{:S(2)}) collective-permute-start(bf16[1280,128]{1,0:T(8,128)(2,1)S(1)} %pad_maximum_fusion.1), channel_id=1, source_target_pairs={{0,4},{4,0},{8,12},{12,8},{1,5},{5,1},{9,13},{13,9},{2,6},{6,2},{1... | collective-permute-start | bytes 983048 | tf_op jit(solution)/shard_map/ppermute | solution.py:29
  15.4 8.0 %collective-permute-start.4 = (bf16[512,128]{1,0:T(8,128)(2,1)S(1)}, bf16[512,128]{1,0:T(8,128)(2,1)S(1)}, u32[]{:S(2)}, u32[]{:S(2)}) collective-permute-start(bf16[512,128]{1,0:T(8,128)(2,1)S(1)} %pad_maximum_fusion.7), channel_id=1, source_target_pairs={{0,2},{1,3},{2,0},{3,1},{4,6},{5,7},{6,4},{7,5},{8,10},{9,11},{10,... | collective-permute-start | bytes 393224 | tf_op jit(solution)/shard_map/ppermute | solution.py:29
  16.0 7.4 %collective-permute-start.7 = (bf16[256,128]{1,0:T(8,128)(2,1)S(1)}, bf16[256,128]{1,0:T(8,128)(2,1)S(1)}, u32[]{:S(2)}, u32[]{:S(2)}) collective-permute-start(bf16[256,128]{1,0:T(8,128)(2,1)S(1)} %get-tuple-element.51), channel_id=1, source_target_pairs={{0,4},{4,0},{8,12},{12,8},{1,5},{5,1},{9,13},{13,9},{2,6},{6,2},{1... | collective-permute-start | bytes 196616 | tf_op jit(solution)/shard_map/ppermute | solution.py:29
  20.6 8.0 %collective-permute-start.11 = (bf16[1024,128]{1,0:T(8,128)(2,1)S(1)}, bf16[1024,128]{1,0:T(8,128)(2,1)S(1)}, u32[]{:S(2)}, u32[]{:S(2)}) collective-permute-start(bf16[1024,128]{1,0:T(8,128)(2,1)S(1)} %pad_maximum_fusion.5.values), channel_id=1, source_target_pairs={{0,4},{4,0},{8,12},{12,8},{1,5},{5,1},{9,13},{13,9},{2,6},{6,2},{1... | collective-permute-start | bytes 786440 | tf_op jit(solution)/shard_map/ppermute | solution.py:29
  27.7 5.0 %collective-permute-start.8 = (bf16[512,128]{1,0:T(8,128)(2,1)S(1)}, bf16[512,128]{1,0:T(8,128)(2,1)S(1)}, u32[]{:S(2)}, u32[]{:S(2)}) collective-permute-start(bf16[512,128]{1,0:T(8,128)(2,1)S(1)} %get-tuple-element.31), channel_id=1, source_target_pairs={{0,4},{4,0},{8,12},{12,8},{1,5},{5,1},{9,13},{13,9},{2,6},{6,2},{1... | collective-permute-start | bytes 393224 | tf_op jit(solution)/shard_map/ppermute | solution.py:29
  29.3 11.8 %copy-start = (bf16[1,128,512]{2,1,0:T(8,128)(2,1)S(1)}, bf16[1,128,512]{2,1,0:T(8,128)(2,1)}, u32[]{:S(2)}) copy-start(bf16[1,128,512]{2,1,0:T(8,128)(2,1)} %param.6) | copy-start | bytes 393220
  29.3 5.1 %collective-permute-start.12 = (bf16[512,128]{1,0:T(8,128)(2,1)S(1)}, bf16[512,128]{1,0:T(8,128)(2,1)S(1)}, u32[]{:S(2)}, u32[]{:S(2)}) collective-permute-start(bf16[512,128]{1,0:T(8,128)(2,1)S(1)} %get-tuple-element.37), channel_id=1, source_target_pairs={{0,2},{1,3},{2,0},{3,1},{4,6},{5,7},{6,4},{7,5},{8,10},{9,11},{10,... | collective-permute-start | bytes 393224 | tf_op jit(solution)/shard_map/ppermute | solution.py:29
  32.8 5.9 %collective-permute-start.9 = (bf16[256,128]{1,0:T(8,128)(2,1)S(1)}, bf16[256,128]{1,0:T(8,128)(2,1)S(1)}, u32[]{:S(2)}, u32[]{:S(2)}) collective-permute-start(bf16[256,128]{1,0:T(8,128)(2,1)S(1)} %fusion.2), channel_id=1, source_target_pairs={{0,8},{4,12},{8,0},{12,4},{1,9},{5,13},{9,1},{13,5},{2,10},{6,14},... | collective-permute-start | bytes 196616 | tf_op jit(solution)/shard_map/ppermute | solution.py:29
  34.5 5.2 %collective-permute-start.13 = (bf16[256,128]{1,0:T(8,128)(2,1)S(1)}, bf16[256,128]{1,0:T(8,128)(2,1)S(1)}, u32[]{:S(2)}, u32[]{:S(2)}) collective-permute-start(bf16[256,128]{1,0:T(8,128)(2,1)S(1)} %fusion), channel_id=1, source_target_pairs={{0,8},{4,12},{8,0},{12,4},{1,9},{5,13},{9,1},{13,5},{2,10},{6,14},... | collective-permute-start | bytes 196616 | tf_op jit(solution)/shard_map/ppermute | solution.py:29
  38.8 1.3 %collective-permute-start.10 = (f32[128,128]{1,0:T(8,128)S(1)}, f32[128,128]{1,0:T(8,128)S(1)}, u32[]{:S(2)}, u32[]{:S(2)}) collective-permute-start(f32[128,128]{1,0:T(8,128)S(1)} %get-tuple-element.49), channel_id=1, source_target_pairs={{0,1},{1,0},{2,3},{3,2},{4,5},{5,4},{6,7},{7,6},{8,9},{9,8},{10,11... | collective-permute-start | bytes 196616 | tf_op jit(solution)/shard_map/ppermute | solution.py:29
  39.8 1.3 %collective-permute-start.14 = (f32[128,128]{1,0:T(8,128)S(1)}, f32[128,128]{1,0:T(8,128)S(1)}, u32[]{:S(2)}, u32[]{:S(2)}) collective-permute-start(f32[128,128]{1,0:T(8,128)S(1)} %get-tuple-element.47), channel_id=1, source_target_pairs={{0,1},{1,0},{2,3},{3,2},{4,5},{5,4},{6,7},{7,6},{8,9},{9,8},{10,11... | collective-permute-start | bytes 196616 | tf_op jit(solution)/shard_map/ppermute | solution.py:29

commit v7 on v6

--- a/solution.py
+++ b/solution.py
@@ -177,7 +177,7 @@
 def finish_kernel(gate_ref, first_mine, first_theirs, second_mine, second_theirs, out_ref):
     core = lax.rem(lax.axis_index("blk"), 2)
     mine = jnp.concatenate([first_mine[...], second_mine[...]], axis=1)
-    theirs = jnp.concatenate([first_theirs[...], second_theirs[...]], axis=1)
+    theirs = jnp.concatenate([first_theirs[...], second_theirs[...]], axis=1).astype(jnp.float32)
     squares = jnp.sum(mine * mine, axis=1, keepdims=True)
     squares = squares + jnp.sum(theirs * theirs, axis=1, keepdims=True)
     factor = lax.rsqrt(squares / (HEADS * HEAD_DIM) + 1e-05)
@@ -231,7 +231,7 @@
     )
     pieces = []
     for x in (first, second):
-        pieces += [x[:count], swapped(x[count:], "blk", 1)]
+        pieces += [x[:count], swapped(x[count:].astype(b16), "blk", 1)]
     gate = gate_values[0]
     inputs = [gate, *pieces]
     return call(finish_kernel, [(gate.shape, gate.dtype)], *inputs)[0][None]

time: 42 us -> 42 us (level)
  no operation moved by 1% of the time
where the time goes in v7:
time: 42 us; the launch traced here: 41.8 us
  waiting for transfers between devices  15.5 us (37%)
  starting transfers between devices  15.4 us (37%)
  Pallas kernels  10.3 us (25%)
    ppermute x15, waiting for transfers between devices, swapped(): return lax.ppermute(block, axis, [(i, i ^ mask) for i in range(size)])  15.5 us
    ppermute x15, starting transfers between devices, swapped(): return lax.ppermute(block, axis, [(i, i ^ mask) for i in range(size)])  15.4 us
    pallas_call x5, Pallas kernels, call(): pl.pallas_call(kernel, out_shape=[jax.ShapeDtypeStruct(shape, kind) for s...  8.83 us
    pallas_call x1, Pallas kernels, pack(): pl.pallas_call(pack_kernel, out_shape=[row_shape] * 2 + [both_shape] * 4,...  1.44 us
  transfers between devices with their start and end apart: 15, of which 8 were waited for; matrix products, arithmetic and copies ran while one was open for 1% of the time, Pallas kernels for 19%

profile of v7, /device:TPU:0, one launch (start us, length us, event | category | flops | bytes accessed | tf_op | source)
XLA Modules:
  0.0 41.8 jit_solution(15589033973538004251)
XLA Ops:
  0.0 1.4 %shard_map.55 = (bf16[128,256]{1,0:T(8,128)(2,1)S(1)}, bf16[128,256]{1,0:T(8,128)(2,1)S(1)}, bf16[1024,128]{1,0:T(8,128)(2,1)S(1)}, bf16[1024,128]{1,0:T(8,128)(...) custom-call(bf16[128,512]{1,0:T(8,128)(2,1)} %bitcast.4, bf16[512,512]{1,0:T(8,128)(2,1)} %keys.1, ...), custom_call_target="tpu_custom_call" | custom-call | flops 1 | bytes 1 | tf_op jit(solution)/shard_map/pallas_call | solution.py:65
  1.4 0.5 %collective-permute-start.1 = (bf16[1024,128]{1,0:T(8,128)(2,1)S(1)}, bf16[1024,128]{1,0:T(8,128)(2,1)S(1)}, u32[]{:S(2)}, u32[]{:S(2)}) collective-permute-start(bf16[1024,128]{1,0:T(8,128)(2,1)S(1)} %get-tuple-element.25), channel_id=1, source_target_pairs={{0,1},{1,0},{2,3},{3,2},{4,5},{5,4},{6,7},{7,6},{8,9},{9,8},{10,11... | collective-permute-start | bytes 786440 | tf_op jit(solution)/shard_map/ppermute | solution.py:29
  2.0 0.1 collective-permute-start
  2.0 0.4 %collective-permute-start.5 = (bf16[1024,128]{1,0:T(8,128)(2,1)S(1)}, bf16[1024,128]{1,0:T(8,128)(2,1)S(1)}, u32[]{:S(2)}, u32[]{:S(2)}) collective-permute-start(bf16[1024,128]{1,0:T(8,128)(2,1)S(1)} %get-tuple-element.29), channel_id=1, source_target_pairs={{0,1},{1,0},{2,3},{3,2},{4,5},{5,4},{6,7},{7,6},{8,9},{9,8},{10,11... | collective-permute-start | bytes 786440 | tf_op jit(solution)/shard_map/ppermute | solution.py:29
  2.5 0.7 %collective-permute-done = bf16[128,256]{1,0:T(8,128)(2,1)S(1)} collective-permute-done((bf16[128,256]{1,0:T(8,128)(2,1)S(1)}, bf16[128,256]{1,0:T(8,128)(2,1)S(1)}, u32[]{:S(2)}, u32[]{:S(2)}) %collective-permute-start) | collective-permute-done | bytes 65568 | tf_op jit(solution)/shard_map/ppermute | solution.py:29
  3.2 0.0 collective-permute-done.1
  3.3 0.0 copy-start.1
  3.4 2.9 %collective-permute-start.3 = (bf16[2048,128]{1,0:T(8,128)(2,1)S(1)}, bf16[2048,128]{1,0:T(8,128)(2,1)S(1)}, u32[]{:S(2)}, u32[]{:S(2)}) collective-permute-start(bf16[2048,128]{1,0:T(8,128)(2,1)S(1)} %pad_maximum_fusion), channel_id=1, source_target_pairs={{0,2},{1,3},{2,0},{3,1},{4,6},{5,7},{6,4},{7,5},{8,10},{9,11},{10,... | collective-permute-start | bytes 1572872 | tf_op jit(solution)/shard_map/ppermute | solution.py:29
  6.3 2.6 %collective-permute-start.2 = (bf16[256,256]{1,0:T(8,128)(2,1)S(1)}, bf16[256,256]{1,0:T(8,128)(2,1)S(1)}, u32[]{:S(2)}, u32[]{:S(2)}) collective-permute-start(bf16[256,256]{1,0:T(8,128)(2,1)S(1)} %pad_maximum_fusion.6.own), channel_id=1, source_target_pairs={{0,8},{4,12},{8,0},{12,4},{1,9},{5,13},{9,1},{13,5},{2,10},{6,14},... | collective-permute-start | bytes 393224 | tf_op jit(solution)/shard_map/ppermute | solution.py:29
  8.9 0.0 collective-permute-done.5
  9.0 1.6 %collective-permute-start.6 = (bf16[1280,128]{1,0:T(8,128)(2,1)S(1)}, bf16[1280,128]{1,0:T(8,128)(2,1)S(1)}, u32[]{:S(2)}, u32[]{:S(2)}) collective-permute-start(bf16[1280,128]{1,0:T(8,128)(2,1)S(1)} %pad_maximum_fusion.1), channel_id=1, source_target_pairs={{0,4},{4,0},{8,12},{12,8},{1,5},{5,1},{9,13},{13,9},{2,6},{6,2},{1... | collective-permute-start | bytes 983048 | tf_op jit(solution)/shard_map/ppermute | solution.py:29
  10.6 4.7 %collective-permute-done.2.far = bf16[256,256]{1,0:T(8,128)(2,1)S(1)} collective-permute-done((bf16[256,256]{1,0:T(8,128)(2,1)S(1)}, bf16[256,256]{1,0:T(8,128)(2,1)S(1)}, u32[]{:S(2)}, u32[]{:S(2)}) %collective-permute-start.2) | collective-permute-done | bytes 131104 | tf_op jit(solution)/shard_map/ppermute | solution.py:29
  15.4 0.6 %collective-permute-start.4 = (bf16[512,128]{1,0:T(8,128)(2,1)S(1)}, bf16[512,128]{1,0:T(8,128)(2,1)S(1)}, u32[]{:S(2)}, u32[]{:S(2)}) collective-permute-start(bf16[512,128]{1,0:T(8,128)(2,1)S(1)} %pad_maximum_fusion.7), channel_id=1, source_target_pairs={{0,2},{1,3},{2,0},{3,1},{4,6},{5,7},{6,4},{7,5},{8,10},{9,11},{10,... | collective-permute-start | bytes 393224 | tf_op jit(solution)/shard_map/ppermute | solution.py:29
  16.0 0.7 %collective-permute-start.7 = (bf16[256,128]{1,0:T(8,128)(2,1)S(1)}, bf16[256,128]{1,0:T(8,128)(2,1)S(1)}, u32[]{:S(2)}, u32[]{:S(2)}) collective-permute-start(bf16[256,128]{1,0:T(8,128)(2,1)S(1)} %get-tuple-element.47), channel_id=1, source_target_pairs={{0,4},{4,0},{8,12},{12,8},{1,5},{5,1},{9,13},{13,9},{2,6},{6,2},{1... | collective-permute-start | bytes 196616 | tf_op jit(solution)/shard_map/ppermute | solution.py:29
  16.7 0.0 copy-done.1
  16.7 1.5 %shard_map.56.start = f32[512,128]{1,0:T(8,128)S(1)} custom-call(s32[16,16]{1,0:T(8,128)S(1)} %copy-done.1, bf16[256,256]{1,0:T(8,128)(2,1)S(1)} %pad_maximum_fusion.6.own, bf16[256,256]{1,0:T(8,128)(2,1)S(1)} %collective-permute-done.2.far, bf16[1024,128]{1,0:T(8,128)(2,1)S(1)} %pad_maximum_fusion.2.keys.first_keys, ...), custom_call_target="tpu_custom_call" | custom-call | flops 1 | bytes 1 | tf_op jit(solution)/shard_map/pallas_call | solution.py:165
  18.2 2.4 %collective-permute-done.6.near_pack = bf16[1280,128]{1,0:T(8,128)(2,1)S(1)} collective-permute-done((bf16[1280,128]{1,0:T(8,128)(2,1)S(1)}, bf16[1280,128]{1,0:T(8,128)(2,1)S(1)}, u32[]{:S(2)}, u32[]{:S(2)}) %collective-permute-start.6) | collective-permute-done | bytes 327712 | tf_op jit(solution)/shard_map/ppermute | solution.py:29
  20.6 1.3 %collective-permute-start.11 = (bf16[1024,128]{1,0:T(8,128)(2,1)S(1)}, bf16[1024,128]{1,0:T(8,128)(2,1)S(1)}, u32[]{:S(2)}, u32[]{:S(2)}) collective-permute-start(bf16[1024,128]{1,0:T(8,128)(2,1)S(1)} %pad_maximum_fusion.5.values), channel_id=1, source_target_pairs={{0,4},{4,0},{8,12},{12,8},{1,5},{5,1},{9,13},{13,9},{2,6},{6,2},{1... | collective-permute-start | bytes 786440 | tf_op jit(solution)/shard_map/ppermute | solution.py:29
  21.9 0.0 collective-permute-done.3.far_hist
  21.9 1.5 %shard_map.57 = (f32[256,128]{1,0:T(8,128)S(1)}, f32[256,128]{1,0:T(8,128)S(1)}) custom-call(s32[16,16]{1,0:T(8,128)S(1)} %copy-done.1, bf16[256,256]{1,0:T(8,128)(2,1)S(1)} %pad_maximum_fusion.6.own, bf16[256,256]{1,0:T(8,128)(2,1)S(1)} %collective-permute-done.2.far, bf16[2048,128]{1,0:T(8,128)(2,1)S(1)} %collective-permute-done.3.far_hist, ...), custom_call_target="tpu_custom_call" | custom-call | flops 1 | bytes 1 | tf_op jit(solution)/shard_map/pallas_call | solution.py:165
  23.4 0.0 collective-permute-done.7.both
  23.4 0.0 collective-permute-done.4.crosses
  23.4 4.4 %shard_map.58 = (f32[1024,128]{1,0:T(8,128)S(1)}, bf16[1024,1024]{1,0:T(8,128)(2,1)S(1)}, bf16[512,128]{1,0:T(8,128)(2,1)S(1)}) custom-call(s32[16,16]{1,0:T(8,128)S(1)} %copy-done.1, bf16[256,256]{1,0:T(8,128)(2,1)S(1)} %pad_maximum_fusion.6.own, bf16[512,128]{1,0:T(8,128)(2,1)S(1)} %collective-permute-done.4.crosses, ...), custom_call_target="tpu_custom_call" | custom-call | flops 10000000000 | bytes 1 | tf_op jit(solution)/shard_map/pallas_call | solution.py:165
  27.7 0.8 %collective-permute-start.8 = (bf16[512,128]{1,0:T(8,128)(2,1)S(1)}, bf16[512,128]{1,0:T(8,128)(2,1)S(1)}, u32[]{:S(2)}, u32[]{:S(2)}) collective-permute-start(bf16[512,128]{1,0:T(8,128)(2,1)S(1)} %get-tuple-element.31), channel_id=1, source_target_pairs={{0,4},{4,0},{8,12},{12,8},{1,5},{5,1},{9,13},{13,9},{2,6},{6,2},{1... | collective-permute-start | bytes 393224 | tf_op jit(solution)/shard_map/ppermute | solution.py:29
  28.6 0.0 collective-permute-done.11.near_values
  28.6 0.7 %shard_map.59 = (f32[256,128]{1,0:T(8,128)S(1)}, f32[256,128]{1,0:T(8,128)S(1)}, bf16[512,128]{1,0:T(8,128)(2,1)S(1)}) custom-call(bf16[1024,1024]{1,0:T(8,128)(2,1)S(1)} %get-tuple-element.33.weights, bf16[1024,128]{1,0:T(8,128)(2,1)S(1)} %collective-permute-done.11.near_values, f32[1024,128]{1,0:T(8,128)S(1)} %get-tuple-element.35.start), custom_call_target="tpu_custom_call" | custom-call | flops 10000000000 | bytes 1 | tf_op jit(solution)/shard_map/pallas_call | solution.py:165
  29.3 0.0 copy-start
  29.3 0.5 %collective-permute-start.12 = (bf16[512,128]{1,0:T(8,128)(2,1)S(1)}, bf16[512,128]{1,0:T(8,128)(2,1)S(1)}, u32[]{:S(2)}, u32[]{:S(2)}) collective-permute-start(bf16[512,128]{1,0:T(8,128)(2,1)S(1)} %get-tuple-element.37), channel_id=1, source_target_pairs={{0,2},{1,3},{2,0},{3,1},{4,6},{5,7},{6,4},{7,5},{8,10},{9,11},{10,... | collective-permute-start | bytes 393224 | tf_op jit(solution)/shard_map/ppermute | solution.py:29
  29.9 2.9 %collective-permute-done.8 = bf16[512,128]{1,0:T(8,128)(2,1)S(1)} collective-permute-done((bf16[512,128]{1,0:T(8,128)(2,1)S(1)}, bf16[512,128]{1,0:T(8,128)(2,1)S(1)}, u32[]{:S(2)}, u32[]{:S(2)}) %collective-permute-start.8) | collective-permute-done | bytes 131104 | tf_op jit(solution)/shard_map/ppermute | solution.py:29
  32.8 1.6 %collective-permute-start.9 = (bf16[256,128]{1,0:T(8,128)(2,1)S(1)}, bf16[256,128]{1,0:T(8,128)(2,1)S(1)}, u32[]{:S(2)}, u32[]{:S(2)}) collective-permute-start(bf16[256,128]{1,0:T(8,128)(2,1)S(1)} %fusion.2), channel_id=1, source_target_pairs={{0,8},{4,12},{8,0},{12,4},{1,9},{5,13},{9,1},{13,5},{2,10},{6,14},... | collective-permute-start | bytes 196616 | tf_op jit(solution)/shard_map/ppermute | solution.py:29
  34.4 0.0 collective-permute-done.12
  34.5 1.6 %collective-permute-start.13 = (bf16[256,128]{1,0:T(8,128)(2,1)S(1)}, bf16[256,128]{1,0:T(8,128)(2,1)S(1)}, u32[]{:S(2)}, u32[]{:S(2)}) collective-permute-start(bf16[256,128]{1,0:T(8,128)(2,1)S(1)} %fusion), channel_id=1, source_target_pairs={{0,8},{4,12},{8,0},{12,4},{1,9},{5,13},{9,1},{13,5},{2,10},{6,14},... | collective-permute-start | bytes 196616 | tf_op jit(solution)/shard_map/ppermute | solution.py:29
  36.0 2.7 %collective-permute-done.9 = bf16[256,128]{1,0:T(8,128)(2,1)S(1)} collective-permute-done((bf16[256,128]{1,0:T(8,128)(2,1)S(1)}, bf16[256,128]{1,0:T(8,128)(2,1)S(1)}, u32[]{:S(2)}, u32[]{:S(2)}) %collective-permute-start.9) | collective-permute-done | bytes 65568 | tf_op jit(solution)/shard_map/ppermute | solution.py:29
  38.8 0.1 collective-permute-start.10
  38.9 0.8 %collective-permute-done.13 = bf16[256,128]{1,0:T(8,128)(2,1)S(1)} collective-permute-done((bf16[256,128]{1,0:T(8,128)(2,1)S(1)}, bf16[256,128]{1,0:T(8,128)(2,1)S(1)}, u32[]{:S(2)}, u32[]{:S(2)}) %collective-permute-start.13) | collective-permute-done | bytes 65568 | tf_op jit(solution)/shard_map/ppermute | solution.py:29
  39.8 0.1 collective-permute-start.14
  39.9 0.2 collective-permute-done.10.first_theirs
  40.1 1.0 %collective-permute-done.14.second_theirs = bf16[128,128]{1,0:T(8,128)(2,1)S(1)} collective-permute-done((bf16[128,128]{1,0:T(8,128)(2,1)S(1)}, bf16[128,128]{1,0:T(8,128)(2,1)S(1)}, u32[]{:S(2)}, u32[]{:S(2)}) %collective-permute-start.14) | collective-permute-done | bytes 32800 | tf_op jit(solution)/shard_map/ppermute | solution.py:29
  41.0 0.0 copy-done
  41.0 0.8 %shard_map.60 = bf16[128,512]{1,0:T(8,128)(2,1)} custom-call(bf16[128,512]{1,0:T(8,128)(2,1)S(1)} %bitcast.3, f32[128,128]{1,0:T(8,128)S(1)} %slice.90.first_mine, bf16[128,128]{1,0:T(8,128)(2,1)S(1)} %collective-permute-done.10.first_theirs, f32[128,128]{1,0:T(8,128)S(1)} %slice.94.second_mine, bf16[128,128]{1,0:T(8,128)(2,1)S(1)} %collective-permute-done.14.second_theirs), custom_call_target="tpu_custom_call" | custom-call | flops 1 | bytes 1 | tf_op jit(solution)/shard_map/pallas_call | solution.py:165
  (23 shorter events, 0.4 us)
Async XLA Ops:
  1.4 1.8 %collective-permute-start.1 = (bf16[1024,128]{1,0:T(8,128)(2,1)S(1)}, bf16[1024,128]{1,0:T(8,128)(2,1)S(1)}, u32[]{:S(2)}, u32[]{:S(2)}) collective-permute-start(bf16[1024,128]{1,0:T(8,128)(2,1)S(1)} %get-tuple-element.25), channel_id=1, source_target_pairs={{0,1},{1,0},{2,3},{3,2},{4,5},{5,4},{6,7},{7,6},{8,9},{9,8},{10,11... | collective-permute-start | bytes 786440 | tf_op jit(solution)/shard_map/ppermute | solution.py:29
  2.0 1.3 %collective-permute-start = (bf16[128,256]{1,0:T(8,128)(2,1)S(1)}, bf16[128,256]{1,0:T(8,128)(2,1)S(1)}, u32[]{:S(2)}, u32[]{:S(2)}) collective-permute-start(bf16[128,256]{1,0:T(8,128)(2,1)S(1)} %get-tuple-element.23), channel_id=1, source_target_pairs={{0,1},{1,0},{2,3},{3,2},{4,5},{5,4},{6,7},{7,6},{8,9},{9,8},{10,11... | collective-permute-start | bytes 196616 | tf_op jit(solution)/shard_map/ppermute | solution.py:29
  2.0 6.8 %collective-permute-start.5 = (bf16[1024,128]{1,0:T(8,128)(2,1)S(1)}, bf16[1024,128]{1,0:T(8,128)(2,1)S(1)}, u32[]{:S(2)}, u32[]{:S(2)}) collective-permute-start(bf16[1024,128]{1,0:T(8,128)(2,1)S(1)} %get-tuple-element.29), channel_id=1, source_target_pairs={{0,1},{1,0},{2,3},{3,2},{4,5},{5,4},{6,7},{7,6},{8,9},{9,8},{10,11... | collective-permute-start | bytes 786440 | tf_op jit(solution)/shard_map/ppermute | solution.py:29
  3.3 13.4 %copy-start.1 = (s32[16,16]{1,0:T(8,128)S(1)}, s32[16,16]{1,0:T(8,128)}, u32[]{:S(2)}) copy-start(s32[16,16]{1,0:T(8,128)} %pattern.5) | copy-start | bytes 3076
  3.4 18.5 %collective-permute-start.3 = (bf16[2048,128]{1,0:T(8,128)(2,1)S(1)}, bf16[2048,128]{1,0:T(8,128)(2,1)S(1)}, u32[]{:S(2)}, u32[]{:S(2)}) collective-permute-start(bf16[2048,128]{1,0:T(8,128)(2,1)S(1)} %pad_maximum_fusion), channel_id=1, source_target_pairs={{0,2},{1,3},{2,0},{3,1},{4,6},{5,7},{6,4},{7,5},{8,10},{9,11},{10,... | collective-permute-start | bytes 1572872 | tf_op jit(solution)/shard_map/ppermute | solution.py:29
  6.3 9.1 %collective-permute-start.2 = (bf16[256,256]{1,0:T(8,128)(2,1)S(1)}, bf16[256,256]{1,0:T(8,128)(2,1)S(1)}, u32[]{:S(2)}, u32[]{:S(2)}) collective-permute-start(bf16[256,256]{1,0:T(8,128)(2,1)S(1)} %pad_maximum_fusion.6.own), channel_id=1, source_target_pairs={{0,8},{4,12},{8,0},{12,4},{1,9},{5,13},{9,1},{13,5},{2,10},{6,14},... | collective-permute-start | bytes 393224 | tf_op jit(solution)/shard_map/ppermute | solution.py:29
  9.0 11.7 %collective-permute-start.6 = (bf16[1280,128]{1,0:T(8,128)(2,1)S(1)}, bf16[1280,128]{1,0:T(8,128)(2,1)S(1)}, u32[]{:S(2)}, u32[]{:S(2)}) collective-permute-start(bf16[1280,128]{1,0:T(8,128)(2,1)S(1)} %pad_maximum_fusion.1), channel_id=1, source_target_pairs={{0,4},{4,0},{8,12},{12,8},{1,5},{5,1},{9,13},{13,9},{2,6},{6,2},{1... | collective-permute-start | bytes 983048 | tf_op jit(solution)/shard_map/ppermute | solution.py:29
  15.4 8.0 %collective-permute-start.4 = (bf16[512,128]{1,0:T(8,128)(2,1)S(1)}, bf16[512,128]{1,0:T(8,128)(2,1)S(1)}, u32[]{:S(2)}, u32[]{:S(2)}) collective-permute-start(bf16[512,128]{1,0:T(8,128)(2,1)S(1)} %pad_maximum_fusion.7), channel_id=1, source_target_pairs={{0,2},{1,3},{2,0},{3,1},{4,6},{5,7},{6,4},{7,5},{8,10},{9,11},{10,... | collective-permute-start | bytes 393224 | tf_op jit(solution)/shard_map/ppermute | solution.py:29
  16.0 7.4 %collective-permute-start.7 = (bf16[256,128]{1,0:T(8,128)(2,1)S(1)}, bf16[256,128]{1,0:T(8,128)(2,1)S(1)}, u32[]{:S(2)}, u32[]{:S(2)}) collective-permute-start(bf16[256,128]{1,0:T(8,128)(2,1)S(1)} %get-tuple-element.47), channel_id=1, source_target_pairs={{0,4},{4,0},{8,12},{12,8},{1,5},{5,1},{9,13},{13,9},{2,6},{6,2},{1... | collective-permute-start | bytes 196616 | tf_op jit(solution)/shard_map/ppermute | solution.py:29
  20.6 8.0 %collective-permute-start.11 = (bf16[1024,128]{1,0:T(8,128)(2,1)S(1)}, bf16[1024,128]{1,0:T(8,128)(2,1)S(1)}, u32[]{:S(2)}, u32[]{:S(2)}) collective-permute-start(bf16[1024,128]{1,0:T(8,128)(2,1)S(1)} %pad_maximum_fusion.5.values), channel_id=1, source_target_pairs={{0,4},{4,0},{8,12},{12,8},{1,5},{5,1},{9,13},{13,9},{2,6},{6,2},{1... | collective-permute-start | bytes 786440 | tf_op jit(solution)/shard_map/ppermute | solution.py:29
  27.7 5.0 %collective-permute-start.8 = (bf16[512,128]{1,0:T(8,128)(2,1)S(1)}, bf16[512,128]{1,0:T(8,128)(2,1)S(1)}, u32[]{:S(2)}, u32[]{:S(2)}) collective-permute-start(bf16[512,128]{1,0:T(8,128)(2,1)S(1)} %get-tuple-element.31), channel_id=1, source_target_pairs={{0,4},{4,0},{8,12},{12,8},{1,5},{5,1},{9,13},{13,9},{2,6},{6,2},{1... | collective-permute-start | bytes 393224 | tf_op jit(solution)/shard_map/ppermute | solution.py:29
  29.3 11.7 %copy-start = (bf16[1,128,512]{2,1,0:T(8,128)(2,1)S(1)}, bf16[1,128,512]{2,1,0:T(8,128)(2,1)}, u32[]{:S(2)}) copy-start(bf16[1,128,512]{2,1,0:T(8,128)(2,1)} %param.6) | copy-start | bytes 393220
  29.3 5.1 %collective-permute-start.12 = (bf16[512,128]{1,0:T(8,128)(2,1)S(1)}, bf16[512,128]{1,0:T(8,128)(2,1)S(1)}, u32[]{:S(2)}, u32[]{:S(2)}) collective-permute-start(bf16[512,128]{1,0:T(8,128)(2,1)S(1)} %get-tuple-element.37), channel_id=1, source_target_pairs={{0,2},{1,3},{2,0},{3,1},{4,6},{5,7},{6,4},{7,5},{8,10},{9,11},{10,... | collective-permute-start | bytes 393224 | tf_op jit(solution)/shard_map/ppermute | solution.py:29
  32.8 5.9 %collective-permute-start.9 = (bf16[256,128]{1,0:T(8,128)(2,1)S(1)}, bf16[256,128]{1,0:T(8,128)(2,1)S(1)}, u32[]{:S(2)}, u32[]{:S(2)}) collective-permute-start(bf16[256,128]{1,0:T(8,128)(2,1)S(1)} %fusion.2), channel_id=1, source_target_pairs={{0,8},{4,12},{8,0},{12,4},{1,9},{5,13},{9,1},{13,5},{2,10},{6,14},... | collective-permute-start | bytes 196616 | tf_op jit(solution)/shard_map/ppermute | solution.py:29
  34.5 5.2 %collective-permute-start.13 = (bf16[256,128]{1,0:T(8,128)(2,1)S(1)}, bf16[256,128]{1,0:T(8,128)(2,1)S(1)}, u32[]{:S(2)}, u32[]{:S(2)}) collective-permute-start(bf16[256,128]{1,0:T(8,128)(2,1)S(1)} %fusion), channel_id=1, source_target_pairs={{0,8},{4,12},{8,0},{12,4},{1,9},{5,13},{9,1},{13,5},{2,10},{6,14},... | collective-permute-start | bytes 196616 | tf_op jit(solution)/shard_map/ppermute | solution.py:29
  38.8 1.3 %collective-permute-start.10 = (bf16[128,128]{1,0:T(8,128)(2,1)S(1)}, bf16[128,128]{1,0:T(8,128)(2,1)S(1)}, u32[]{:S(2)}, u32[]{:S(2)}) collective-permute-start(bf16[128,128]{1,0:T(8,128)(2,1)S(1)} %slice.111), channel_id=1, source_target_pairs={{0,1},{1,0},{2,3},{3,2},{4,5},{5,4},{6,7},{7,6},{8,9},{9,8},{10,11... | collective-permute-start | bytes 98312 | tf_op jit(solution)/shard_map/ppermute | solution.py:29
  39.8 1.3 %collective-permute-start.14 = (bf16[128,128]{1,0:T(8,128)(2,1)S(1)}, bf16[128,128]{1,0:T(8,128)(2,1)S(1)}, u32[]{:S(2)}, u32[]{:S(2)}) collective-permute-start(bf16[128,128]{1,0:T(8,128)(2,1)S(1)} %slice.110), channel_id=1, source_target_pairs={{0,1},{1,0},{2,3},{3,2},{4,5},{5,4},{6,7},{7,6},{8,9},{9,8},{10,11... | collective-permute-start | bytes 98312 | tf_op jit(solution)/shard_map/ppermute | solution.py:29
